TPU v7x, 32 devices: a whole 2x2x4 slice. The times are simulated.
32 devices in a mesh: groups: 2 (over y), expert: 4 (over z), tensor: 4 (over x, core).
Axes of the slice: x: 2, y: 2, z: 4, core: 2. Of those that a mesh axis runs over, the one named last changes fastest.
Arguments:
- tokens: bfloat16 [640, 6144], P(('groups', 'expert'), 'tensor'), parts along dimension 0, may hold values from -6 to 6
- expert_ids: int32 [640, 4], P(('groups', 'expert')), parts along dimension 0, may hold values from 0 to 15, as said below
- route_weights: float32 [640, 4], P(('groups', 'expert')), parts along dimension 0, may hold values from 0.1 to 1
- w_gate: bfloat16 [6144, 32768], P(None, ('expert', 'tensor')), may hold values from -0.078125 to 0.078125
- w_up: bfloat16 [6144, 32768], P(None, ('expert', 'tensor')), may hold values from -0.078125 to 0.078125
- w_down: bfloat16 [32768, 6144], P(('expert', 'tensor')), may hold values from -0.0625 to 0.0625
Outputs:
- moe_output: bfloat16 [640, 6144], P(('groups', 'expert'), 'tensor'), parts along dimension 0
There are 2 independent parts, one for each index of `groups`. A program takes and returns all parts, laid end to end along the dimension named above; an argument that names none is the same for every part. Nothing has to cross between parts.
Inputs may be any that keep to these rules, and one draw needn't show every extreme that they name: `expert_ids`: each token names 4 different experts. In each block of 80 tokens in order (the tokens of one index of expert), each expert below 4 is named by at most 10 tokens, and one of them by exactly 10.
All inputs are finite; a program needn't handle non-finite values.
Results may differ from a plain program's by a relative error of at most 0.012.
Values may be sent and summed in bfloat16 or wider, within the bound.
No kernel may reach another device: no remote copies, remote signals or barrier semaphores. Data moves between devices by JAX's collectives and lax.ppermute only.
A program may use at most 192 MiB of HBM per device.

v0:
```python
import jax
import jax.numpy as jnp
from jax import lax
from jax.sharding import PartitionSpec as P

E_W = 4
SLOT = 10


def per_device(tokens, expert_ids, route_weights, w_gate, w_up, w_down):
    groups_count = lax.axis_size("expert")
    replicas = groups_count // E_W
    slots = SLOT
    picked = expert_ids[:, :, None] == jnp.arange(E_W, dtype=jnp.int32)[None, None, :]
    weight_e = jnp.sum(jnp.where(picked, route_weights[:, :, None], jnp.float32(0.0)), axis=1)
    member = jnp.any(picked, axis=1)
    position = jnp.cumsum(member.astype(jnp.int32), axis=0) - 1
    placed = (position[None, :, :] == jnp.arange(slots, dtype=jnp.int32)[:, None, None]) & member[
        None, :, :
    ]
    placed_onehot = jnp.transpose(placed, (2, 0, 1)).astype(jnp.bfloat16)
    full_rows = lax.all_gather(tokens, "tensor", axis=1, tiled=True)
    selected = jnp.einsum(
        "est,td->esd", placed_onehot, full_rows, preferred_element_type=jnp.float32
    )
    outgoing = jnp.repeat(selected.astype(jnp.bfloat16), replicas, axis=0)
    arrived = lax.all_to_all(outgoing, "expert", split_axis=0, concat_axis=0, tiled=True)
    gate_proj = jnp.einsum("isd,dh->ish", arrived, w_gate, preferred_element_type=jnp.float32)
    up_proj = jnp.einsum("isd,dh->ish", arrived, w_up, preferred_element_type=jnp.float32)
    hidden = (jax.nn.silu(gate_proj) * up_proj).astype(jnp.bfloat16)
    hidden = hidden.reshape(groups_count * slots, w_gate.shape[1])
    summed = lax.psum_scatter(
        lax.dot_general(
            w_down, hidden, (((0,), (1,)), ((), ())), preferred_element_type=jnp.float32
        ).astype(jnp.bfloat16),
        "tensor",
        scatter_dimension=0,
        tiled=True,
    )
    returned_rows = lax.all_to_all(summed, "expert", split_axis=1, concat_axis=1, tiled=True)
    feature_count = returned_rows.shape[0]
    per_expert = jnp.sum(
        returned_rows.astype(jnp.float32).reshape(feature_count, E_W, replicas, slots), axis=2
    )
    combine = placed.astype(jnp.float32) * weight_e[None, :, :]
    mixed_cols = jnp.einsum("des,ste->dt", per_expert, combine, precision=lax.Precision.HIGHEST)
    return mixed_cols.T.astype(jnp.bfloat16)


def solution(mesh):
    return jax.shard_map(
        per_device,
        mesh=mesh,
        in_specs=(
            P(("groups", "expert"), "tensor"),
            P(("groups", "expert"), None),
            P(("groups", "expert"), None),
            P(None, ("expert", "tensor")),
            P(None, ("expert", "tensor")),
            P(("expert", "tensor"), None),
        ),
        out_specs=P(("groups", "expert"), "tensor"),
        check_vma=False,
    )
```

profile of v0, /device:TPU:0, one launch (start us, length us, event | category | flops | bytes accessed | tf_op | source)
XLA Modules:
  0.0 118.9 jit_solution(12071102183653864229)
XLA Ops:
  6.5 0.0 reduce-scatter.2.cloned.1.call-start
  6.5 0.7 fusion.24
  7.2 0.1 copy.19
  7.3 0.1 reduce_window_sum.11
  7.5 0.1 copy.21
  7.5 11.3 %all_gather.3 = bf16[80,6144]{1,0:T(8,128)(2,1)S(1)} all-gather(bf16[80,1536]{1,0:T(8,128)(2,1)} %param.6), channel_id=1, replica_groups=mesh['groups'=2,'expert'=4,'tensor'=4] {'tensor'}, dimensions={1}, use_global_device_ids=true | all-gather | bytes 1228800 | tf_op jit(solution)/shard_map/all_gather | solution.py:22
  18.9 0.4 convolution_convert_fusion
  19.2 25.3 %all_to_all.14 = bf16[4,10,6144]{2,1,0:T(8,128)(2,1)S(1)} all-to-all(bf16[4,10,6144]{2,1,0:T(8,128)(2,1)S(1)} %convolution_convert_fusion), channel_id=1, replica_groups=mesh['groups'=2,'expert'=4,'tensor'=4] {'expert'}, dimensions={0} | all-to-all | bytes 983040 | tf_op jit(solution)/shard_map/all_to_all | solution.py:27
  44.5 10.5 %fusion.2 = f32[4,10,2048]{2,1,0:T(8,128)S(1)} fusion(bf16[4,10,6144]{2,1,0:T(8,128)(2,1)S(1)} %all_to_all.14, bf16[6144,2048]{1,0:T(8,128)(2,1)} %param.9), kind=kOutput, calls=%fused_computation.2 | convolution fusion | flops 1006632960 | bytes 25985024 | tf_op jit(solution)/shard_map/isd,dh->ish/dot_general | solution.py:28
  55.0 10.6 %fusion.9 = bf16[4,10,2048]{2,1,0:T(8,128)(2,1)S(1)} fusion(bf16[4,10,6144]{2,1,0:T(8,128)(2,1)S(1)} %all_to_all.14, bf16[6144,2048]{1,0:T(8,128)(2,1)} %param.10, f32[4,10,2048]{2,1,0:T(8,128)S(1)} %fusion.2), kind=kOutput, calls=%fused_computation.10 | convolution fusion | flops 1007124480 | bytes 26148864 | tf_op jit(solution)/shard_map/isd,dh->ish/dot_general | solution.py:29
  65.7 0.0 copy-start
  65.7 0.0 copy-start.1
  65.7 0.1 reshape.22
  65.8 11.3 %fusion.4 = bf16[6144,40]{0,1:T(8,128)(2,1)} fusion(bf16[40,2048]{1,0:T(8,128)(2,1)S(1)} %reshape.22, bf16[2048,6144]{1,0:T(8,128)(2,1)} %param.11), kind=kOutput, calls=%fused_computation.6 | convolution fusion | flops 1006878720 | bytes 25821184 | tf_op jit(solution)/shard_map/dot_general | solution.py:33
  77.0 0.0 reduce-scatter.2.cloned.1.call-update
  77.0 20.3 %reduce-scatter.2.cloned.1.call-done = bf16[1536,40]{0,1:T(8,128)(2,1)} async-done(((bf16[6144,40]{0,1:T(8,128)(2,1)}), bf16[1536,40]{0,1:T(8,128)(2,1)}) %reduce-scatter.2.cloned.1.call-update) | async-done | bytes 122896 | tf_op jit(solution)/shard_map/reduce_scatter | solution.py:32
  97.3 1.6 %all_to_all.10 = bf16[1536,4,10]{0,2,1:T(8,128)(2,1)} reshape(bf16[1536,40]{0,1:T(8,128)(2,1)} %reduce-scatter.2.cloned.1.call-done) | data formatting | bytes 245760 | tf_op jit(solution)/shard_map/all_to_all | solution.py:40
  98.9 4.6 %all-to-all-start.1 = ((bf16[1536,4,10]{0,2,1:T(8,128)(2,1)}), bf16[1536,4,10]{0,2,1:T(8,128)(2,1)S(1)}, u32[]{:S(2)}, u32[]{:S(2)}) async-start(bf16[1536,4,10]{0,2,1:T(8,128)(2,1)} %all_to_all.10), calls=%async_computation.2 | async-start | bytes 393216 | tf_op jit(solution)/shard_map/all_to_all | solution.py:40
  103.5 0.1 copy.20
  103.6 0.0 copy-done
  103.6 0.0 copy-done.1
  103.6 7.4 %all-to-all-done.1 = bf16[1536,4,10]{0,2,1:T(8,128)(2,1)S(1)} async-done(((bf16[1536,4,10]{0,2,1:T(8,128)(2,1)}), bf16[1536,4,10]{0,2,1:T(8,128)(2,1)S(1)}, u32[]{:S(2)}, u32[]{:S(2)}) %all-to-all-start.1) | async-done | bytes 122912 | tf_op jit(solution)/shard_map/all_to_all | solution.py:40
  111.0 1.1 fusion.5
  (3 shorter events, 0.0 us)
Async XLA Ops:
  6.5 90.8 %reduce-scatter.2.cloned.1.call-start = ((), (), s32[]{:S(2)}) async-start(), calls=%async_computation.3 | async-start | bytes 614400 | tf_op jit(solution)/shard_map/reduce_scatter | solution.py:32
  65.7 37.9 %copy-start = (s32[80,4]{0,1:T(4,128)S(1)}, s32[80,4]{0,1:T(4,128)}, u32[]{:S(2)}) copy-start(s32[80,4]{0,1:T(4,128)} %param.7) | copy-start | bytes 3844
  65.7 37.9 %copy-start.1 = (f32[80,4]{0,1:T(4,128)S(1)}, f32[80,4]{0,1:T(4,128)}, u32[]{:S(2)}) copy-start(f32[80,4]{0,1:T(4,128)} %param.8) | copy-start | bytes 3844
  98.9 12.1 %all-to-all-start.1 = ((bf16[1536,4,10]{0,2,1:T(8,128)(2,1)}), bf16[1536,4,10]{0,2,1:T(8,128)(2,1)S(1)}, u32[]{:S(2)}, u32[]{:S(2)}) async-start(bf16[1536,4,10]{0,2,1:T(8,128)(2,1)} %all_to_all.10), calls=%async_computation.2 | async-start | bytes 393216 | tf_op jit(solution)/shard_map/all_to_all | solution.py:40
Sparse Core Ops, SparseCore 0:
  77.2 20.0 reduce-scatter.1
where the time goes:
time: 119 us
  blocking collectives  36.6 us (31%)
  matrix products  33.8 us (28%)
  waiting for transfers between devices  27.6 us (23%)
  between operations  13.4 us (11%)
  starting transfers between devices  4.6 us (4%)
  local copies, waits for them, and re-layouts  1.94 us (2%)
    all_to_all x1, blocking collectives, per_device(): lax.all_to_all(outgoing, 'expert', split_axis=0, concat_axis=0, tiled=True)  25.3 us
    reduce_scatter x1, waiting for transfers between devices, per_device(): lax.psum_scatter(lax.dot_general(w_down, hidden, (((0,), (1,)), ((), ()))...  20.3 us
    all_gather x1, blocking collectives, per_device(): full_rows = lax.all_gather(tokens, 'tensor', axis=1, tiled=True)  11.3 us
    dot_general x1, matrix products, per_device(): lax.dot_general(w_down, hidden, (((0,), (1,)), ((), ())), preferred_eleme...  11.3 us
    dot_general x1, matrix products, per_device(): jnp.einsum('isd,dh->ish', arrived, w_up, preferred_element_type=jnp.float32)  10.6 us
    dot_general x1, matrix products, per_device(): jnp.einsum('isd,dh->ish', arrived, w_gate, preferred_element_type=jnp.flo...  10.5 us
    all_to_all x1, waiting for transfers between devices, per_device(): lax.all_to_all(summed, 'expert', split_axis=1, concat_axis=1, tiled=True)  7.36 us
    all_to_all x1, starting transfers between devices, per_device(): lax.all_to_all(summed, 'expert', split_axis=1, concat_axis=1, tiled=True)  4.6 us
  transfers between devices with their start and end apart: 2, of which 2 were waited for; matrix products, arithmetic and copies ran while one was open for 0% of the time, Pallas kernels for 0%

commit v1 on v0

v1 whole, which is shorter than its diff:
```python
import functools

import jax
import jax.numpy as jnp
from jax import lax
from jax.experimental import pallas as pl
from jax.experimental.pallas import tpu as pltpu
from jax.sharding import PartitionSpec as P

E_W = 4
SLOT = 10
SLAB = 16
AHEAD0 = 2
AHEAD1 = 2
WINDOW = 3
MIB = 1 << 20
VMEM = pltpu.VMEM
HBM = pltpu.HBM


def spec(space):
    return pl.BlockSpec(memory_space=space)


def dot(a, b, dims=(((1,), (0,)), ((), ()))):
    return lax.dot_general(a, b, dims, preferred_element_type=jnp.float32)


def iota(shape, dim):
    return lax.broadcasted_iota(jnp.int32, shape, dim)


def select_kernel(n, ids_ref, route_ref, tok_ref, comb_ref, *slabs):
    me = lax.axis_index("expert")
    replicas = n // E_W
    ids, route, tok = ids_ref[...], route_ref[...], tok_ref[...]
    count = tok.shape[0]
    before = (iota((count, count), 0) <= iota((count, count), 1)).astype(jnp.bfloat16)
    slot = iota((SLAB, count), 0).astype(jnp.float32)
    for k in range(n):
        hit = ids == (me ^ k) // replicas
        member = jnp.sum(jnp.where(hit, 1.0, 0.0), axis=0, keepdims=True)
        weight = jnp.sum(jnp.where(hit, route, 0.0), axis=0, keepdims=True)
        member = jnp.broadcast_to(member, (SLAB, count))
        position = dot(member.astype(jnp.bfloat16), before) - 1.0
        placed = jnp.where(position == slot, member, 0.0)
        slabs[k][...] = dot(placed.astype(jnp.bfloat16), tok).astype(jnp.bfloat16)
        comb_ref[k * SLAB : (k + 1) * SLAB, :] = placed * weight


def select(n, ids, route, tokens):
    count, width = tokens.shape
    out = pl.pallas_call(
        functools.partial(select_kernel, n),
        out_shape=[VMEM((n * SLAB, count), jnp.float32)]
        + [VMEM((SLAB, width), jnp.bfloat16)] * n,
        in_specs=[spec(VMEM)] * 3,
        out_specs=[spec(VMEM)] * (n + 1),
        compiler_params=pltpu.CompilerParams(vmem_limit_bytes=4 * MIB),
        name="select",
    )(ids, route, tokens)
    return out[0], out[1:]


def compact_kernel(n, *refs):
    slabs, rows_ref = refs[:n], refs[-1]
    full = jnp.concatenate([ref[...] for ref in slabs], axis=0)
    col = iota((n * SLOT, n * SLAB), 1)
    s = col % SLAB
    take = (iota((n * SLOT, n * SLAB), 0) == (col // SLAB) * SLOT + s) & (s < SLOT)
    rows_ref[...] = dot(take.astype(jnp.bfloat16), full).astype(jnp.bfloat16)


def compact(slabs, after):
    n, width = len(slabs), slabs[0].shape[1]
    return pl.pallas_call(
        functools.partial(compact_kernel, n),
        out_shape=VMEM((n * SLOT, width), jnp.bfloat16),
        in_specs=[spec(VMEM)] * (n + 1),
        out_specs=spec(VMEM),
        compiler_params=pltpu.CompilerParams(vmem_limit_bytes=4 * MIB),
        name="compact",
    )(*slabs, after)


def half_rows(unit, half, q):
    return pl.ds(pl.multiple_of((q ^ (unit // 2)) * 2 * half + (unit % 2) * half, 128), half)


def fetch_kernel(units, half, order_ref, gate_hbm, up_hbm, gate_ref, up_ref, sems):
    q = lax.axis_index("tensor")
    copies = []
    for i, unit in enumerate(units):
        at = half_rows(unit, half, q)
        copies.append(pltpu.make_async_copy(gate_hbm.at[at, :], gate_ref.at[i], sems.at[0, i]))
        copies.append(pltpu.make_async_copy(up_hbm.at[at, :], up_ref.at[i], sems.at[1, i]))
    for copy in copies:
        copy.start()
    for copy in copies:
        copy.wait()


def fetch(units, half, order, w_gate, w_up):
    shape = (len(units), half, w_gate.shape[1])
    return pl.pallas_call(
        functools.partial(fetch_kernel, units, half),
        out_shape=[VMEM(shape, jnp.bfloat16)] * 2,
        in_specs=[spec(VMEM)] + [spec(HBM)] * 2,
        out_specs=[spec(VMEM)] * 2,
        scratch_shapes=[pltpu.SemaphoreType.DMA((2, len(units)))],
        compiler_params=pltpu.CompilerParams(vmem_limit_bytes=2 * MIB),
        cost_estimate=pl.CostEstimate(
            flops=0, bytes_accessed=4 * shape[0] * shape[1] * shape[2], transcendentals=0
        ),
        name="fetch",
    )(order, w_gate, w_up)


def own_kernel(
    units, half, rows_ref, gate0, up0, gate_hbm, up_hbm, sum_g, sum_u, gate_ref, up_ref, sems
):
    q = lax.axis_index("tensor")
    copies = []
    for i, unit in enumerate(units):
        at = half_rows(unit, half, q)
        copies.append(pltpu.make_async_copy(gate_hbm.at[at, :], gate_ref.at[i], sems.at[0, i]))
        copies.append(pltpu.make_async_copy(up_hbm.at[at, :], up_ref.at[i], sems.at[1, i]))
    for copy in copies:
        copy.start()
    low, high = rows_ref[:, :half], rows_ref[:, half:]
    sum_g[...] = dot(low, gate0[0]) + dot(high, gate0[1])
    sum_u[...] = dot(low, up0[0]) + dot(high, up0[1])
    for copy in copies:
        copy.wait()


def own(units, half, rows, gate0, up0, w_gate, w_up):
    m, n = rows.shape[0], w_gate.shape[1]
    shape = (len(units), half, n)
    return pl.pallas_call(
        functools.partial(own_kernel, units, half),
        out_shape=[VMEM((m, n), jnp.float32)] * 2 + [VMEM(shape, jnp.bfloat16)] * 2,
        in_specs=[spec(VMEM)] * 3 + [spec(HBM)] * 2,
        out_specs=[spec(VMEM)] * 4,
        scratch_shapes=[pltpu.SemaphoreType.DMA((2, len(units)))],
        compiler_params=pltpu.CompilerParams(vmem_limit_bytes=4 * MIB),
        cost_estimate=pl.CostEstimate(
            flops=0, bytes_accessed=4 * shape[0] * shape[1] * shape[2], transcendentals=0
        ),
        name="own",
    )(rows, gate0, up0, w_gate, w_up)


def rest_kernel(parts, first, half, outs, *refs):
    rows = refs[: parts - 1]
    sum_g, sum_u, gate1, up1, gate_hbm, up_hbm, down_hbm = refs[parts - 1 : parts + 6]
    hidden_ref = refs[parts + 6]
    sent = refs[parts + 7 : parts + 7 + len(outs)]
    ring, down2, acc_g, acc_u, sems, down_sems = refs[parts + 7 + len(outs) :]
    q = lax.axis_index("tensor")
    count = 2 * parts
    queue = []
    for unit in range(first, count):
        for source in (gate_hbm, up_hbm):
            slot = len(queue) % (WINDOW + 1)
            at = half_rows(unit, half, q)
            queue.append(
                pltpu.make_async_copy(source.at[at, :], ring.at[slot], sems.at[slot])
            )
    jobs = len(queue)
    for i, k in enumerate(outs):
        at = pl.ds(pl.multiple_of((q ^ k) * 2 * half, 128), 2 * half)
        queue.append(pltpu.make_async_copy(down_hbm.at[:, at], down2.at[i], down_sems.at[i]))
    for copy in queue[:WINDOW]:
        copy.start()

    def arrive(job):
        queue[job].wait()
        if job + WINDOW < len(queue):
            queue[job + WINDOW].start()

    acc_g[...] = sum_g[...]
    acc_u[...] = sum_u[...]
    for unit in range(2, count):
        row = rows[unit // 2 - 1]
        row = row[:, half:] if unit % 2 else row[:, :half]
        if unit < first:
            acc_g[...] += dot(row, gate1[unit - 2])
            acc_u[...] += dot(row, up1[unit - 2])
        else:
            job = 2 * (unit - first)
            arrive(job)
            acc_g[...] += dot(row, ring[job % (WINDOW + 1)])
            arrive(job + 1)
            acc_u[...] += dot(row, ring[(job + 1) % (WINDOW + 1)])
    gate = acc_g[...]
    hidden = (gate / (1.0 + jnp.exp(-gate)) * acc_u[...]).astype(jnp.bfloat16)
    hidden_ref[...] = hidden
    for i in range(len(outs)):
        arrive(jobs + i)
        sent[i][...] = dot(hidden_ref[...], down2[i]).astype(jnp.bfloat16)


def rest(parts, first, half, outs, rows, sum_g, sum_u, gate1, up1, w_gate, w_up, w_down):
    m, n = sum_g.shape
    left = 2 * parts - first
    width = 2 * half
    return pl.pallas_call(
        functools.partial(rest_kernel, parts, first, half, outs),
        out_shape=[VMEM((m, n), jnp.bfloat16)] + [VMEM((m, width), jnp.bfloat16)] * len(outs),
        in_specs=[spec(VMEM)] * (parts - 1 + 4) + [spec(HBM)] * 3,
        out_specs=[spec(VMEM)] * (1 + len(outs)),
        scratch_shapes=[
            VMEM((WINDOW + 1, half, n), jnp.bfloat16),
            VMEM((len(outs), n, width), jnp.bfloat16),
            VMEM((m, n), jnp.float32),
            VMEM((m, n), jnp.float32),
            pltpu.SemaphoreType.DMA((WINDOW + 1,)),
            pltpu.SemaphoreType.DMA((len(outs),)),
        ],
        compiler_params=pltpu.CompilerParams(vmem_limit_bytes=30 * MIB),
        cost_estimate=pl.CostEstimate(
            flops=0, bytes_accessed=4 * left * half * n, transcendentals=0
        ),
        name="rest",
    )(*rows, sum_g, sum_u, gate1, up1, w_gate, w_up, w_down)


def down_kernel(outs, width, hidden_ref, down_hbm, *refs):
    sent = refs[: len(outs)]
    buf, sems = refs[len(outs) :]
    q = lax.axis_index("tensor")
    downs = []
    for i, k in enumerate(outs):
        at = pl.ds(pl.multiple_of((q ^ k) * width, 128), width)
        downs.append(pltpu.make_async_copy(down_hbm.at[:, at], buf.at[i], sems.at[i]))
    for copy in downs:
        copy.start()
    for i in range(len(outs)):
        downs[i].wait()
        sent[i][...] = dot(hidden_ref[...], buf[i]).astype(jnp.bfloat16)


def down(outs, width, hidden, w_down):
    m, n = hidden.shape
    return pl.pallas_call(
        functools.partial(down_kernel, outs, width),
        out_shape=[VMEM((m, width), jnp.bfloat16)] * len(outs),
        in_specs=[spec(VMEM), spec(HBM)],
        out_specs=[spec(VMEM)] * len(outs),
        scratch_shapes=[
            VMEM((len(outs), n, width), jnp.bfloat16),
            pltpu.SemaphoreType.DMA((len(outs),)),
        ],
        compiler_params=pltpu.CompilerParams(vmem_limit_bytes=20 * MIB),
        cost_estimate=pl.CostEstimate(
            flops=0, bytes_accessed=2 * len(outs) * n * width, transcendentals=0
        ),
        name="down",
    )(hidden, w_down)


def add_kernel(n, parts, *refs):
    terms, slabs = refs[:parts], refs[parts:]
    total = terms[0][...].astype(jnp.float32)
    for term in terms[1:]:
        total = total + term[...].astype(jnp.float32)
    total = total.astype(jnp.bfloat16)
    s, row = iota((SLAB, n * SLOT), 0), iota((SLAB, n * SLOT), 1)
    for k in range(n):
        take = (row == s + k * SLOT) & (s < SLOT)
        slabs[k][...] = dot(take.astype(jnp.bfloat16), total).astype(jnp.bfloat16)


def add(n, terms):
    width = terms[0].shape[1]
    return pl.pallas_call(
        functools.partial(add_kernel, n, len(terms)),
        out_shape=[VMEM((SLAB, width), jnp.bfloat16)] * n,
        in_specs=[spec(VMEM)] * len(terms),
        out_specs=[spec(VMEM)] * n,
        compiler_params=pltpu.CompilerParams(vmem_limit_bytes=4 * MIB),
        name="add",
    )(*terms)


def combine_kernel(n, comb_ref, *refs):
    slabs, out_ref = refs[:n], refs[n]
    full = jnp.concatenate([ref[...] for ref in slabs], axis=0)
    comb = comb_ref[...].T
    high = comb.astype(jnp.bfloat16)
    comb = comb - high.astype(jnp.float32)
    mid = comb.astype(jnp.bfloat16)
    low = (comb - mid.astype(jnp.float32)).astype(jnp.bfloat16)
    out_ref[...] = (dot(high, full) + (dot(mid, full) + dot(low, full))).astype(jnp.bfloat16)


def combine(comb, slabs):
    n, width = len(slabs), slabs[0].shape[1]
    return pl.pallas_call(
        functools.partial(combine_kernel, n),
        out_shape=jax.ShapeDtypeStruct((comb.shape[1], width), jnp.bfloat16),
        in_specs=[spec(VMEM)] * (n + 1),
        out_specs=spec(VMEM),
        compiler_params=pltpu.CompilerParams(vmem_limit_bytes=4 * MIB),
        name="combine",
    )(comb, *slabs)


def swap(x, axis, k):
    size = lax.axis_size(axis)
    return lax.ppermute(x, axis, [(i, i ^ k) for i in range(size)])


def per_device(tokens, expert_ids, route_weights, w_gate, w_up, w_down):
    n, parts = lax.axis_size("expert"), lax.axis_size("tensor")
    width = tokens.shape[1]
    half = width // 2
    w_gate, w_up, w_down = (
        pltpu.with_memory_space_constraint(w, HBM) for w in (w_gate, w_up, w_down)
    )
    comb, slabs = select(n, expert_ids.T, route_weights.T, tokens)
    slabs = [slabs[0]] + [swap(slabs[k], "expert", k) for k in range(1, n)]
    gate0, up0 = fetch(range(0, AHEAD0), half, comb, w_gate, w_up)
    mine = compact(slabs, gate0)
    rows = [swap(mine, "tensor", k) for k in range(1, parts)]
    first = AHEAD0 + AHEAD1
    sum_g, sum_u, gate1, up1 = own(range(AHEAD0, first), half, mine, gate0, up0, w_gate, w_up)
    early = list(range(parts - 1, 1, -1))
    hidden, *sent = rest(
        parts, first, half, early, rows, sum_g, sum_u, gate1, up1, w_gate, w_up, w_down
    )
    terms = [swap(x, "tensor", k) for k, x in zip(early, sent)]
    last, kept = down([1, 0], width, hidden, w_down)
    terms = [kept, swap(last, "tensor", 1)] + terms
    back = add(n, terms)
    back = [back[0]] + [swap(back[k], "expert", k) for k in range(1, n)]
    return combine(comb, back)


def solution(mesh):
    return jax.shard_map(
        per_device,
        mesh=mesh,
        in_specs=(
            P(("groups", "expert"), "tensor"),
            P(("groups", "expert"), None),
            P(("groups", "expert"), None),
            P(None, ("expert", "tensor")),
            P(None, ("expert", "tensor")),
            P(("expert", "tensor"), None),
        ),
        out_specs=P(("groups", "expert"), "tensor"),
        check_vma=False,
    )
```

time: 119 us -> 60.5 us (0.51)
  blocking collectives: 36.6 us -> 0 us
  matrix products: 33.8 us -> 0 us
  Pallas kernels: 0 us -> 32.9 us
  waiting for transfers between devices: 27.6 us -> 11.6 us
  between operations: 13.4 us -> 0.11 us
  starting transfers between devices: 4.6 us -> 13.4 us
    dot_general x5 -> x0, matrix products: 33.8 us -> none  [the longest x1 11.3 us: per_device(): lax.dot_general(w_down, hidden, (((0,), (1,)), ((), ())), preferred_eleme...]
    pallas_call x0 -> x8, Pallas kernels: none -> 32.9 us  [the longest x1 13.3 us: rest(): pl.pallas_call(functools.partial(rest_kernel, parts, first, half, outs),...]
    all_to_all x1 -> x0, blocking collectives: 25.3 us -> none  [per_device(): lax.all_to_all(outgoing, 'expert', split_axis=0, concat_axis=0, tiled=True)]
    reduce_scatter x1 -> x0, waiting for transfers between devices: 20.3 us -> none  [per_device(): lax.psum_scatter(lax.dot_general(w_down, hidden, (((0,), (1,)), ((), ()))...]
    ppermute x0 -> x12, starting transfers between devices: none -> 13.4 us  [swap(): return lax.ppermute(x, axis, [(i, i ^ k) for i in range(size)])]
    ppermute x0 -> x12, waiting for transfers between devices: none -> 11.6 us  [swap(): return lax.ppermute(x, axis, [(i, i ^ k) for i in range(size)])]
    all_gather x1 -> x0, blocking collectives: 11.3 us -> none  [per_device(): full_rows = lax.all_gather(tokens, 'tensor', axis=1, tiled=True)]
    all_to_all x1 -> x0, waiting for transfers between devices: 7.36 us -> none  [per_device(): lax.all_to_all(summed, 'expert', split_axis=1, concat_axis=1, tiled=True)]
  transfers between devices with their start and end apart: 2 -> 12, of which waited for: 2 -> 6; matrix products, arithmetic and copies ran while one was open for 0% -> 0% of each run, Pallas kernels for 0% -> 19%
where the time goes in v1:
time: 60.5 us; the launch traced here: 60.3 us
  Pallas kernels  32.9 us (54%)
  starting transfers between devices  13.4 us (22%)
  waiting for transfers between devices  11.6 us (19%)
  local copies, waits for them, and re-layouts  2.31 us (4%)
    ppermute x12, starting transfers between devices, swap(): return lax.ppermute(x, axis, [(i, i ^ k) for i in range(size)])  13.4 us
    pallas_call x1, Pallas kernels, rest(): pl.pallas_call(functools.partial(rest_kernel, parts, first, half, outs),...  13.3 us
    ppermute x12, waiting for transfers between devices, swap(): return lax.ppermute(x, axis, [(i, i ^ k) for i in range(size)])  11.6 us
    pallas_call x1, Pallas kernels, own(): pl.pallas_call(functools.partial(own_kernel, units, half), out_shape=[VME...  6.84 us
    pallas_call x1, Pallas kernels, down(): pl.pallas_call(functools.partial(down_kernel, outs, width), out_shape=[VM...  5.83 us
    pallas_call x1, Pallas kernels, fetch(): pl.pallas_call(functools.partial(fetch_kernel, units, half), out_shape=[V...  4.68 us
    unnamed x6, local copies, waits for them, and re-layouts  2.31 us
  transfers between devices with their start and end apart: 12, of which 6 were waited for; matrix products, arithmetic and copies ran while one was open for 0% of the time, Pallas kernels for 19%

profile of v1, /device:TPU:0, one launch (start us, length us, event | category | flops | bytes accessed | tf_op | source)
XLA Modules:
  0.0 60.3 jit_solution(10235148367970040157)
XLA Ops:
  0.0 0.9 %copy-done = bf16[80,1536]{1,0:T(8,128)(2,1)S(1)} copy-done((bf16[80,1536]{1,0:T(8,128)(2,1)S(1)}, bf16[80,1536]{1,0:T(8,128)(2,1)}, u32[]{:S(2)}) %copy-start) | copy-done | bytes 245784
  0.9 0.7 %copy-done.1 = s32[80,4]{0,1:T(4,128)S(1)} copy-done((s32[80,4]{0,1:T(4,128)S(1)}, s32[80,4]{0,1:T(4,128)}, u32[]{:S(2)}) %copy-start.1) | copy-done | bytes 1304
  1.6 0.7 %copy-done.2 = f32[80,4]{0,1:T(4,128)S(1)} copy-done((f32[80,4]{0,1:T(4,128)S(1)}, f32[80,4]{0,1:T(4,128)}, u32[]{:S(2)}) %copy-start.2) | copy-done | bytes 1304
  2.3 0.7 %select.1 = (f32[64,80]{1,0:T(8,128)S(1)}, bf16[16,1536]{1,0:T(8,128)(2,1)S(1)}, bf16[16,1536]{1,0:T(8,128)(2,1)S(1)}, bf16[16,1536]{1,0:T(8,128)(2,1)S(1)}, bf16[16,1536]{1,0:T(8,128)(2,1)S(1)}) custom-call(s32[4,80]{1,0:T(4,128)S(1)} %bitcast.2, f32[4,80]{1,0:T(4,128)S(1)} %bitcast.3, bf16[80,1536]{1,0:T(8,128)(2,1)S(1)} %copy-done), custom_call_target="tpu_custom_call" | custom-call | tf_op jit(solution)/shard_map/select/pallas_call | solution.py:53
  3.0 3.1 %collective-permute-start = (bf16[16,1536]{1,0:T(8,128)(2,1)S(1)}, bf16[16,1536]{1,0:T(8,128)(2,1)S(1)}, u32[]{:S(2)}, u32[]{:S(2)}) collective-permute-start(bf16[16,1536]{1,0:T(8,128)(2,1)S(1)} %get-tuple-element.27), channel_id=1, source_target_pairs={{0,4},{4,0},{8,12},{12,8},{1,5},{5,1},{9,13},{13,9},{2,6},{6,2},{1... | collective-permute-start | bytes 147464 | tf_op jit(solution)/shard_map/ppermute | solution.py:312
  6.1 2.6 %collective-permute-start.1 = (bf16[16,1536]{1,0:T(8,128)(2,1)S(1)}, bf16[16,1536]{1,0:T(8,128)(2,1)S(1)}, u32[]{:S(2)}, u32[]{:S(2)}) collective-permute-start(bf16[16,1536]{1,0:T(8,128)(2,1)S(1)} %get-tuple-element.28), channel_id=1, source_target_pairs={{0,8},{4,12},{8,0},{12,4},{1,9},{5,13},{9,1},{13,5},{2,10},{6,14},... | collective-permute-start | bytes 147464 | tf_op jit(solution)/shard_map/ppermute | solution.py:312
  8.7 4.7 %fetch.1 = (bf16[2,768,2048]{2,1,0:T(8,128)(2,1)S(1)}, bf16[2,768,2048]{2,1,0:T(8,128)(2,1)S(1)}) custom-call(f32[64,80]{1,0:T(8,128)S(1)} %get-tuple-element.25.order_ref.comb_ref, bf16[6144,2048]{1,0:T(8,128)(2,1)} %refs_7_.1, bf16[6144,2048]{1,0:T(8,128)(2,1)} %refs_8_.1), custom_call_target="tpu_custom_call" | custom-call | bytes 12582912 | tf_op jit(solution)/shard_map/fetch/pallas_call | solution.py:105
  13.4 1.2 %collective-permute-done.2.refs_3_ = bf16[16,1536]{1,0:T(8,128)(2,1)S(1)} collective-permute-done((bf16[16,1536]{1,0:T(8,128)(2,1)S(1)}, bf16[16,1536]{1,0:T(8,128)(2,1)S(1)}, u32[]{:S(2)}, u32[]{:S(2)}) %collective-permute-start.2) | collective-permute-done | bytes 49184 | tf_op jit(solution)/shard_map/ppermute | solution.py:312
  14.8 1.6 %collective-permute-start.4 = (bf16[40,1536]{1,0:T(8,128)(2,1)S(1)}, bf16[40,1536]{1,0:T(8,128)(2,1)S(1)}, u32[]{:S(2)}, u32[]{:S(2)}) collective-permute-start(bf16[40,1536]{1,0:T(8,128)(2,1)S(1)} %compact.1.rows_ref), channel_id=1, source_target_pairs={{0,2},{1,3},{2,0},{3,1},{4,6},{5,7},{6,4},{7,5},{8,10},{9,11},{10,... | collective-permute-start | bytes 368648 | tf_op jit(solution)/shard_map/ppermute | solution.py:312
  16.4 0.3 collective-permute-start.5
  16.7 6.8 %own.1 = (f32[40,2048]{1,0:T(8,128)S(1)}, f32[40,2048]{1,0:T(8,128)S(1)}, bf16[2,768,2048]{2,1,0:T(8,128)(2,1)S(1)}, bf16[2,768,2048]{2,1,0:T(8,128)(2,1)S(1)}) custom-call(bf16[40,1536]{1,0:T(8,128)(2,1)S(1)} %compact.1.rows_ref, bf16[2,768,2048]{2,1,0:T(8,128)(2,1)S(1)} %get-tuple-element.30.refs_4_.gate0, ...), custom_call_target="tpu_custom_call" | custom-call | bytes 12582912 | tf_op jit(solution)/shard_map/own/pallas_call | solution.py:140
  23.6 13.3 %rest.1 = (bf16[40,2048]{1,0:T(8,128)(2,1)S(1)}, bf16[40,1536]{1,0:T(8,128)(2,1)S(1)}, bf16[40,1536]{1,0:T(8,128)(2,1)S(1)}) custom-call(bf16[40,1536]{1,0:T(8,128)(2,1)S(1)} %collective-permute-done.3.refs_0_, bf16[40,1536]{1,0:T(8,128)(2,1)S(1)} %collective-permute-done.4.refs_1_, bf16[40,1536]{1,0:T(8,128)(2,1)S(1)} %collective-permute-done.5.refs_2_, ...), custom_call_target="tpu_custom_call" | custom-call | bytes 25165824 | tf_op jit(solution)/shard_map/rest/pallas_call | solution.py:208
  36.9 5.8 %down.1 = (bf16[40,1536]{1,0:T(8,128)(2,1)S(1)}, bf16[40,1536]{1,0:T(8,128)(2,1)S(1)}) custom-call(bf16[40,2048]{1,0:T(8,128)(2,1)S(1)} %get-tuple-element.36.hidden_ref, bf16[2048,6144]{1,0:T(8,128)(2,1)} %down_hbm.1), custom_call_target="tpu_custom_call" | custom-call | bytes 12582912 | tf_op jit(solution)/shard_map/down/pallas_call | solution.py:246
  42.7 0.4 collective-permute-start.6
  43.1 1.3 %collective-permute-start.7 = (bf16[40,1536]{1,0:T(8,128)(2,1)S(1)}, bf16[40,1536]{1,0:T(8,128)(2,1)S(1)}, u32[]{:S(2)}, u32[]{:S(2)}) collective-permute-start(bf16[40,1536]{1,0:T(8,128)(2,1)S(1)} %get-tuple-element.39), channel_id=1, source_target_pairs={{0,3},{1,2},{2,1},{3,0},{4,7},{5,6},{6,5},{7,4},{8,11},{9,10},{10,... | collective-permute-start | bytes 368648 | tf_op jit(solution)/shard_map/ppermute | solution.py:312
  44.4 0.5 collective-permute-start.8
  44.9 3.5 %collective-permute-done.7.refs_2_ = bf16[40,1536]{1,0:T(8,128)(2,1)S(1)} collective-permute-done((bf16[40,1536]{1,0:T(8,128)(2,1)S(1)}, bf16[40,1536]{1,0:T(8,128)(2,1)S(1)}, u32[]{:S(2)}, u32[]{:S(2)}) %collective-permute-start.7) | collective-permute-done | bytes 122912 | tf_op jit(solution)/shard_map/ppermute | solution.py:312
  48.4 3.0 %collective-permute-done.8.refs_3_ = bf16[40,1536]{1,0:T(8,128)(2,1)S(1)} collective-permute-done((bf16[40,1536]{1,0:T(8,128)(2,1)S(1)}, bf16[40,1536]{1,0:T(8,128)(2,1)S(1)}, u32[]{:S(2)}, u32[]{:S(2)}) %collective-permute-start.8) | collective-permute-done | bytes 122912 | tf_op jit(solution)/shard_map/ppermute | solution.py:312
  51.6 0.8 %collective-permute-start.10 = (bf16[16,1536]{1,0:T(8,128)(2,1)S(1)}, bf16[16,1536]{1,0:T(8,128)(2,1)S(1)}, u32[]{:S(2)}, u32[]{:S(2)}) collective-permute-start(bf16[16,1536]{1,0:T(8,128)(2,1)S(1)} %get-tuple-element.43), channel_id=1, source_target_pairs={{0,8},{4,12},{8,0},{12,4},{1,9},{5,13},{9,1},{13,5},{2,10},{6,14},... | collective-permute-start | bytes 147464 | tf_op jit(solution)/shard_map/ppermute | solution.py:312
  52.5 2.0 %collective-permute-start.11 = (bf16[16,1536]{1,0:T(8,128)(2,1)S(1)}, bf16[16,1536]{1,0:T(8,128)(2,1)S(1)}, u32[]{:S(2)}, u32[]{:S(2)}) collective-permute-start(bf16[16,1536]{1,0:T(8,128)(2,1)S(1)} %get-tuple-element.44), channel_id=1, source_target_pairs={{0,12},{4,8},{8,4},{12,0},{1,13},{5,9},{9,5},{13,1},{2,14},{6,10},... | collective-permute-start | bytes 147464 | tf_op jit(solution)/shard_map/ppermute | solution.py:312
  54.5 0.8 %collective-permute-start.9 = (bf16[16,1536]{1,0:T(8,128)(2,1)S(1)}, bf16[16,1536]{1,0:T(8,128)(2,1)S(1)}, u32[]{:S(2)}, u32[]{:S(2)}) collective-permute-start(bf16[16,1536]{1,0:T(8,128)(2,1)S(1)} %get-tuple-element.42), channel_id=1, source_target_pairs={{0,4},{4,0},{8,12},{12,8},{1,5},{5,1},{9,13},{13,9},{2,6},{6,2},{1... | collective-permute-start | bytes 147464 | tf_op jit(solution)/shard_map/ppermute | solution.py:312
  55.2 3.1 %collective-permute-done.10.refs_2_ = bf16[16,1536]{1,0:T(8,128)(2,1)S(1)} collective-permute-done((bf16[16,1536]{1,0:T(8,128)(2,1)S(1)}, bf16[16,1536]{1,0:T(8,128)(2,1)S(1)}, u32[]{:S(2)}, u32[]{:S(2)}) %collective-permute-start.10) | collective-permute-done | bytes 49184 | tf_op jit(solution)/shard_map/ppermute | solution.py:312
  58.3 0.6 %collective-permute-done.11.refs_3_ = bf16[16,1536]{1,0:T(8,128)(2,1)S(1)} collective-permute-done((bf16[16,1536]{1,0:T(8,128)(2,1)S(1)}, bf16[16,1536]{1,0:T(8,128)(2,1)S(1)}, u32[]{:S(2)}, u32[]{:S(2)}) %collective-permute-start.11) | collective-permute-done | bytes 49184 | tf_op jit(solution)/shard_map/ppermute | solution.py:312
  59.2 1.1 %combine.1 = bf16[80,1536]{1,0:T(8,128)(2,1)} custom-call(f32[64,80]{1,0:T(8,128)S(1)} %get-tuple-element.25.order_ref.comb_ref, bf16[16,1536]{1,0:T(8,128)(2,1)S(1)} %get-tuple-element.41.refs_0_, bf16[16,1536]{1,0:T(8,128)(2,1)S(1)} %collective-permute-done.9.refs_1_, bf16[16,1536]{1,0:T(8,128)(2,1)S(1)} %collective-permute-done.10.refs_2_, ...), custom_call_target="tpu_custom_call" | custom-call | tf_op jit(solution)/shard_map/combine/pallas_call | solution.py:300
  (14 shorter events, 0.8 us)
Async XLA Ops:
  0.0 0.9 %copy-start = (bf16[80,1536]{1,0:T(8,128)(2,1)S(1)}, bf16[80,1536]{1,0:T(8,128)(2,1)}, u32[]{:S(2)}) copy-start(bf16[80,1536]{1,0:T(8,128)(2,1)} %tok_ref.1) | copy-start | bytes 737284
  0.9 0.7 %copy-start.1 = (s32[80,4]{0,1:T(4,128)S(1)}, s32[80,4]{0,1:T(4,128)}, u32[]{:S(2)}) copy-start(s32[80,4]{0,1:T(4,128)} %param.7) | copy-start | bytes 3844
  1.6 0.7 %copy-start.2 = (f32[80,4]{0,1:T(4,128)S(1)}, f32[80,4]{0,1:T(4,128)}, u32[]{:S(2)}) copy-start(f32[80,4]{0,1:T(4,128)} %param.8) | copy-start | bytes 3844
  3.0 10.4 %collective-permute-start = (bf16[16,1536]{1,0:T(8,128)(2,1)S(1)}, bf16[16,1536]{1,0:T(8,128)(2,1)S(1)}, u32[]{:S(2)}, u32[]{:S(2)}) collective-permute-start(bf16[16,1536]{1,0:T(8,128)(2,1)S(1)} %get-tuple-element.27), channel_id=1, source_target_pairs={{0,4},{4,0},{8,12},{12,8},{1,5},{5,1},{9,13},{13,9},{2,6},{6,2},{1... | collective-permute-start | bytes 147464 | tf_op jit(solution)/shard_map/ppermute | solution.py:312
  6.1 7.3 %collective-permute-start.1 = (bf16[16,1536]{1,0:T(8,128)(2,1)S(1)}, bf16[16,1536]{1,0:T(8,128)(2,1)S(1)}, u32[]{:S(2)}, u32[]{:S(2)}) collective-permute-start(bf16[16,1536]{1,0:T(8,128)(2,1)S(1)} %get-tuple-element.28), channel_id=1, source_target_pairs={{0,8},{4,12},{8,0},{12,4},{1,9},{5,13},{9,1},{13,5},{2,10},{6,14},... | collective-permute-start | bytes 147464 | tf_op jit(solution)/shard_map/ppermute | solution.py:312
  8.7 5.9 %collective-permute-start.2 = (bf16[16,1536]{1,0:T(8,128)(2,1)S(1)}, bf16[16,1536]{1,0:T(8,128)(2,1)S(1)}, u32[]{:S(2)}, u32[]{:S(2)}) collective-permute-start(bf16[16,1536]{1,0:T(8,128)(2,1)S(1)} %get-tuple-element.29), channel_id=1, source_target_pairs={{0,12},{4,8},{8,4},{12,0},{1,13},{5,9},{9,5},{13,1},{2,14},{6,10},... | collective-permute-start | bytes 147464 | tf_op jit(solution)/shard_map/ppermute | solution.py:312
  14.8 8.8 %collective-permute-start.3 = (bf16[40,1536]{1,0:T(8,128)(2,1)S(1)}, bf16[40,1536]{1,0:T(8,128)(2,1)S(1)}, u32[]{:S(2)}, u32[]{:S(2)}) collective-permute-start(bf16[40,1536]{1,0:T(8,128)(2,1)S(1)} %compact.1.rows_ref), channel_id=1, source_target_pairs={{0,1},{1,0},{2,3},{3,2},{4,5},{5,4},{6,7},{7,6},{8,9},{9,8},{10,11... | collective-permute-start | bytes 368648 | tf_op jit(solution)/shard_map/ppermute | solution.py:312
  14.8 8.7 %collective-permute-start.4 = (bf16[40,1536]{1,0:T(8,128)(2,1)S(1)}, bf16[40,1536]{1,0:T(8,128)(2,1)S(1)}, u32[]{:S(2)}, u32[]{:S(2)}) collective-permute-start(bf16[40,1536]{1,0:T(8,128)(2,1)S(1)} %compact.1.rows_ref), channel_id=1, source_target_pairs={{0,2},{1,3},{2,0},{3,1},{4,6},{5,7},{6,4},{7,5},{8,10},{9,11},{10,... | collective-permute-start | bytes 368648 | tf_op jit(solution)/shard_map/ppermute | solution.py:312
  16.4 7.2 %collective-permute-start.5 = (bf16[40,1536]{1,0:T(8,128)(2,1)S(1)}, bf16[40,1536]{1,0:T(8,128)(2,1)S(1)}, u32[]{:S(2)}, u32[]{:S(2)}) collective-permute-start(bf16[40,1536]{1,0:T(8,128)(2,1)S(1)} %compact.1.rows_ref), channel_id=1, source_target_pairs={{0,3},{1,2},{2,1},{3,0},{4,7},{5,6},{6,5},{7,4},{8,11},{9,10},{10,... | collective-permute-start | bytes 368648 | tf_op jit(solution)/shard_map/ppermute | solution.py:312
  42.7 2.2 %collective-permute-start.6 = (bf16[40,1536]{1,0:T(8,128)(2,1)S(1)}, bf16[40,1536]{1,0:T(8,128)(2,1)S(1)}, u32[]{:S(2)}, u32[]{:S(2)}) collective-permute-start(bf16[40,1536]{1,0:T(8,128)(2,1)S(1)} %get-tuple-element.38), channel_id=1, source_target_pairs={{0,1},{1,0},{2,3},{3,2},{4,5},{5,4},{6,7},{7,6},{8,9},{9,8},{10,11... | collective-permute-start | bytes 368648 | tf_op jit(solution)/shard_map/ppermute | solution.py:312
  43.1 5.3 %collective-permute-start.7 = (bf16[40,1536]{1,0:T(8,128)(2,1)S(1)}, bf16[40,1536]{1,0:T(8,128)(2,1)S(1)}, u32[]{:S(2)}, u32[]{:S(2)}) collective-permute-start(bf16[40,1536]{1,0:T(8,128)(2,1)S(1)} %get-tuple-element.39), channel_id=1, source_target_pairs={{0,3},{1,2},{2,1},{3,0},{4,7},{5,6},{6,5},{7,4},{8,11},{9,10},{10,... | collective-permute-start | bytes 368648 | tf_op jit(solution)/shard_map/ppermute | solution.py:312
  44.4 7.0 %collective-permute-start.8 = (bf16[40,1536]{1,0:T(8,128)(2,1)S(1)}, bf16[40,1536]{1,0:T(8,128)(2,1)S(1)}, u32[]{:S(2)}, u32[]{:S(2)}) collective-permute-start(bf16[40,1536]{1,0:T(8,128)(2,1)S(1)} %get-tuple-element.40), channel_id=1, source_target_pairs={{0,2},{1,3},{2,0},{3,1},{4,6},{5,7},{6,4},{7,5},{8,10},{9,11},{10,... | collective-permute-start | bytes 368648 | tf_op jit(solution)/shard_map/ppermute | solution.py:312
  51.6 6.6 %collective-permute-start.10 = (bf16[16,1536]{1,0:T(8,128)(2,1)S(1)}, bf16[16,1536]{1,0:T(8,128)(2,1)S(1)}, u32[]{:S(2)}, u32[]{:S(2)}) collective-permute-start(bf16[16,1536]{1,0:T(8,128)(2,1)S(1)} %get-tuple-element.43), channel_id=1, source_target_pairs={{0,8},{4,12},{8,0},{12,4},{1,9},{5,13},{9,1},{13,5},{2,10},{6,14},... | collective-permute-start | bytes 147464 | tf_op jit(solution)/shard_map/ppermute | solution.py:312
  52.5 6.4 %collective-permute-start.11 = (bf16[16,1536]{1,0:T(8,128)(2,1)S(1)}, bf16[16,1536]{1,0:T(8,128)(2,1)S(1)}, u32[]{:S(2)}, u32[]{:S(2)}) collective-permute-start(bf16[16,1536]{1,0:T(8,128)(2,1)S(1)} %get-tuple-element.44), channel_id=1, source_target_pairs={{0,12},{4,8},{8,4},{12,0},{1,13},{5,9},{9,5},{13,1},{2,14},{6,10},... | collective-permute-start | bytes 147464 | tf_op jit(solution)/shard_map/ppermute | solution.py:312
  54.5 4.7 %collective-permute-start.9 = (bf16[16,1536]{1,0:T(8,128)(2,1)S(1)}, bf16[16,1536]{1,0:T(8,128)(2,1)S(1)}, u32[]{:S(2)}, u32[]{:S(2)}) collective-permute-start(bf16[16,1536]{1,0:T(8,128)(2,1)S(1)} %get-tuple-element.42), channel_id=1, source_target_pairs={{0,4},{4,0},{8,12},{12,8},{1,5},{5,1},{9,13},{13,9},{2,6},{6,2},{1... | collective-permute-start | bytes 147464 | tf_op jit(solution)/shard_map/ppermute | solution.py:312

commit v2 on v0

v2 whole, which is shorter than its diff:
```python
import functools

import jax
import jax.numpy as jnp
from jax import lax
from jax.experimental import pallas as pl
from jax.experimental.pallas import tpu as pltpu
from jax.sharding import PartitionSpec as P

E_W = 4
SLOT = 10
SLAB = 16
CUTS = (2, 5, 11)
RING = 3
DOWNS = 4
TILE = 512
MIB = 1 << 20
VMEM = pltpu.VMEM
HBM = pltpu.HBM
DMA = pltpu.SemaphoreType.DMA


def spec(space):
    return pl.BlockSpec(memory_space=space)


def limit(mib):
    return pltpu.CompilerParams(vmem_limit_bytes=mib * MIB)


def traffic(size):
    return pl.CostEstimate(flops=0, bytes_accessed=2 * size, transcendentals=0)


def dot(a, b):
    return lax.dot_general(a, b, (((1,), (0,)), ((), ())), preferred_element_type=jnp.float32)


def iota(shape, dim):
    return lax.broadcasted_iota(jnp.int32, shape, dim)


def job_copy(job, half, gate_hbm, up_hbm, target, sem):
    q = lax.axis_index("tensor")
    unit = job // 2
    start = (q ^ (unit // 2)) * 2 * half + (unit % 2) * half
    at = pl.ds(pl.multiple_of(start, 128), half)
    return pltpu.make_async_copy((up_hbm if job % 2 else gate_hbm).at[at, :], target, sem)


def job_copies(jobs, half, gate_hbm, up_hbm, targets, sems):
    return [
        job_copy(job, half, gate_hbm, up_hbm, targets[i], sems.at[i])
        for i, job in enumerate(jobs)
    ]


def half_of(rows, job):
    half = rows.shape[1] // 2
    return rows[:, half:] if job // 2 % 2 else rows[:, :half]


def select_kernel(n, jobs, half, ids_hbm, route_hbm, tok_hbm, gate_hbm, up_hbm, *refs):
    comb_ref, slabs, held = refs[0], refs[1 : n + 1], refs[n + 1 : -5]
    ids_ref, route_ref, tok_ref, sems, held_sems = refs[-5:]
    inputs = [
        pltpu.make_async_copy(source, target, sems.at[i])
        for i, (source, target) in enumerate(
            ((ids_hbm, ids_ref), (route_hbm, route_ref), (tok_hbm, tok_ref))
        )
    ]
    copies = job_copies(jobs, half, gate_hbm, up_hbm, held, held_sems)
    for copy in inputs + copies:
        copy.start()
    for copy in inputs:
        copy.wait()
    me = lax.axis_index("expert")
    replicas = n // E_W
    ids, route, tok = ids_ref[...], route_ref[...], tok_ref[...]
    count = tok.shape[0]
    before = (iota((count, count), 0) <= iota((count, count), 1)).astype(jnp.bfloat16)
    slot = iota((SLAB, count), 0).astype(jnp.float32)
    for k in range(n):
        hit = ids == (me ^ k) // replicas
        member = jnp.sum(jnp.where(hit, 1.0, 0.0), axis=0, keepdims=True)
        weight = jnp.sum(jnp.where(hit, route, 0.0), axis=0, keepdims=True)
        member = jnp.broadcast_to(member, (SLAB, count))
        position = dot(member.astype(jnp.bfloat16), before) - 1.0
        placed = jnp.where(position == slot, member, 0.0)
        slabs[k][...] = dot(placed.astype(jnp.bfloat16), tok).astype(jnp.bfloat16)
        comb_ref[k * SLAB : (k + 1) * SLAB, :] = placed * weight
    for copy in copies:
        copy.wait()


def select(n, jobs, ids, route, tokens, w_gate, w_up):
    count, width = tokens.shape
    held = VMEM((width // 2, w_gate.shape[1]), jnp.bfloat16)
    out = pl.pallas_call(
        functools.partial(select_kernel, n, jobs, width // 2),
        out_shape=[VMEM((n * SLAB, count), jnp.float32)]
        + [VMEM((SLAB, width), jnp.bfloat16)] * n
        + [held] * len(jobs),
        in_specs=[spec(HBM)] * 5,
        out_specs=[spec(VMEM)] * (n + 1 + len(jobs)),
        scratch_shapes=[
            VMEM(ids.shape, ids.dtype),
            VMEM(route.shape, route.dtype),
            VMEM(tokens.shape, tokens.dtype),
            DMA((3,)),
            DMA((len(jobs),)),
        ],
        compiler_params=limit(4),
        name="select",
    )(ids, route, tokens, w_gate, w_up)
    return out[0], out[1 : n + 1], out[n + 1 :]


def compact_kernel(n, *refs):
    slabs, rows_ref = refs[:n], refs[-1]
    full = jnp.concatenate([ref[...] for ref in slabs], axis=0)
    col = iota((n * SLOT, n * SLAB), 1)
    s = col % SLAB
    take = (iota((n * SLOT, n * SLAB), 0) == (col // SLAB) * SLOT + s) & (s < SLOT)
    rows_ref[...] = dot(take.astype(jnp.bfloat16), full).astype(jnp.bfloat16)


def compact(slabs, after):
    n, width = len(slabs), slabs[0].shape[1]
    return pl.pallas_call(
        functools.partial(compact_kernel, n),
        out_shape=VMEM((n * SLOT, width), jnp.bfloat16),
        in_specs=[spec(VMEM)] * (n + 1),
        out_specs=spec(VMEM),
        compiler_params=limit(4),
        name="compact",
    )(*slabs, after)


def fetch_kernel(jobs, half, order_ref, gate_hbm, up_hbm, *refs):
    held, sems = refs[:-1], refs[-1]
    copies = job_copies(jobs, half, gate_hbm, up_hbm, held, sems)
    for copy in copies:
        copy.start()
    for copy in copies:
        copy.wait()


def fetch(jobs, half, order, w_gate, w_up):
    shape = (half, w_gate.shape[1])
    return pl.pallas_call(
        functools.partial(fetch_kernel, jobs, half),
        out_shape=[VMEM(shape, jnp.bfloat16)] * len(jobs),
        in_specs=[spec(VMEM)] + [spec(HBM)] * 2,
        out_specs=[spec(VMEM)] * len(jobs),
        scratch_shapes=[DMA((len(jobs),))],
        compiler_params=limit(2),
        cost_estimate=traffic(len(jobs) * shape[0] * shape[1]),
        name="fetch",
    )(order, w_gate, w_up)


def own_kernel(jobs, half, rows_ref, *refs):
    weights, gate_hbm, up_hbm, sum_g, sum_u = refs[:4], *refs[4:8]
    held, sems = refs[8:-1], refs[-1]
    copies = job_copies(jobs, half, gate_hbm, up_hbm, held, sems)
    for copy in copies:
        copy.start()
    n = gate_hbm.shape[1]
    tile = min(TILE, n)
    low, high = rows_ref[:, :half], rows_ref[:, half:]
    steps = [(out, job, at) for job, out in ((0, sum_g), (1, sum_u)) for at in range(0, n, tile)]
    done = 0
    for i, (out, job, at) in enumerate(steps):
        at = slice(at, at + tile)
        out[:, at] = dot(low, weights[job][:, at]) + dot(high, weights[job + 2][:, at])
        while done < len(copies) and done * len(steps) < (i + 1) * len(copies):
            copies[done].wait()
            done += 1
    for copy in copies[done:]:
        copy.wait()


def own(jobs, half, rows, held, w_gate, w_up):
    m, n = rows.shape[0], w_gate.shape[1]
    shape = (half, n)
    return pl.pallas_call(
        functools.partial(own_kernel, jobs, half),
        out_shape=[VMEM((m, n), jnp.float32)] * 2 + [VMEM(shape, jnp.bfloat16)] * len(jobs),
        in_specs=[spec(VMEM)] * 5 + [spec(HBM)] * 2,
        out_specs=[spec(VMEM)] * (2 + len(jobs)),
        scratch_shapes=[DMA((len(jobs),))],
        compiler_params=limit(4),
        cost_estimate=traffic(len(jobs) * shape[0] * shape[1]),
        name="own",
    )(rows, *held, w_gate, w_up)


def down_copy(k, down_hbm, target, sem):
    width = target.shape[1]
    q = lax.axis_index("tensor")
    at = pl.ds(pl.multiple_of((q ^ k) * width, 128), width)
    return pltpu.make_async_copy(down_hbm.at[:, at], target, sem)


def rest_kernel(parts, first, half, outs, *refs):
    rows, refs = refs[: parts - 1], refs[parts - 1 :]
    held, refs = refs[: first - 4], refs[first - 4 :]
    sum_g, sum_u, gate_hbm, up_hbm, down_hbm = refs[:5]
    hidden_ref, sent = refs[5], refs[6 : 6 + len(outs)]
    ring, down2, acc_g, acc_u, sems, down_sems = refs[6 + len(outs) :]
    count = 4 * parts
    slots, deep = down2.shape[:2]
    cuts = hidden_ref.shape[1] // deep

    weights = []
    for i, job in enumerate(range(first, count)):
        slot = i % ring.shape[0]
        weights.append(job_copy(job, half, gate_hbm, up_hbm, ring.at[slot], sems.at[slot]))
    downs = []
    for i in range(cuts * len(outs)):
        rows_at, slot = down_hbm.at[pl.ds(i % cuts * deep, deep), :], i % slots
        downs.append(down_copy(outs[i // cuts], rows_at, down2.at[slot], down_sems.at[slot]))
    for copy in weights[: ring.shape[0]] + downs[:1]:
        copy.start()
    ahead = 1

    def more_downs(number):
        nonlocal ahead
        for copy in downs[ahead : min(ahead + number, slots)]:
            copy.start()
            ahead += 1

    def add(job, weight):
        row = half_of(rows[job // 4 - 1], job)
        acc = acc_u if job % 2 else acc_g
        acc[...] += dot(row, weight[...])

    acc_g[...] = sum_g[...]
    acc_u[...] = sum_u[...]
    now = 4
    for i, job in enumerate(range(first, count)):
        until = 4 + (first - 4) * (i + 1) // len(weights)
        for held_job in range(now, until):
            add(held_job, held[held_job - 4])
        now = until
        weights[i].wait()
        add(job, ring.at[i % ring.shape[0]])
        if i + ring.shape[0] < len(weights):
            weights[i + ring.shape[0]].start()
        else:
            more_downs(1)
    more_downs(slots)
    gate = acc_g[...]
    hidden_ref[...] = (gate / (1.0 + jnp.exp(-gate)) * acc_u[...]).astype(jnp.bfloat16)
    for i in range(len(outs)):
        total = None
        for j in range(cuts):
            at = cuts * i + j
            downs[at].wait()
            part = dot(hidden_ref[:, j * deep : (j + 1) * deep], down2[at % slots])
            total = part if total is None else total + part
            if at + slots < len(downs):
                downs[at + slots].start()
        sent[i][...] = total.astype(jnp.bfloat16)


def rest(parts, half, outs, rows, held, sum_g, sum_u, w_gate, w_up, w_down):
    m, n = sum_g.shape
    width = 2 * half
    first = 4 + len(held)
    size = ((4 * parts - first) * half + len(outs) * width) * n
    cuts = 2 if n % 256 == 0 else 1
    return pl.pallas_call(
        functools.partial(rest_kernel, parts, first, half, outs),
        out_shape=[VMEM((m, n), jnp.bfloat16)]
        + [VMEM((m, width), jnp.bfloat16)] * len(outs),
        in_specs=[spec(VMEM)] * (parts + 1 + len(held)) + [spec(HBM)] * 3,
        out_specs=[spec(VMEM)] * (1 + len(outs)),
        scratch_shapes=[
            VMEM((RING, half, n), jnp.bfloat16),
            VMEM((DOWNS, n // cuts, width), jnp.bfloat16),
            VMEM((m, n), jnp.float32),
            VMEM((m, n), jnp.float32),
            DMA((RING,)),
            DMA((DOWNS,)),
        ],
        compiler_params=limit(26),
        cost_estimate=traffic(size),
        name="rest",
    )(*rows, *held, sum_g, sum_u, w_gate, w_up, w_down)


def near_kernel(hidden_ref, down_hbm, sent, next_ref, buf, sems):
    cuts, deep = buf.shape[:2]
    copies = []
    for j in range(cuts):
        rows_at = down_hbm.at[pl.ds(j * deep, deep), :]
        copies.append(down_copy(1, rows_at, buf.at[j], sems.at[j]))
    for j in range(cuts):
        at = pl.ds(j * deep, deep)
        copies.append(down_copy(0, down_hbm.at[at, :], next_ref.at[at, :], sems.at[cuts + j]))
    for copy in copies:
        copy.start()
    total = None
    for j in range(cuts):
        copies[j].wait()
        part = dot(hidden_ref[:, j * deep : (j + 1) * deep], buf[j])
        total = part if total is None else total + part
    sent[...] = total.astype(jnp.bfloat16)
    for copy in copies[cuts:]:
        copy.wait()


def near(width, hidden, w_down):
    m, n = hidden.shape
    cuts = 2 if n % 256 == 0 else 1
    return pl.pallas_call(
        near_kernel,
        out_shape=[VMEM((m, width), jnp.bfloat16), VMEM((n, width), jnp.bfloat16)],
        in_specs=[spec(VMEM), spec(HBM)],
        out_specs=[spec(VMEM)] * 2,
        scratch_shapes=[VMEM((cuts, n // cuts, width), jnp.bfloat16), DMA((2 * cuts,))],
        compiler_params=limit(12),
        cost_estimate=traffic(2 * n * width),
        name="near",
    )(hidden, w_down)


def keep_kernel(hidden_ref, weight_ref, *refs):
    terms, total_ref = refs[:-1], refs[-1]
    total = dot(hidden_ref[...], weight_ref[...])
    for term in terms:
        total = total + term[...].astype(jnp.float32)
    total_ref[...] = total


def keep(hidden, weight, terms):
    m, width = hidden.shape[0], weight.shape[1]
    return pl.pallas_call(
        keep_kernel,
        out_shape=VMEM((m, width), jnp.float32),
        in_specs=[spec(VMEM)] * (2 + len(terms)),
        out_specs=spec(VMEM),
        compiler_params=limit(4),
        cost_estimate=traffic(weight.size // 2),
        name="keep",
    )(hidden, weight, *terms)


def add_kernel(n, total_ref, term_ref, *slabs):
    total = (total_ref[...] + term_ref[...].astype(jnp.float32)).astype(jnp.bfloat16)
    s, row = iota((SLAB, n * SLOT), 0), iota((SLAB, n * SLOT), 1)
    for k in range(n):
        take = (row == s + k * SLOT) & (s < SLOT)
        slabs[k][...] = dot(take.astype(jnp.bfloat16), total).astype(jnp.bfloat16)


def add(n, total, term):
    return pl.pallas_call(
        functools.partial(add_kernel, n),
        out_shape=[VMEM((SLAB, total.shape[1]), jnp.bfloat16)] * n,
        in_specs=[spec(VMEM)] * 2,
        out_specs=[spec(VMEM)] * n,
        compiler_params=limit(4),
        name="add",
    )(total, term)


def combine_kernel(n, comb_ref, *refs):
    slabs, out_ref = refs[:n], refs[n]
    full = jnp.concatenate([ref[...] for ref in slabs], axis=0)
    comb = comb_ref[...].T
    high = comb.astype(jnp.bfloat16)
    comb = comb - high.astype(jnp.float32)
    mid = comb.astype(jnp.bfloat16)
    low = (comb - mid.astype(jnp.float32)).astype(jnp.bfloat16)
    out_ref[...] = (dot(high, full) + (dot(mid, full) + dot(low, full))).astype(jnp.bfloat16)


def combine(comb, slabs):
    n, width = len(slabs), slabs[0].shape[1]
    return pl.pallas_call(
        functools.partial(combine_kernel, n),
        out_shape=jax.ShapeDtypeStruct((comb.shape[1], width), jnp.bfloat16),
        in_specs=[spec(VMEM)] * (n + 1),
        out_specs=spec(VMEM),
        compiler_params=limit(4),
        name="combine",
    )(comb, *slabs)


def swap(x, axis, k):
    size = lax.axis_size(axis)
    return lax.ppermute(x, axis, [(i, i ^ k) for i in range(size)])


def per_device(*args):
    tokens, ids, route, w_gate, w_up, w_down = (
        pltpu.with_memory_space_constraint(x, HBM)
        for x in (args[0], args[1].T, args[2].T, *args[3:])
    )
    n, parts = lax.axis_size("expert"), lax.axis_size("tensor")
    half = tokens.shape[1] // 2
    comb, slabs, held = select(n, range(CUTS[0]), ids, route, tokens, w_gate, w_up)
    slabs = [slabs[0]] + [swap(slabs[k], "expert", k) for k in range(1, n)]
    held += fetch(range(CUTS[0], CUTS[1]), half, comb, w_gate, w_up)
    mine = compact(slabs, held[-1])
    rows = [swap(mine, "tensor", k) for k in range(1, parts)]
    sum_g, sum_u, *more = own(range(CUTS[1], CUTS[2]), half, mine, held[:4], w_gate, w_up)
    held = [*held[4:], *more]
    far = list(range(parts - 1, 1, -1))
    hidden, *sent = rest(
        parts, half, far, rows, held, sum_g, sum_u, w_gate, w_up, w_down
    )
    terms = [swap(x, "tensor", k) for k, x in zip(far, sent)]
    sent, weight0 = near(2 * half, hidden, w_down)
    last = swap(sent, "tensor", 1)
    total = keep(hidden, weight0, terms)
    back = add(n, total, last)
    back = [back[0]] + [swap(back[k], "expert", k) for k in range(1, n)]
    return combine(comb, back)


def solution(mesh):
    return jax.shard_map(
        per_device,
        mesh=mesh,
        in_specs=(
            P(("groups", "expert"), "tensor"),
            P(("groups", "expert"), None),
            P(("groups", "expert"), None),
            P(None, ("expert", "tensor")),
            P(None, ("expert", "tensor")),
            P(("expert", "tensor"), None),
        ),
        out_specs=P(("groups", "expert"), "tensor"),
        check_vma=False,
    )
```

time: 119 us -> 53.2 us (0.45)
  blocking collectives: 36.6 us -> 0 us
  matrix products: 33.8 us -> 0 us
  Pallas kernels: 0 us -> 32.8 us
  waiting for transfers between devices: 27.6 us -> 6.8 us
  between operations: 13.4 us -> 0.14 us
  starting transfers between devices: 4.6 us -> 13.3 us
  local copies, waits for them, and re-layouts: 1.94 us -> 0 us
    dot_general x5 -> x0, matrix products: 33.8 us -> none  [the longest x1 11.3 us: per_device(): lax.dot_general(w_down, hidden, (((0,), (1,)), ((), ())), preferred_eleme...]
    pallas_call x0 -> x9, Pallas kernels: none -> 32.8 us  [the longest x1 11.5 us: rest(): pl.pallas_call(functools.partial(rest_kernel, parts, first, half, outs),...]
    all_to_all x1 -> x0, blocking collectives: 25.3 us -> none  [per_device(): lax.all_to_all(outgoing, 'expert', split_axis=0, concat_axis=0, tiled=True)]
    reduce_scatter x1 -> x0, waiting for transfers between devices: 20.3 us -> none  [per_device(): lax.psum_scatter(lax.dot_general(w_down, hidden, (((0,), (1,)), ((), ()))...]
    ppermute x0 -> x12, starting transfers between devices: none -> 13.3 us  [swap(): return lax.ppermute(x, axis, [(i, i ^ k) for i in range(size)])]
    all_gather x1 -> x0, blocking collectives: 11.3 us -> none  [per_device(): full_rows = lax.all_gather(tokens, 'tensor', axis=1, tiled=True)]
    all_to_all x1 -> x0, waiting for transfers between devices: 7.36 us -> none  [per_device(): lax.all_to_all(summed, 'expert', split_axis=1, concat_axis=1, tiled=True)]
    ppermute x0 -> x12, waiting for transfers between devices: none -> 6.8 us  [swap(): return lax.ppermute(x, axis, [(i, i ^ k) for i in range(size)])]
  transfers between devices with their start and end apart: 2 -> 12, of which waited for: 2 -> 5; matrix products, arithmetic and copies ran while one was open for 0% -> 0% of each run, Pallas kernels for 0% -> 32%
where the time goes in v2:
time: 53.2 us; the launch traced here: 53 us
  Pallas kernels  32.8 us (62%)
  starting transfers between devices  13.3 us (25%)
  waiting for transfers between devices  6.8 us (13%)
    ppermute x12, starting transfers between devices, swap(): return lax.ppermute(x, axis, [(i, i ^ k) for i in range(size)])  13.3 us
    pallas_call x1, Pallas kernels, rest(): pl.pallas_call(functools.partial(rest_kernel, parts, first, half, outs),...  11.5 us
    pallas_call x1, Pallas kernels, own(): pl.pallas_call(functools.partial(own_kernel, jobs, half), out_shape=[VMEM...  7.13 us
    ppermute x12, waiting for transfers between devices, swap(): return lax.ppermute(x, axis, [(i, i ^ k) for i in range(size)])  6.8 us
    pallas_call x1, Pallas kernels, near(): pl.pallas_call(near_kernel, out_shape=[VMEM((m, width), jnp.bfloat16), VM...  4.71 us
    pallas_call x1, Pallas kernels, fetch(): pl.pallas_call(functools.partial(fetch_kernel, jobs, half), out_shape=[VM...  3.78 us
    pallas_call x1, Pallas kernels, select(): pl.pallas_call(functools.partial(select_kernel, n, jobs, width // 2), out...  3.06 us
    pallas_call x1, Pallas kernels, keep(): pl.pallas_call(keep_kernel, out_shape=VMEM((m, width), jnp.float32), in_s...  1.18 us
  transfers between devices with their start and end apart: 12, of which 5 were waited for; matrix products, arithmetic and copies ran while one was open for 0% of the time, Pallas kernels for 32%

profile of v2, /device:TPU:0, one launch (start us, length us, event | category | flops | bytes accessed | tf_op | source)
XLA Modules:
  0.0 53.0 jit_solution(10975955825845798030)
XLA Ops:
  0.0 3.1 %select.1 = (f32[64,80]{1,0:T(8,128)S(1)}, bf16[16,1536]{1,0:T(8,128)(2,1)S(1)}, bf16[16,1536]{1,0:T(8,128)(2,1)S(1)}, bf16[16,1536]{1,0:T(8,128)(2,1)S(1)}, bf1...) custom-call(s32[4,80]{1,0:T(4,128)} %bitcast.2, f32[4,80]{1,0:T(4,128)} %bitcast.3, ...), custom_call_target="tpu_custom_call" | custom-call | tf_op jit(solution)/shard_map/select/pallas_call | solution.py:99
  3.1 3.1 %collective-permute-start = (bf16[16,1536]{1,0:T(8,128)(2,1)S(1)}, bf16[16,1536]{1,0:T(8,128)(2,1)S(1)}, u32[]{:S(2)}, u32[]{:S(2)}) collective-permute-start(bf16[16,1536]{1,0:T(8,128)(2,1)S(1)} %get-tuple-element.34), channel_id=1, source_target_pairs={{0,4},{4,0},{8,12},{12,8},{1,5},{5,1},{9,13},{13,9},{2,6},{6,2},{1... | collective-permute-start | bytes 147464 | tf_op jit(solution)/shard_map/ppermute | solution.py:395
  6.2 2.6 %collective-permute-start.1 = (bf16[16,1536]{1,0:T(8,128)(2,1)S(1)}, bf16[16,1536]{1,0:T(8,128)(2,1)S(1)}, u32[]{:S(2)}, u32[]{:S(2)}) collective-permute-start(bf16[16,1536]{1,0:T(8,128)(2,1)S(1)} %get-tuple-element.35), channel_id=1, source_target_pairs={{0,8},{4,12},{8,0},{12,4},{1,9},{5,13},{9,1},{13,5},{2,10},{6,14},... | collective-permute-start | bytes 147464 | tf_op jit(solution)/shard_map/ppermute | solution.py:395
  8.7 3.8 %fetch.1 = (bf16[768,2048]{1,0:T(8,128)(2,1)S(1)}, bf16[768,2048]{1,0:T(8,128)(2,1)S(1)}, bf16[768,2048]{1,0:T(8,128)(2,1)S(1)}) custom-call(f32[64,80]{1,0:T(8,128)S(1)} %get-tuple-element.32.order_ref.comb_ref, bf16[6144,2048]{1,0:T(8,128)(2,1)} %refs_12_.1, bf16[6144,2048]{1,0:T(8,128)(2,1)} %refs_13_.1), custom_call_target="tpu_custom_call" | custom-call | bytes 9437184 | tf_op jit(solution)/shard_map/fetch/pallas_call | solution.py:151
  12.6 2.1 %collective-permute-done.2.refs_3_ = bf16[16,1536]{1,0:T(8,128)(2,1)S(1)} collective-permute-done((bf16[16,1536]{1,0:T(8,128)(2,1)S(1)}, bf16[16,1536]{1,0:T(8,128)(2,1)S(1)}, u32[]{:S(2)}, u32[]{:S(2)}) %collective-permute-start.2) | collective-permute-done | bytes 49184 | tf_op jit(solution)/shard_map/ppermute | solution.py:395
  14.6 0.2 compact.1.rows_ref
  14.8 0.1 collective-permute-start.3
  14.9 1.6 %collective-permute-start.4 = (bf16[40,1536]{1,0:T(8,128)(2,1)S(1)}, bf16[40,1536]{1,0:T(8,128)(2,1)S(1)}, u32[]{:S(2)}, u32[]{:S(2)}) collective-permute-start(bf16[40,1536]{1,0:T(8,128)(2,1)S(1)} %compact.1.rows_ref), channel_id=1, source_target_pairs={{0,2},{1,3},{2,0},{3,1},{4,6},{5,7},{6,4},{7,5},{8,10},{9,11},{10,... | collective-permute-start | bytes 368648 | tf_op jit(solution)/shard_map/ppermute | solution.py:395
  16.4 0.3 collective-permute-start.5
  16.7 7.1 %own.1 = (f32[40,2048]{1,0:T(8,128)S(1)}, f32[40,2048]{1,0:T(8,128)S(1)}, bf16[768,2048]{1,0:T(8,128)(2,1)S(1)}, bf16[768,2048]{1,0:T(8,128)(2,1)S(1)}, bf16[768...) custom-call(bf16[40,1536]{1,0:T(8,128)(2,1)S(1)} %compact.1.rows_ref, ...), custom_call_target="tpu_custom_call" | custom-call | bytes 18874368 | tf_op jit(solution)/shard_map/own/pallas_call | solution.py:187
  23.9 11.5 %rest.1 = (bf16[40,2048]{1,0:T(8,128)(2,1)S(1)}, bf16[40,1536]{1,0:T(8,128)(2,1)S(1)}, bf16[40,1536]{1,0:T(8,128)(2,1)S(1)}) custom-call(bf16[40,1536]{1,0:T(8,128)(2,1)S(1)} %collective-permute-done.3.refs_0_, bf16[40,1536]{1,0:T(8,128)(2,1)S(1)} %collective-permute-done.4.refs_1_, bf16[40,1536]{1,0:T(8,128)(2,1)S(1)} %collective-permute-done.5.refs_2_, ...), custom_call_target="tpu_custom_call" | custom-call | bytes 28311552 | tf_op jit(solution)/shard_map/rest/pallas_call | solution.py:274
  35.4 1.5 %collective-permute-start.6 = (bf16[40,1536]{1,0:T(8,128)(2,1)S(1)}, bf16[40,1536]{1,0:T(8,128)(2,1)S(1)}, u32[]{:S(2)}, u32[]{:S(2)}) collective-permute-start(bf16[40,1536]{1,0:T(8,128)(2,1)S(1)} %get-tuple-element.52), channel_id=1, source_target_pairs={{0,3},{1,2},{2,1},{3,0},{4,7},{5,6},{6,5},{7,4},{8,11},{9,10},{10,... | collective-permute-start | bytes 368648 | tf_op jit(solution)/shard_map/ppermute | solution.py:395
  36.9 0.5 %collective-permute-start.7 = (bf16[40,1536]{1,0:T(8,128)(2,1)S(1)}, bf16[40,1536]{1,0:T(8,128)(2,1)S(1)}, u32[]{:S(2)}, u32[]{:S(2)}) collective-permute-start(bf16[40,1536]{1,0:T(8,128)(2,1)S(1)} %get-tuple-element.53), channel_id=1, source_target_pairs={{0,2},{1,3},{2,0},{3,1},{4,6},{5,7},{6,4},{7,5},{8,10},{9,11},{10,... | collective-permute-start | bytes 368648 | tf_op jit(solution)/shard_map/ppermute | solution.py:395
  37.4 4.7 %near.1 = (bf16[40,1536]{1,0:T(8,128)(2,1)S(1)}, bf16[2048,1536]{1,0:T(8,128)(2,1)S(1)}) custom-call(bf16[40,2048]{1,0:T(8,128)(2,1)S(1)} %get-tuple-element.50.hidden_ref, bf16[2048,6144]{1,0:T(8,128)(2,1)} %down_hbm.1), custom_call_target="tpu_custom_call" | custom-call | bytes 12582912 | tf_op jit(solution)/shard_map/near/pallas_call | solution.py:318
  42.2 1.5 %collective-permute-done.7.refs_1_ = bf16[40,1536]{1,0:T(8,128)(2,1)S(1)} collective-permute-done((bf16[40,1536]{1,0:T(8,128)(2,1)S(1)}, bf16[40,1536]{1,0:T(8,128)(2,1)S(1)}, u32[]{:S(2)}, u32[]{:S(2)}) %collective-permute-start.7) | collective-permute-done | bytes 122912 | tf_op jit(solution)/shard_map/ppermute | solution.py:395
  43.7 1.2 %keep.1.total_ref = f32[40,1536]{1,0:T(8,128)S(1)} custom-call(bf16[40,2048]{1,0:T(8,128)(2,1)S(1)} %get-tuple-element.50.hidden_ref, bf16[2048,1536]{1,0:T(8,128)(2,1)S(1)} %get-tuple-element.51.weight_ref, bf16[40,1536]{1,0:T(8,128)(2,1)S(1)} %collective-permute-done.6.refs_0_, bf16[40,1536]{1,0:T(8,128)(2,1)S(1)} %collective-permute-done.7.refs_1_), custom_call_target="tpu_custom_call" | custom-call | bytes 3145728 | tf_op jit(solution)/shard_map/keep/pallas_call | solution.py:340
  44.9 0.2 add.1
  45.1 0.4 collective-permute-start.10
  45.6 1.5 %collective-permute-start.11 = (bf16[16,1536]{1,0:T(8,128)(2,1)S(1)}, bf16[16,1536]{1,0:T(8,128)(2,1)S(1)}, u32[]{:S(2)}, u32[]{:S(2)}) collective-permute-start(bf16[16,1536]{1,0:T(8,128)(2,1)S(1)} %get-tuple-element.58), channel_id=1, source_target_pairs={{0,12},{4,8},{8,4},{12,0},{1,13},{5,9},{9,5},{13,1},{2,14},{6,10},... | collective-permute-start | bytes 147464 | tf_op jit(solution)/shard_map/ppermute | solution.py:395
  47.0 1.6 %collective-permute-start.9 = (bf16[16,1536]{1,0:T(8,128)(2,1)S(1)}, bf16[16,1536]{1,0:T(8,128)(2,1)S(1)}, u32[]{:S(2)}, u32[]{:S(2)}) collective-permute-start(bf16[16,1536]{1,0:T(8,128)(2,1)S(1)} %get-tuple-element.56), channel_id=1, source_target_pairs={{0,4},{4,0},{8,12},{12,8},{1,5},{5,1},{9,13},{13,9},{2,6},{6,2},{1... | collective-permute-start | bytes 147464 | tf_op jit(solution)/shard_map/ppermute | solution.py:395
  48.7 2.3 %collective-permute-done.10.refs_2_ = bf16[16,1536]{1,0:T(8,128)(2,1)S(1)} collective-permute-done((bf16[16,1536]{1,0:T(8,128)(2,1)S(1)}, bf16[16,1536]{1,0:T(8,128)(2,1)S(1)}, u32[]{:S(2)}, u32[]{:S(2)}) %collective-permute-start.10) | collective-permute-done | bytes 49184 | tf_op jit(solution)/shard_map/ppermute | solution.py:395
  51.0 0.6 %collective-permute-done.11.refs_3_ = bf16[16,1536]{1,0:T(8,128)(2,1)S(1)} collective-permute-done((bf16[16,1536]{1,0:T(8,128)(2,1)S(1)}, bf16[16,1536]{1,0:T(8,128)(2,1)S(1)}, u32[]{:S(2)}, u32[]{:S(2)}) %collective-permute-start.11) | collective-permute-done | bytes 49184 | tf_op jit(solution)/shard_map/ppermute | solution.py:395
  51.6 0.3 collective-permute-done.9.refs_1_
  51.9 1.1 %combine.1 = bf16[80,1536]{1,0:T(8,128)(2,1)} custom-call(f32[64,80]{1,0:T(8,128)S(1)} %get-tuple-element.32.order_ref.comb_ref, bf16[16,1536]{1,0:T(8,128)(2,1)S(1)} %get-tuple-element.55.refs_0_, bf16[16,1536]{1,0:T(8,128)(2,1)S(1)} %collective-permute-done.9.refs_1_, bf16[16,1536]{1,0:T(8,128)(2,1)S(1)} %collective-permute-done.10.refs_2_, ...), custom_call_target="tpu_custom_call" | custom-call | tf_op jit(solution)/shard_map/combine/pallas_call | solution.py:383
  (9 shorter events, 0.1 us)
Async XLA Ops:
  3.1 9.5 %collective-permute-start = (bf16[16,1536]{1,0:T(8,128)(2,1)S(1)}, bf16[16,1536]{1,0:T(8,128)(2,1)S(1)}, u32[]{:S(2)}, u32[]{:S(2)}) collective-permute-start(bf16[16,1536]{1,0:T(8,128)(2,1)S(1)} %get-tuple-element.34), channel_id=1, source_target_pairs={{0,4},{4,0},{8,12},{12,8},{1,5},{5,1},{9,13},{13,9},{2,6},{6,2},{1... | collective-permute-start | bytes 147464 | tf_op jit(solution)/shard_map/ppermute | solution.py:395
  6.2 6.4 %collective-permute-start.1 = (bf16[16,1536]{1,0:T(8,128)(2,1)S(1)}, bf16[16,1536]{1,0:T(8,128)(2,1)S(1)}, u32[]{:S(2)}, u32[]{:S(2)}) collective-permute-start(bf16[16,1536]{1,0:T(8,128)(2,1)S(1)} %get-tuple-element.35), channel_id=1, source_target_pairs={{0,8},{4,12},{8,0},{12,4},{1,9},{5,13},{9,1},{13,5},{2,10},{6,14},... | collective-permute-start | bytes 147464 | tf_op jit(solution)/shard_map/ppermute | solution.py:395
  8.7 5.9 %collective-permute-start.2 = (bf16[16,1536]{1,0:T(8,128)(2,1)S(1)}, bf16[16,1536]{1,0:T(8,128)(2,1)S(1)}, u32[]{:S(2)}, u32[]{:S(2)}) collective-permute-start(bf16[16,1536]{1,0:T(8,128)(2,1)S(1)} %get-tuple-element.36), channel_id=1, source_target_pairs={{0,12},{4,8},{8,4},{12,0},{1,13},{5,9},{9,5},{13,1},{2,14},{6,10},... | collective-permute-start | bytes 147464 | tf_op jit(solution)/shard_map/ppermute | solution.py:395
  14.8 9.1 %collective-permute-start.3 = (bf16[40,1536]{1,0:T(8,128)(2,1)S(1)}, bf16[40,1536]{1,0:T(8,128)(2,1)S(1)}, u32[]{:S(2)}, u32[]{:S(2)}) collective-permute-start(bf16[40,1536]{1,0:T(8,128)(2,1)S(1)} %compact.1.rows_ref), channel_id=1, source_target_pairs={{0,1},{1,0},{2,3},{3,2},{4,5},{5,4},{6,7},{7,6},{8,9},{9,8},{10,11... | collective-permute-start | bytes 368648 | tf_op jit(solution)/shard_map/ppermute | solution.py:395
  14.9 9.0 %collective-permute-start.4 = (bf16[40,1536]{1,0:T(8,128)(2,1)S(1)}, bf16[40,1536]{1,0:T(8,128)(2,1)S(1)}, u32[]{:S(2)}, u32[]{:S(2)}) collective-permute-start(bf16[40,1536]{1,0:T(8,128)(2,1)S(1)} %compact.1.rows_ref), channel_id=1, source_target_pairs={{0,2},{1,3},{2,0},{3,1},{4,6},{5,7},{6,4},{7,5},{8,10},{9,11},{10,... | collective-permute-start | bytes 368648 | tf_op jit(solution)/shard_map/ppermute | solution.py:395
  16.4 7.5 %collective-permute-start.5 = (bf16[40,1536]{1,0:T(8,128)(2,1)S(1)}, bf16[40,1536]{1,0:T(8,128)(2,1)S(1)}, u32[]{:S(2)}, u32[]{:S(2)}) collective-permute-start(bf16[40,1536]{1,0:T(8,128)(2,1)S(1)} %compact.1.rows_ref), channel_id=1, source_target_pairs={{0,3},{1,2},{2,1},{3,0},{4,7},{5,6},{6,5},{7,4},{8,11},{9,10},{10,... | collective-permute-start | bytes 368648 | tf_op jit(solution)/shard_map/ppermute | solution.py:395
  35.4 6.8 %collective-permute-start.6 = (bf16[40,1536]{1,0:T(8,128)(2,1)S(1)}, bf16[40,1536]{1,0:T(8,128)(2,1)S(1)}, u32[]{:S(2)}, u32[]{:S(2)}) collective-permute-start(bf16[40,1536]{1,0:T(8,128)(2,1)S(1)} %get-tuple-element.52), channel_id=1, source_target_pairs={{0,3},{1,2},{2,1},{3,0},{4,7},{5,6},{6,5},{7,4},{8,11},{9,10},{10,... | collective-permute-start | bytes 368648 | tf_op jit(solution)/shard_map/ppermute | solution.py:395
  36.9 6.8 %collective-permute-start.7 = (bf16[40,1536]{1,0:T(8,128)(2,1)S(1)}, bf16[40,1536]{1,0:T(8,128)(2,1)S(1)}, u32[]{:S(2)}, u32[]{:S(2)}) collective-permute-start(bf16[40,1536]{1,0:T(8,128)(2,1)S(1)} %get-tuple-element.53), channel_id=1, source_target_pairs={{0,2},{1,3},{2,0},{3,1},{4,6},{5,7},{6,4},{7,5},{8,10},{9,11},{10,... | collective-permute-start | bytes 368648 | tf_op jit(solution)/shard_map/ppermute | solution.py:395
  42.2 2.8 %collective-permute-start.8 = (bf16[40,1536]{1,0:T(8,128)(2,1)S(1)}, bf16[40,1536]{1,0:T(8,128)(2,1)S(1)}, u32[]{:S(2)}, u32[]{:S(2)}) collective-permute-start(bf16[40,1536]{1,0:T(8,128)(2,1)S(1)} %get-tuple-element.54), channel_id=1, source_target_pairs={{0,1},{1,0},{2,3},{3,2},{4,5},{5,4},{6,7},{7,6},{8,9},{9,8},{10,11... | collective-permute-start | bytes 368648 | tf_op jit(solution)/shard_map/ppermute | solution.py:395
  45.1 5.8 %collective-permute-start.10 = (bf16[16,1536]{1,0:T(8,128)(2,1)S(1)}, bf16[16,1536]{1,0:T(8,128)(2,1)S(1)}, u32[]{:S(2)}, u32[]{:S(2)}) collective-permute-start(bf16[16,1536]{1,0:T(8,128)(2,1)S(1)} %get-tuple-element.57), channel_id=1, source_target_pairs={{0,8},{4,12},{8,0},{12,4},{1,9},{5,13},{9,1},{13,5},{2,10},{6,14},... | collective-permute-start | bytes 147464 | tf_op jit(solution)/shard_map/ppermute | solution.py:395
  45.6 6.0 %collective-permute-start.11 = (bf16[16,1536]{1,0:T(8,128)(2,1)S(1)}, bf16[16,1536]{1,0:T(8,128)(2,1)S(1)}, u32[]{:S(2)}, u32[]{:S(2)}) collective-permute-start(bf16[16,1536]{1,0:T(8,128)(2,1)S(1)} %get-tuple-element.58), channel_id=1, source_target_pairs={{0,12},{4,8},{8,4},{12,0},{1,13},{5,9},{9,5},{13,1},{2,14},{6,10},... | collective-permute-start | bytes 147464 | tf_op jit(solution)/shard_map/ppermute | solution.py:395
  47.0 4.9 %collective-permute-start.9 = (bf16[16,1536]{1,0:T(8,128)(2,1)S(1)}, bf16[16,1536]{1,0:T(8,128)(2,1)S(1)}, u32[]{:S(2)}, u32[]{:S(2)}) collective-permute-start(bf16[16,1536]{1,0:T(8,128)(2,1)S(1)} %get-tuple-element.56), channel_id=1, source_target_pairs={{0,4},{4,0},{8,12},{12,8},{1,5},{5,1},{9,13},{13,9},{2,6},{6,2},{1... | collective-permute-start | bytes 147464 | tf_op jit(solution)/shard_map/ppermute | solution.py:395

commit v3 on v2

v3 whole, which is shorter than its diff:
```python
import functools

import jax
import jax.numpy as jnp
from jax import lax
from jax.experimental import pallas as pl
from jax.experimental.pallas import tpu as pltpu
from jax.sharding import PartitionSpec as P

E_W = 4
SLOT = 10
SLAB = 16
FETCH = 2
OWN = 5
DOWNS = 3
TILE = 512
WIDE = 512
MICRO = 1_150_000_000
MIB = 1 << 20
VMEM = pltpu.VMEM
HBM = pltpu.HBM
DMA = pltpu.SemaphoreType.DMA


def spec(space):
    return pl.BlockSpec(memory_space=space)


def limit(mib):
    return pltpu.CompilerParams(vmem_limit_bytes=mib * MIB)


def lasts(micros):
    return pl.CostEstimate(flops=int(micros * MICRO), bytes_accessed=0, transcendentals=0)


def dot(a, b):
    return lax.dot_general(a, b, (((1,), (0,)), ((), ())), preferred_element_type=jnp.float32)


def iota(shape, dim):
    return lax.broadcasted_iota(jnp.int32, shape, dim)


def job_copies(jobs, half, up_hbm, targets, sems):
    q = lax.axis_index("tensor")
    copies = []
    for i, job in enumerate(jobs):
        start = (q ^ (job // 2)) * 2 * half + (job % 2) * half
        at = pl.ds(pl.multiple_of(start, 128), half)
        copies.append(pltpu.make_async_copy(up_hbm.at[at, :], targets[i], sems.at[i]))
    return copies


def select_kernel(n, ids_hbm, route_hbm, tok_hbm, comb_ref, *refs):
    slabs, (ids_ref, route_ref, tok_ref, sems) = refs[:n], refs[n:]
    inputs = [
        pltpu.make_async_copy(source, target, sems.at[i])
        for i, (source, target) in enumerate(
            ((ids_hbm, ids_ref), (route_hbm, route_ref), (tok_hbm, tok_ref))
        )
    ]
    for copy in inputs:
        copy.start()
    for copy in inputs:
        copy.wait()
    me = lax.axis_index("expert")
    replicas = n // E_W
    ids, route, tok = ids_ref[...], route_ref[...], tok_ref[...]
    count = tok.shape[0]
    before = (iota((count, count), 0) <= iota((count, count), 1)).astype(jnp.bfloat16)
    slot = iota((SLAB, count), 0).astype(jnp.float32)
    for k in range(n):
        hit = ids == (me ^ k) // replicas
        member = jnp.sum(jnp.where(hit, 1.0, 0.0), axis=0, keepdims=True)
        weight = jnp.sum(jnp.where(hit, route, 0.0), axis=0, keepdims=True)
        member = jnp.broadcast_to(member, (SLAB, count))
        position = dot(member.astype(jnp.bfloat16), before) - 1.0
        placed = jnp.where(position == slot, member, 0.0)
        slabs[k][...] = dot(placed.astype(jnp.bfloat16), tok).astype(jnp.bfloat16)
        comb_ref[k * SLAB : (k + 1) * SLAB, :] = placed * weight


def select(n, ids, route, tokens):
    count, width = tokens.shape
    out = pl.pallas_call(
        functools.partial(select_kernel, n),
        out_shape=[VMEM((n * SLAB, count), jnp.float32)]
        + [VMEM((SLAB, width), jnp.bfloat16)] * n,
        in_specs=[spec(HBM)] * 3,
        out_specs=[spec(VMEM)] * (n + 1),
        scratch_shapes=[
            VMEM(ids.shape, ids.dtype),
            VMEM(route.shape, route.dtype),
            VMEM(tokens.shape, tokens.dtype),
            DMA((3,)),
        ],
        compiler_params=limit(4),
        cost_estimate=lasts(40),
        name="select",
    )(ids, route, tokens)
    return out[0], out[1:]


def compact_kernel(n, *refs):
    slabs, rows_ref = refs[:n], refs[-1]
    full = jnp.concatenate([ref[...] for ref in slabs], axis=0)
    col = iota((n * SLOT, n * SLAB), 1)
    s = col % SLAB
    take = (iota((n * SLOT, n * SLAB), 0) == (col // SLAB) * SLOT + s) & (s < SLOT)
    rows_ref[...] = dot(take.astype(jnp.bfloat16), full).astype(jnp.bfloat16)


def compact(slabs, after):
    n, width = len(slabs), slabs[0].shape[1]
    return pl.pallas_call(
        functools.partial(compact_kernel, n),
        out_shape=VMEM((n * SLOT, width), jnp.bfloat16),
        in_specs=[spec(VMEM)] * (n + 1),
        out_specs=spec(VMEM),
        compiler_params=limit(4),
        name="compact",
    )(*slabs, after)


def chunk(weight_ref, k, width, side, half, tile):
    start = (lax.axis_index("tensor") ^ k) * width + side
    return weight_ref[pl.ds(pl.multiple_of(start, 128), half), tile]


def tiles(n):
    return [slice(at, at + min(TILE, n)) for at in range(0, n, min(TILE, n))]


def fetch_kernel(jobs, half, order_ref, up_hbm, *refs):
    held, sems = refs[:-1], refs[-1]
    copies = job_copies(jobs, half, up_hbm, held, sems)
    for copy in copies:
        copy.start()
    for copy in copies:
        copy.wait()


def fetch(jobs, half, order, w_up):
    shape = (half, w_up.shape[1])
    return pl.pallas_call(
        functools.partial(fetch_kernel, jobs, half),
        out_shape=[VMEM(shape, jnp.bfloat16)] * len(jobs),
        in_specs=[spec(VMEM), spec(HBM)],
        out_specs=[spec(VMEM)] * len(jobs),
        scratch_shapes=[DMA((len(jobs),))],
        compiler_params=limit(2),
        cost_estimate=lasts(0.2),
        name="fetch",
    )(order, w_up)


def own_kernel(jobs, rows_ref, up_low, up_high, up_hbm, sum_u, *refs):
    held, sems = refs[:-1], refs[-1]
    half = rows_ref.shape[1] // 2
    copies = job_copies(jobs, half, up_hbm, held, sems)
    for copy in copies:
        copy.start()
    low, high = rows_ref[:, :half], rows_ref[:, half:]
    steps = tiles(sum_u.shape[1])
    done = 0
    for i, tile in enumerate(steps):
        sum_u[:, tile] = dot(low, up_low[:, tile]) + dot(high, up_high[:, tile])
        while done < len(copies) and done * len(steps) < (i + 1) * len(copies):
            copies[done].wait()
            done += 1
    for copy in copies[done:]:
        copy.wait()


def own(jobs, rows, held, w_up):
    (m, width), n = rows.shape, w_up.shape[1]
    return pl.pallas_call(
        functools.partial(own_kernel, jobs),
        out_shape=[VMEM((m, n), jnp.float32)]
        + [VMEM((width // 2, n), jnp.bfloat16)] * len(jobs),
        in_specs=[spec(VMEM)] * 3 + [spec(HBM)],
        out_specs=[spec(VMEM)] * (1 + len(jobs)),
        scratch_shapes=[DMA((len(jobs),))],
        compiler_params=limit(2),
        cost_estimate=lasts(0.2),
        name="own",
    )(rows, *held, w_up)


def down_copy(k, down_hbm, target, sem):
    width = target.shape[1]
    q = lax.axis_index("tensor")
    at = pl.ds(pl.multiple_of((q ^ k) * width, 128), width)
    return pltpu.make_async_copy(down_hbm.at[:, at], target, sem)


def rest_kernel(outs, first, *refs):
    parts = len(outs) + 2
    rows, refs = refs[:parts], refs[parts:]
    held, refs = refs[: first - 2], refs[first - 2 :]
    start_u, gate_ref, up_hbm, down_hbm, hidden_ref = refs[:5]
    sent, refs = refs[5 : 5 + len(outs)], refs[5 + len(outs) :]
    late, down2, sum_g, late_sems, down_sems = refs
    width = rows[0].shape[1]
    half = width // 2
    slots, deep = down2.shape[:2]
    n = hidden_ref.shape[1]
    wide = min(WIDE, n)
    deep_gate = 256 if width % 256 == 0 else 128
    cuts = n // deep
    jobs = range(first, 2 * parts)
    lates = job_copies(jobs, half, up_hbm, [late.at[i] for i in range(len(jobs))], late_sems)
    downs = []
    for i in range(cuts * len(outs)):
        rows_at, slot = down_hbm.at[pl.ds(i % cuts * deep, deep), :], i % slots
        downs.append(down_copy(outs[i // cuts], rows_at, down2.at[slot], down_sems.at[slot]))
    for copy in lates:
        copy.start()
    ups = list(held) + [late.at[i] for i in range(len(jobs))]

    def gate_part(step):
        at = pl.ds(pl.multiple_of(step * wide, 128), wide)
        total = None
        for k in range(parts):
            for side in range(0, width, deep_gate):
                row = rows[k][:, side : side + deep_gate]
                part = dot(row, chunk(gate_ref, k, width, side, deep_gate, at))
                total = part if total is None else total + part
        sum_g[:, at] = total

    middle = n // wide // 2
    pl.loop(0, middle)(gate_part)
    for copy in downs[:slots]:
        copy.start()
    pl.loop(middle, n // wide)(gate_part)
    for copy in lates:
        copy.wait()

    @pl.loop(0, n // wide)
    def _(step):
        at = pl.ds(pl.multiple_of(step * wide, 128), wide)
        total = start_u[:, at]
        for k in range(1, parts):
            total += dot(rows[k][:, :half], ups[2 * k - 2][:, at])
            total += dot(rows[k][:, half:], ups[2 * k - 1][:, at])
        gate = sum_g[:, at]
        hidden_ref[:, at] = (gate / (1.0 + jnp.exp(-gate)) * total).astype(jnp.bfloat16)

    for i in range(len(outs)):
        for j in range(cuts):
            piece = cuts * i + j
            downs[piece].wait()

            @pl.loop(0, 2)
            def _(step):
                at = pl.ds(pl.multiple_of(step * half, 128), half)
                mid = hidden_ref[:, j * deep : (j + 1) * deep]
                part = dot(mid, down2[piece % slots, :, at])
                if j > 0:
                    part += sum_g[:, at]
                if j < cuts - 1:
                    sum_g[:, at] = part
                else:
                    sent[i][:, at] = part.astype(jnp.bfloat16)

            if piece + slots < len(downs):
                downs[piece + slots].start()


def rest(outs, rows, held, sum_u, w_gate, w_up, w_down):
    m, n = sum_u.shape
    width = rows[0].shape[1]
    cuts = 2 if n % 256 == 0 else 1
    first = 2 + len(held)
    late = max(1, 2 * len(rows) - first)
    return pl.pallas_call(
        functools.partial(rest_kernel, outs, first),
        out_shape=[VMEM((m, n), jnp.bfloat16)] + [VMEM((m, width), jnp.bfloat16)] * len(outs),
        in_specs=[spec(VMEM)] * (len(rows) + len(held) + 2) + [spec(HBM)] * 2,
        out_specs=[spec(VMEM)] * (1 + len(outs)),
        scratch_shapes=[
            VMEM((late, width // 2, n), jnp.bfloat16),
            VMEM((DOWNS, n // cuts, width), jnp.bfloat16),
            VMEM((m, max(n, width)), jnp.float32),
            DMA((late,)),
            DMA((DOWNS,)),
        ],
        compiler_params=limit(19),
        cost_estimate=lasts(10),
        name="rest",
    )(*rows, *held, sum_u, w_gate, w_up, w_down)


def near_kernel(hidden_ref, down_hbm, sent, next_ref, buf, total, sems):
    cuts, deep = buf.shape[:2]
    copies = []
    for j in range(cuts):
        rows_at = down_hbm.at[pl.ds(j * deep, deep), :]
        copies.append(down_copy(1, rows_at, buf.at[j], sems.at[j]))
    for j in range(cuts):
        at = pl.ds(j * deep, deep)
        copies.append(down_copy(0, down_hbm.at[at, :], next_ref.at[at, :], sems.at[cuts + j]))
    for copy in copies:
        copy.start()
    for j in range(cuts):
        copies[j].wait()
        mid = hidden_ref[:, j * deep : (j + 1) * deep]
        for tile in tiles(sent.shape[1]):
            part = dot(mid, buf[j, :, tile])
            if j > 0:
                part += total[:, tile]
            if j < cuts - 1:
                total[:, tile] = part
            else:
                sent[:, tile] = part.astype(jnp.bfloat16)
    for copy in copies[cuts:]:
        copy.wait()


def near(width, hidden, w_down):
    m, n = hidden.shape
    cuts = 2 if n % 256 == 0 else 1
    return pl.pallas_call(
        near_kernel,
        out_shape=[VMEM((m, width), jnp.bfloat16), VMEM((n, width), jnp.bfloat16)],
        in_specs=[spec(VMEM), spec(HBM)],
        out_specs=[spec(VMEM)] * 2,
        scratch_shapes=[
            VMEM((cuts, n // cuts, width), jnp.bfloat16),
            VMEM((m, width), jnp.float32),
            DMA((2 * cuts,)),
        ],
        compiler_params=limit(12),
        cost_estimate=lasts(4),
        name="near",
    )(hidden, w_down)


def keep_kernel(hidden_ref, weight_ref, total_ref):
    total_ref[...] = dot(hidden_ref[...], weight_ref[...])


def keep(hidden, weight):
    m, width = hidden.shape[0], weight.shape[1]
    return pl.pallas_call(
        keep_kernel,
        out_shape=VMEM((m, width), jnp.float32),
        in_specs=[spec(VMEM)] * 2,
        out_specs=spec(VMEM),
        compiler_params=limit(4),
        cost_estimate=lasts(1),
        name="keep",
    )(hidden, weight)


def gather_kernel(total_ref, *refs):
    terms, sum_ref = refs[:-1], refs[-1]
    total = total_ref[...]
    for term in terms:
        total = total + term[...].astype(jnp.float32)
    sum_ref[...] = total


def gather(total, terms):
    return pl.pallas_call(
        gather_kernel,
        out_shape=VMEM(total.shape, jnp.float32),
        in_specs=[spec(VMEM)] * (1 + len(terms)),
        out_specs=spec(VMEM),
        compiler_params=limit(4),
        cost_estimate=lasts(2),
        name="gather",
    )(total, *terms)


def add_kernel(n, total_ref, *refs):
    terms, slabs = refs[:-n], refs[-n:]
    total = total_ref[...]
    for term in terms:
        total = total + term[...].astype(jnp.float32)
    total = total.astype(jnp.bfloat16)
    s, row = iota((SLAB, n * SLOT), 0), iota((SLAB, n * SLOT), 1)
    for k in range(n):
        take = (row == s + k * SLOT) & (s < SLOT)
        slabs[k][...] = dot(take.astype(jnp.bfloat16), total).astype(jnp.bfloat16)


def add(n, total, terms):
    return pl.pallas_call(
        functools.partial(add_kernel, n),
        out_shape=[VMEM((SLAB, total.shape[1]), jnp.bfloat16)] * n,
        in_specs=[spec(VMEM)] * (1 + len(terms)),
        out_specs=[spec(VMEM)] * n,
        compiler_params=limit(4),
        name="add",
    )(total, *terms)


def combine_kernel(n, comb_ref, *refs):
    slabs, out_ref = refs[:n], refs[n]
    full = jnp.concatenate([ref[...] for ref in slabs], axis=0)
    comb = comb_ref[...].T
    high = comb.astype(jnp.bfloat16)
    comb = comb - high.astype(jnp.float32)
    mid = comb.astype(jnp.bfloat16)
    low = (comb - mid.astype(jnp.float32)).astype(jnp.bfloat16)
    out_ref[...] = (dot(high, full) + (dot(mid, full) + dot(low, full))).astype(jnp.bfloat16)


def combine(comb, slabs):
    n, width = len(slabs), slabs[0].shape[1]
    return pl.pallas_call(
        functools.partial(combine_kernel, n),
        out_shape=jax.ShapeDtypeStruct((comb.shape[1], width), jnp.bfloat16),
        in_specs=[spec(VMEM)] * (n + 1),
        out_specs=spec(VMEM),
        compiler_params=limit(4),
        name="combine",
    )(comb, *slabs)


def swap(x, axis, k):
    size = lax.axis_size(axis)
    return lax.ppermute(x, axis, [(i, i ^ k) for i in range(size)])


def per_device(*args):
    tokens, ids, route, w_up, w_down = (
        pltpu.with_memory_space_constraint(x, HBM)
        for x in (args[0], args[1].T, args[2].T, args[4], args[5])
    )
    w_gate = args[3]
    n, parts = lax.axis_size("expert"), lax.axis_size("tensor")
    width = tokens.shape[1]
    comb, slabs = select(n, ids, route, tokens)
    slabs = [slabs[0]] + [swap(slabs[k], "expert", k) for k in range(1, n)]
    held = fetch(range(FETCH), width // 2, comb, w_up)
    mine = compact(slabs, held[-1])
    rows = [mine] + [swap(mine, "tensor", k) for k in range(1, parts)]
    sum_u, *more = own(range(FETCH, OWN), mine, held[:2], w_up)
    held = [*held[2:], *more]
    far = list(range(parts - 1, 1, -1))
    hidden, *sent = rest(far, rows, held, sum_u, w_gate, w_up, w_down)
    terms = [swap(x, "tensor", k) for k, x in zip(far, sent)]
    sent, weight0 = near(width, hidden, w_down)
    last = swap(sent, "tensor", 1)
    total = gather(keep(hidden, weight0), terms)
    back = add(n, total, [last])
    back = [back[0]] + [swap(back[k], "expert", k) for k in range(1, n)]
    return combine(comb, back)


def solution(mesh):
    return jax.shard_map(
        per_device,
        mesh=mesh,
        in_specs=(
            P(("groups", "expert"), "tensor"),
            P(("groups", "expert"), None),
            P(("groups", "expert"), None),
            P(None, ("expert", "tensor")),
            P(None, ("expert", "tensor")),
            P(("expert", "tensor"), None),
        ),
        out_specs=P(("groups", "expert"), "tensor"),
        check_vma=False,
    )
```

time: 53.2 us -> 51.4 us (0.966)
  Pallas kernels: 32.8 us -> 28.5 us
  local copies, waits for them, and re-layouts: 0 us -> 1.35 us
  waiting for transfers between devices: 6.8 us -> 7.99 us
    pallas_call x3 -> x4, Pallas kernels: 21.7 us -> 18.1 us  [the longest x1 11.8 us: rest(): pl.pallas_call(functools.partial(rest_kernel, outs, first), out_shape=[VM...]
    unnamed x0 -> x12, local copies, waits for them, and re-layouts: none -> 1.35 us
    ppermute x12, waiting for transfers between devices: 6.8 us -> 7.99 us  [swap(): return lax.ppermute(x, axis, [(i, i ^ k) for i in range(size)])]
    pallas_call x1, Pallas kernels: 3.78 us -> 3.01 us  [fetch(): pl.pallas_call(functools.partial(fetch_kernel, jobs, half), out_shape=[VM...]
  transfers between devices with their start and end apart: 12 -> 12, of which waited for: 5 -> 6; matrix products, arithmetic and copies ran while one was open for 0% -> 0% of each run, Pallas kernels for 32% -> 26%
where the time goes in v3:
time: 51.4 us; the launch traced here: 51.2 us
  Pallas kernels  28.5 us (55%)
  starting transfers between devices  13.3 us (26%)
  waiting for transfers between devices  7.99 us (16%)
  local copies, waits for them, and re-layouts  1.35 us (3%)
    ppermute x12, starting transfers between devices, swap(): return lax.ppermute(x, axis, [(i, i ^ k) for i in range(size)])  13.3 us
    pallas_call x1, Pallas kernels, rest(): pl.pallas_call(functools.partial(rest_kernel, outs, first), out_shape=[VM...  11.8 us
    ppermute x12, waiting for transfers between devices, swap(): return lax.ppermute(x, axis, [(i, i ^ k) for i in range(size)])  7.99 us
    pallas_call x1, Pallas kernels, near(): pl.pallas_call(near_kernel, out_shape=[VMEM((m, width), jnp.bfloat16), VM...  4.71 us
    pallas_call x1, Pallas kernels, own(): pl.pallas_call(functools.partial(own_kernel, jobs), out_shape=[VMEM((m, n...  4.56 us
    pallas_call x1, Pallas kernels, fetch(): pl.pallas_call(functools.partial(fetch_kernel, jobs, half), out_shape=[VM...  3.01 us
    pallas_call x1, Pallas kernels, select(): pl.pallas_call(functools.partial(select_kernel, n), out_shape=[VMEM((n *...  1.74 us
    unnamed x12, local copies, waits for them, and re-layouts  1.35 us
  transfers between devices with their start and end apart: 12, of which 6 were waited for; matrix products, arithmetic and copies ran while one was open for 0% of the time, Pallas kernels for 26%

profile of v3, /device:TPU:0, one launch (start us, length us, event | category | flops | bytes accessed | tf_op | source)
XLA Modules:
  0.0 51.2 jit_solution(1461793709110348775)
XLA Ops:
  0.0 1.7 %select.1 = (f32[64,80]{1,0:T(8,128)S(1)}, bf16[16,1536]{1,0:T(8,128)(2,1)S(1)}, bf16[16,1536]{1,0:T(8,128)(2,1)S(1)}, bf16[16,1536]{1,0:T(8,128)(2,1)S(1)}, bf16[16,1536]{1,0:T(8,128)(2,1)S(1)}) custom-call(s32[4,80]{1,0:T(4,128)} %bitcast.4, f32[4,80]{1,0:T(4,128)} %bitcast.5, bf16[80,1536]{1,0:T(8,128)(2,1)} %tok_hbm.1), custom_call_target="tpu_custom_call" | custom-call | flops 46000001024 | tf_op jit(solution)/shard_map/select/pallas_call | solution.py:86
  1.8 3.1 %collective-permute-start = (bf16[16,1536]{1,0:T(8,128)(2,1)S(1)}, bf16[16,1536]{1,0:T(8,128)(2,1)S(1)}, u32[]{:S(2)}, u32[]{:S(2)}) collective-permute-start(bf16[16,1536]{1,0:T(8,128)(2,1)S(1)} %get-tuple-element.27), channel_id=1, source_target_pairs={{0,4},{4,0},{8,12},{12,8},{1,5},{5,1},{9,13},{13,9},{2,6},{6,2},{1... | collective-permute-start | bytes 147464 | tf_op jit(solution)/shard_map/ppermute | solution.py:425
  4.8 2.6 %collective-permute-start.1 = (bf16[16,1536]{1,0:T(8,128)(2,1)S(1)}, bf16[16,1536]{1,0:T(8,128)(2,1)S(1)}, u32[]{:S(2)}, u32[]{:S(2)}) collective-permute-start(bf16[16,1536]{1,0:T(8,128)(2,1)S(1)} %get-tuple-element.28), channel_id=1, source_target_pairs={{0,8},{4,12},{8,0},{12,4},{1,9},{5,13},{9,1},{13,5},{2,10},{6,14},... | collective-permute-start | bytes 147464 | tf_op jit(solution)/shard_map/ppermute | solution.py:425
  7.4 3.0 %fetch.1 = (bf16[768,2048]{1,0:T(8,128)(2,1)S(1)}, bf16[768,2048]{1,0:T(8,128)(2,1)S(1)}) custom-call(f32[64,80]{1,0:T(8,128)S(1)} %get-tuple-element.25.order_ref.comb_ref, bf16[6144,2048]{1,0:T(8,128)(2,1)} %refs_9_.1), custom_call_target="tpu_custom_call" | custom-call | flops 230000000 | tf_op jit(solution)/shard_map/fetch/pallas_call | solution.py:146
  10.5 0.3 collective-permute-done.1.refs_2_
  10.8 2.6 %collective-permute-done.2.refs_3_ = bf16[16,1536]{1,0:T(8,128)(2,1)S(1)} collective-permute-done((bf16[16,1536]{1,0:T(8,128)(2,1)S(1)}, bf16[16,1536]{1,0:T(8,128)(2,1)S(1)}, u32[]{:S(2)}, u32[]{:S(2)}) %collective-permute-start.2) | collective-permute-done | bytes 49184 | tf_op jit(solution)/shard_map/ppermute | solution.py:425
  13.6 1.6 %collective-permute-start.4 = (bf16[40,1536]{1,0:T(8,128)(2,1)S(1)}, bf16[40,1536]{1,0:T(8,128)(2,1)S(1)}, u32[]{:S(2)}, u32[]{:S(2)}) collective-permute-start(bf16[40,1536]{1,0:T(8,128)(2,1)S(1)} %compact.1.rows_ref.refs_0_), channel_id=1, source_target_pairs={{0,2},{1,3},{2,0},{3,1},{4,6},{5,7},{6,4},{7,5},{8,10},{9,11},{10,... | collective-permute-start | bytes 368648 | tf_op jit(solution)/shard_map/ppermute | solution.py:425
  15.1 0.3 collective-permute-start.5
  15.4 4.6 %own.1 = (f32[40,2048]{1,0:T(8,128)S(1)}, bf16[768,2048]{1,0:T(8,128)(2,1)S(1)}, bf16[768,2048]{1,0:T(8,128)(2,1)S(1)}, bf16[768,2048]{1,0:T(8,128)(2,1)S(1)}) custom-call(bf16[40,1536]{1,0:T(8,128)(2,1)S(1)} %compact.1.rows_ref.refs_0_, bf16[768,2048]{1,0:T(8,128)(2,1)S(1)} %get-tuple-element.31.up_low, ...), custom_call_target="tpu_custom_call" | custom-call | flops 230000000 | tf_op jit(solution)/shard_map/own/pallas_call | solution.py:178
  20.0 1.5 %collective-permute-done.5.refs_3_ = bf16[40,1536]{1,0:T(8,128)(2,1)S(1)} collective-permute-done((bf16[40,1536]{1,0:T(8,128)(2,1)S(1)}, bf16[40,1536]{1,0:T(8,128)(2,1)S(1)}, u32[]{:S(2)}, u32[]{:S(2)}) %collective-permute-start.5) | collective-permute-done | bytes 122912 | tf_op jit(solution)/shard_map/ppermute | solution.py:425
  21.6 1.2 %slice-done.5 = s8[4194304]{0:T(1024)(128)(4,1)S(1)} async-done(((s8[25165824]{0:T(1024)(128)(4,1)}), s8[4194304]{0:T(1024)(128)(4,1)S(1)}, s32[]{:S(2)}) %slice-start.5) | async-done | bytes 4194328
  22.8 11.8 %rest.1 = (bf16[40,2048]{1,0:T(8,128)(2,1)S(1)}, bf16[40,1536]{1,0:T(8,128)(2,1)S(1)}, bf16[40,1536]{1,0:T(8,128)(2,1)S(1)}) custom-call(bf16[40,1536]{1,0:T(8,128)(2,1)S(1)} %compact.1.rows_ref.refs_0_, bf16[40,1536]{1,0:T(8,128)(2,1)S(1)} %collective-permute-done.3.refs_1_, bf16[40,1536]{1,0:T(8,128)(2,1)S(1)} %collective-permute-done.4.refs_2_, ...), custom_call_target="tpu_custom_call" | custom-call | flops 11500000256 | tf_op jit(solution)/shard_map/rest/pallas_call | solution.py:277
  34.6 1.5 %collective-permute-start.6 = (bf16[40,1536]{1,0:T(8,128)(2,1)S(1)}, bf16[40,1536]{1,0:T(8,128)(2,1)S(1)}, u32[]{:S(2)}, u32[]{:S(2)}) collective-permute-start(bf16[40,1536]{1,0:T(8,128)(2,1)S(1)} %get-tuple-element.38), channel_id=1, source_target_pairs={{0,3},{1,2},{2,1},{3,0},{4,7},{5,6},{6,5},{7,4},{8,11},{9,10},{10,... | collective-permute-start | bytes 368648 | tf_op jit(solution)/shard_map/ppermute | solution.py:425
  36.1 0.5 %collective-permute-start.7 = (bf16[40,1536]{1,0:T(8,128)(2,1)S(1)}, bf16[40,1536]{1,0:T(8,128)(2,1)S(1)}, u32[]{:S(2)}, u32[]{:S(2)}) collective-permute-start(bf16[40,1536]{1,0:T(8,128)(2,1)S(1)} %get-tuple-element.39), channel_id=1, source_target_pairs={{0,2},{1,3},{2,0},{3,1},{4,6},{5,7},{6,4},{7,5},{8,10},{9,11},{10,... | collective-permute-start | bytes 368648 | tf_op jit(solution)/shard_map/ppermute | solution.py:425
  36.7 4.7 %near.1 = (bf16[40,1536]{1,0:T(8,128)(2,1)S(1)}, bf16[2048,1536]{1,0:T(8,128)(2,1)S(1)}) custom-call(bf16[40,2048]{1,0:T(8,128)(2,1)S(1)} %get-tuple-element.36.hidden_ref, bf16[2048,6144]{1,0:T(8,128)(2,1)} %down_hbm.1), custom_call_target="tpu_custom_call" | custom-call | flops 4600000000 | tf_op jit(solution)/shard_map/near/pallas_call | solution.py:324
  41.5 1.2 %keep.1.total_ref = f32[40,1536]{1,0:T(8,128)S(1)} custom-call(bf16[40,2048]{1,0:T(8,128)(2,1)S(1)} %get-tuple-element.36.hidden_ref, bf16[2048,1536]{1,0:T(8,128)(2,1)S(1)} %get-tuple-element.37.weight_ref), custom_call_target="tpu_custom_call" | custom-call | flops 1150000000 | tf_op jit(solution)/shard_map/keep/pallas_call | solution.py:346
  42.7 0.3 collective-permute-done.7.refs_1_
  43.0 0.2 add.1
  43.2 0.4 collective-permute-start.10
  43.6 1.3 %collective-permute-start.11 = (bf16[16,1536]{1,0:T(8,128)(2,1)S(1)}, bf16[16,1536]{1,0:T(8,128)(2,1)S(1)}, u32[]{:S(2)}, u32[]{:S(2)}) collective-permute-start(bf16[16,1536]{1,0:T(8,128)(2,1)S(1)} %get-tuple-element.44), channel_id=1, source_target_pairs={{0,12},{4,8},{8,4},{12,0},{1,13},{5,9},{9,5},{13,1},{2,14},{6,10},... | collective-permute-start | bytes 147464 | tf_op jit(solution)/shard_map/ppermute | solution.py:425
  44.9 1.9 %collective-permute-start.9 = (bf16[16,1536]{1,0:T(8,128)(2,1)S(1)}, bf16[16,1536]{1,0:T(8,128)(2,1)S(1)}, u32[]{:S(2)}, u32[]{:S(2)}) collective-permute-start(bf16[16,1536]{1,0:T(8,128)(2,1)S(1)} %get-tuple-element.42), channel_id=1, source_target_pairs={{0,4},{4,0},{8,12},{12,8},{1,5},{5,1},{9,13},{13,9},{2,6},{6,2},{1... | collective-permute-start | bytes 147464 | tf_op jit(solution)/shard_map/ppermute | solution.py:425
  46.8 2.9 %collective-permute-done.10.refs_2_ = bf16[16,1536]{1,0:T(8,128)(2,1)S(1)} collective-permute-done((bf16[16,1536]{1,0:T(8,128)(2,1)S(1)}, bf16[16,1536]{1,0:T(8,128)(2,1)S(1)}, u32[]{:S(2)}, u32[]{:S(2)}) %collective-permute-start.10) | collective-permute-done | bytes 49184 | tf_op jit(solution)/shard_map/ppermute | solution.py:425
  49.7 0.5 collective-permute-done.9.refs_1_
  50.2 1.1 %combine.1 = bf16[80,1536]{1,0:T(8,128)(2,1)} custom-call(f32[64,80]{1,0:T(8,128)S(1)} %get-tuple-element.25.order_ref.comb_ref, bf16[16,1536]{1,0:T(8,128)(2,1)S(1)} %get-tuple-element.41.refs_0_, bf16[16,1536]{1,0:T(8,128)(2,1)S(1)} %collective-permute-done.9.refs_1_, bf16[16,1536]{1,0:T(8,128)(2,1)S(1)} %collective-permute-done.10.refs_2_, ...), custom_call_target="tpu_custom_call" | custom-call | tf_op jit(solution)/shard_map/combine/pallas_call | solution.py:413
  (23 shorter events, 0.5 us)
Async XLA Ops:
  1.8 8.7 %collective-permute-start = (bf16[16,1536]{1,0:T(8,128)(2,1)S(1)}, bf16[16,1536]{1,0:T(8,128)(2,1)S(1)}, u32[]{:S(2)}, u32[]{:S(2)}) collective-permute-start(bf16[16,1536]{1,0:T(8,128)(2,1)S(1)} %get-tuple-element.27), channel_id=1, source_target_pairs={{0,4},{4,0},{8,12},{12,8},{1,5},{5,1},{9,13},{13,9},{2,6},{6,2},{1... | collective-permute-start | bytes 147464 | tf_op jit(solution)/shard_map/ppermute | solution.py:425
  4.8 5.9 %collective-permute-start.1 = (bf16[16,1536]{1,0:T(8,128)(2,1)S(1)}, bf16[16,1536]{1,0:T(8,128)(2,1)S(1)}, u32[]{:S(2)}, u32[]{:S(2)}) collective-permute-start(bf16[16,1536]{1,0:T(8,128)(2,1)S(1)} %get-tuple-element.28), channel_id=1, source_target_pairs={{0,8},{4,12},{8,0},{12,4},{1,9},{5,13},{9,1},{13,5},{2,10},{6,14},... | collective-permute-start | bytes 147464 | tf_op jit(solution)/shard_map/ppermute | solution.py:425
  7.4 5.9 %collective-permute-start.2 = (bf16[16,1536]{1,0:T(8,128)(2,1)S(1)}, bf16[16,1536]{1,0:T(8,128)(2,1)S(1)}, u32[]{:S(2)}, u32[]{:S(2)}) collective-permute-start(bf16[16,1536]{1,0:T(8,128)(2,1)S(1)} %get-tuple-element.29), channel_id=1, source_target_pairs={{0,12},{4,8},{8,4},{12,0},{1,13},{5,9},{9,5},{13,1},{2,14},{6,10},... | collective-permute-start | bytes 147464 | tf_op jit(solution)/shard_map/ppermute | solution.py:425
  7.4 14.1 %slice-start = ((s8[25165824]{0:T(1024)(128)(4,1)}), s8[4194304]{0:T(1024)(128)(4,1)S(1)}, s32[]{:S(2)}) async-start(s8[25165824]{0:T(1024)(128)(4,1)} %bitcast.2), calls=%async_computation | async-start | bytes 8388608
  7.4 14.1 %slice-start.1 = ((s8[25165824]{0:T(1024)(128)(4,1)}), s8[4194304]{0:T(1024)(128)(4,1)S(1)}, s32[]{:S(2)}) async-start(s8[25165824]{0:T(1024)(128)(4,1)} %bitcast.2), calls=%async_computation.1 | async-start | bytes 8388608
  7.4 14.1 %slice-start.2 = ((s8[25165824]{0:T(1024)(128)(4,1)}), s8[4194304]{0:T(1024)(128)(4,1)S(1)}, s32[]{:S(2)}) async-start(s8[25165824]{0:T(1024)(128)(4,1)} %bitcast.2), calls=%async_computation.2 | async-start | bytes 8388608
  13.5 6.5 %collective-permute-start.3 = (bf16[40,1536]{1,0:T(8,128)(2,1)S(1)}, bf16[40,1536]{1,0:T(8,128)(2,1)S(1)}, u32[]{:S(2)}, u32[]{:S(2)}) collective-permute-start(bf16[40,1536]{1,0:T(8,128)(2,1)S(1)} %compact.1.rows_ref.refs_0_), channel_id=1, source_target_pairs={{0,1},{1,0},{2,3},{3,2},{4,5},{5,4},{6,7},{7,6},{8,9},{9,8},{10,11... | collective-permute-start | bytes 368648 | tf_op jit(solution)/shard_map/ppermute | solution.py:425
  13.6 6.4 %collective-permute-start.4 = (bf16[40,1536]{1,0:T(8,128)(2,1)S(1)}, bf16[40,1536]{1,0:T(8,128)(2,1)S(1)}, u32[]{:S(2)}, u32[]{:S(2)}) collective-permute-start(bf16[40,1536]{1,0:T(8,128)(2,1)S(1)} %compact.1.rows_ref.refs_0_), channel_id=1, source_target_pairs={{0,2},{1,3},{2,0},{3,1},{4,6},{5,7},{6,4},{7,5},{8,10},{9,11},{10,... | collective-permute-start | bytes 368648 | tf_op jit(solution)/shard_map/ppermute | solution.py:425
  15.1 6.4 %collective-permute-start.5 = (bf16[40,1536]{1,0:T(8,128)(2,1)S(1)}, bf16[40,1536]{1,0:T(8,128)(2,1)S(1)}, u32[]{:S(2)}, u32[]{:S(2)}) collective-permute-start(bf16[40,1536]{1,0:T(8,128)(2,1)S(1)} %compact.1.rows_ref.refs_0_), channel_id=1, source_target_pairs={{0,3},{1,2},{2,1},{3,0},{4,7},{5,6},{6,5},{7,4},{8,11},{9,10},{10,... | collective-permute-start | bytes 368648 | tf_op jit(solution)/shard_map/ppermute | solution.py:425
  15.4 6.1 %slice-start.3 = ((s8[25165824]{0:T(1024)(128)(4,1)}), s8[4194304]{0:T(1024)(128)(4,1)S(1)}, s32[]{:S(2)}) async-start(s8[25165824]{0:T(1024)(128)(4,1)} %bitcast.2), calls=%async_computation.3 | async-start | bytes 8388608
  15.4 6.2 %slice-start.4 = ((s8[25165824]{0:T(1024)(128)(4,1)}), s8[4194304]{0:T(1024)(128)(4,1)S(1)}, s32[]{:S(2)}) async-start(s8[25165824]{0:T(1024)(128)(4,1)} %bitcast.2), calls=%async_computation.4 | async-start | bytes 8388608
  15.4 7.4 %slice-start.5 = ((s8[25165824]{0:T(1024)(128)(4,1)}), s8[4194304]{0:T(1024)(128)(4,1)S(1)}, s32[]{:S(2)}) async-start(s8[25165824]{0:T(1024)(128)(4,1)} %bitcast.2), calls=%async_computation.5 | async-start | bytes 8388608
  34.6 8.0 %collective-permute-start.6 = (bf16[40,1536]{1,0:T(8,128)(2,1)S(1)}, bf16[40,1536]{1,0:T(8,128)(2,1)S(1)}, u32[]{:S(2)}, u32[]{:S(2)}) collective-permute-start(bf16[40,1536]{1,0:T(8,128)(2,1)S(1)} %get-tuple-element.38), channel_id=1, source_target_pairs={{0,3},{1,2},{2,1},{3,0},{4,7},{5,6},{6,5},{7,4},{8,11},{9,10},{10,... | collective-permute-start | bytes 368648 | tf_op jit(solution)/shard_map/ppermute | solution.py:425
  36.1 6.8 %collective-permute-start.7 = (bf16[40,1536]{1,0:T(8,128)(2,1)S(1)}, bf16[40,1536]{1,0:T(8,128)(2,1)S(1)}, u32[]{:S(2)}, u32[]{:S(2)}) collective-permute-start(bf16[40,1536]{1,0:T(8,128)(2,1)S(1)} %get-tuple-element.39), channel_id=1, source_target_pairs={{0,2},{1,3},{2,0},{3,1},{4,6},{5,7},{6,4},{7,5},{8,10},{9,11},{10,... | collective-permute-start | bytes 368648 | tf_op jit(solution)/shard_map/ppermute | solution.py:425
  41.4 1.6 %collective-permute-start.8 = (bf16[40,1536]{1,0:T(8,128)(2,1)S(1)}, bf16[40,1536]{1,0:T(8,128)(2,1)S(1)}, u32[]{:S(2)}, u32[]{:S(2)}) collective-permute-start(bf16[40,1536]{1,0:T(8,128)(2,1)S(1)} %get-tuple-element.40), channel_id=1, source_target_pairs={{0,1},{1,0},{2,3},{3,2},{4,5},{5,4},{6,7},{7,6},{8,9},{9,8},{10,11... | collective-permute-start | bytes 368648 | tf_op jit(solution)/shard_map/ppermute | solution.py:425
  43.2 6.5 %collective-permute-start.10 = (bf16[16,1536]{1,0:T(8,128)(2,1)S(1)}, bf16[16,1536]{1,0:T(8,128)(2,1)S(1)}, u32[]{:S(2)}, u32[]{:S(2)}) collective-permute-start(bf16[16,1536]{1,0:T(8,128)(2,1)S(1)} %get-tuple-element.43), channel_id=1, source_target_pairs={{0,8},{4,12},{8,0},{12,4},{1,9},{5,13},{9,1},{13,5},{2,10},{6,14},... | collective-permute-start | bytes 147464 | tf_op jit(solution)/shard_map/ppermute | solution.py:425
  43.6 6.1 %collective-permute-start.11 = (bf16[16,1536]{1,0:T(8,128)(2,1)S(1)}, bf16[16,1536]{1,0:T(8,128)(2,1)S(1)}, u32[]{:S(2)}, u32[]{:S(2)}) collective-permute-start(bf16[16,1536]{1,0:T(8,128)(2,1)S(1)} %get-tuple-element.44), channel_id=1, source_target_pairs={{0,12},{4,8},{8,4},{12,0},{1,13},{5,9},{9,5},{13,1},{2,14},{6,10},... | collective-permute-start | bytes 147464 | tf_op jit(solution)/shard_map/ppermute | solution.py:425
  44.9 5.3 %collective-permute-start.9 = (bf16[16,1536]{1,0:T(8,128)(2,1)S(1)}, bf16[16,1536]{1,0:T(8,128)(2,1)S(1)}, u32[]{:S(2)}, u32[]{:S(2)}) collective-permute-start(bf16[16,1536]{1,0:T(8,128)(2,1)S(1)} %get-tuple-element.42), channel_id=1, source_target_pairs={{0,4},{4,0},{8,12},{12,8},{1,5},{5,1},{9,13},{13,9},{2,6},{6,2},{1... | collective-permute-start | bytes 147464 | tf_op jit(solution)/shard_map/ppermute | solution.py:425

commit v4 on v3

--- a/solution.py
+++ b/solution.py
@@ -11,7 +11,7 @@
 SLOT = 10
 SLAB = 16
 FETCH = 2
-OWN = 5
+OWN = 4
 DOWNS = 3
 TILE = 512
 WIDE = 512
@@ -36,6 +36,23 @@
 
 def dot(a, b):
     return lax.dot_general(a, b, (((1,), (0,)), ((), ())), preferred_element_type=jnp.float32)
+
+
+def folds(width):
+    return 4 if width % 512 == 0 else 1
+
+
+def slab_rows(width):
+    return max(SLAB, folds(width) * SLOT)
+
+
+def stack(slabs):
+    return jnp.concatenate([ref[...].astype(jnp.float32) for ref in slabs], 0).astype(jnp.bfloat16)
+
+
+def pieces(width):
+    size = width // folds(width)
+    return [(p, slice(p * size, (p + 1) * size)) for p in range(folds(width))]
 
 
 def iota(shape, dim):
@@ -70,6 +87,10 @@
     count = tok.shape[0]
     before = (iota((count, count), 0) <= iota((count, count), 1)).astype(jnp.bfloat16)
     slot = iota((SLAB, count), 0).astype(jnp.float32)
+    width = tok.shape[1]
+    tall = slab_rows(width)
+    row = iota((tall, count), 0).astype(jnp.float32)
+    members, positions = [], []
     for k in range(n):
         hit = ids == (me ^ k) // replicas
         member = jnp.sum(jnp.where(hit, 1.0, 0.0), axis=0, keepdims=True)
@@ -77,8 +98,19 @@
         member = jnp.broadcast_to(member, (SLAB, count))
         position = dot(member.astype(jnp.bfloat16), before) - 1.0
         placed = jnp.where(position == slot, member, 0.0)
-        slabs[k][...] = dot(placed.astype(jnp.bfloat16), tok).astype(jnp.bfloat16)
         comb_ref[k * SLAB : (k + 1) * SLAB, :] = placed * weight
+        members.append(jnp.broadcast_to(member[:1], (tall, count)))
+        positions.append(jnp.broadcast_to(position[:1], (tall, count)))
+    total = None
+    for p, piece in pieces(width):
+        take = [
+            jnp.where(position + float(p * SLOT) == row, member, 0.0)
+            for position, member in zip(positions, members)
+        ]
+        part = dot(jnp.concatenate(take, 0).astype(jnp.bfloat16), tok[:, piece])
+        total = part if total is None else total + part
+    for k in range(n):
+        slabs[k][...] = total[k * tall : (k + 1) * tall].astype(jnp.bfloat16)
 
 
 def select(n, ids, route, tokens):
@@ -86,7 +118,7 @@
     out = pl.pallas_call(
         functools.partial(select_kernel, n),
         out_shape=[VMEM((n * SLAB, count), jnp.float32)]
-        + [VMEM((SLAB, width), jnp.bfloat16)] * n,
+        + [VMEM((slab_rows(width), width // folds(width)), jnp.bfloat16)] * n,
         in_specs=[spec(HBM)] * 3,
         out_specs=[spec(VMEM)] * (n + 1),
         scratch_shapes=[
@@ -104,15 +136,17 @@
 
 def compact_kernel(n, *refs):
     slabs, rows_ref = refs[:n], refs[-1]
-    full = jnp.concatenate([ref[...] for ref in slabs], axis=0)
-    col = iota((n * SLOT, n * SLAB), 1)
-    s = col % SLAB
-    take = (iota((n * SLOT, n * SLAB), 0) == (col // SLAB) * SLOT + s) & (s < SLOT)
-    rows_ref[...] = dot(take.astype(jnp.bfloat16), full).astype(jnp.bfloat16)
-
-
-def compact(slabs, after):
-    n, width = len(slabs), slabs[0].shape[1]
+    full = stack(slabs)
+    tall, width = slabs[0].shape[0], rows_ref.shape[1]
+    col = iota((n * SLOT, n * tall), 1)
+    for p, piece in pieces(width):
+        s = col % tall - p * SLOT
+        take = (iota((n * SLOT, n * tall), 0) == col // tall * SLOT + s) & (s >= 0) & (s < SLOT)
+        rows_ref[:, piece] = dot(take.astype(jnp.bfloat16), full).astype(jnp.bfloat16)
+
+
+def compact(width, slabs, after):
+    n = len(slabs)
     return pl.pallas_call(
         functools.partial(compact_kernel, n),
         out_shape=VMEM((n * SLOT, width), jnp.bfloat16),
@@ -155,7 +189,7 @@
     )(order, w_up)
 
 
-def own_kernel(jobs, rows_ref, up_low, up_high, up_hbm, sum_u, *refs):
+def own_kernel(jobs, n, rows_ref, comb_ref, up_low, up_high, up_hbm, sum_u, mix_ref, *refs):
     held, sems = refs[:-1], refs[-1]
     half = rows_ref.shape[1] // 2
     copies = job_copies(jobs, half, up_hbm, held, sems)
@@ -169,23 +203,36 @@
         while done < len(copies) and done * len(steps) < (i + 1) * len(copies):
             copies[done].wait()
             done += 1
+    comb = comb_ref[...].T
+    count, width = comb.shape[0], rows_ref.shape[1]
+    tall = slab_rows(width)
+    row, col = iota((n * SLAB, n * tall), 0), iota((n * SLAB, n * tall), 1)
+    for i in range(3):
+        term = comb.astype(jnp.bfloat16)
+        comb = comb - term.astype(jnp.float32)
+        for p, _ in pieces(width):
+            s = col % tall - p * SLOT
+            take = (row == col // tall * SLAB + s) & (s >= 0) & (s < SLOT)
+            part = dot(term, take.astype(jnp.bfloat16)).astype(jnp.bfloat16)
+            mix_ref[i, p * count : (p + 1) * count, :] = part
     for copy in copies[done:]:
         copy.wait()
 
 
-def own(jobs, rows, held, w_up):
+def own(jobs, axis, rows, comb, held, w_up):
     (m, width), n = rows.shape, w_up.shape[1]
-    return pl.pallas_call(
-        functools.partial(own_kernel, jobs),
-        out_shape=[VMEM((m, n), jnp.float32)]
+    mix = (3, folds(width) * comb.shape[1], axis * slab_rows(width))
+    return pl.pallas_call(
+        functools.partial(own_kernel, jobs, axis),
+        out_shape=[VMEM((m, n), jnp.float32), VMEM(mix, jnp.bfloat16)]
         + [VMEM((width // 2, n), jnp.bfloat16)] * len(jobs),
-        in_specs=[spec(VMEM)] * 3 + [spec(HBM)],
-        out_specs=[spec(VMEM)] * (1 + len(jobs)),
+        in_specs=[spec(VMEM)] * 4 + [spec(HBM)],
+        out_specs=[spec(VMEM)] * (2 + len(jobs)),
         scratch_shapes=[DMA((len(jobs),))],
         compiler_params=limit(2),
         cost_estimate=lasts(0.2),
         name="own",
-    )(rows, *held, w_up)
+    )(rows, comb, *held, w_up)
 
 
 def down_copy(k, down_hbm, target, sem):
@@ -286,7 +333,7 @@
             DMA((late,)),
             DMA((DOWNS,)),
         ],
-        compiler_params=limit(19),
+        compiler_params=limit(22),
         cost_estimate=lasts(10),
         name="rest",
     )(*rows, *held, sum_u, w_gate, w_up, w_down)
@@ -380,16 +427,24 @@
     for term in terms:
         total = total + term[...].astype(jnp.float32)
     total = total.astype(jnp.bfloat16)
-    s, row = iota((SLAB, n * SLOT), 0), iota((SLAB, n * SLOT), 1)
+    width = total.shape[1]
+    tall = slab_rows(width)
+    row, col = iota((n * tall, n * SLOT), 0), iota((n * tall, n * SLOT), 1)
+    full = None
+    for p, piece in pieces(width):
+        s = row % tall - p * SLOT
+        take = (col == row // tall * SLOT + s) & (s >= 0) & (s < SLOT)
+        part = dot(take.astype(jnp.bfloat16), total[:, piece])
+        full = part if full is None else full + part
     for k in range(n):
-        take = (row == s + k * SLOT) & (s < SLOT)
-        slabs[k][...] = dot(take.astype(jnp.bfloat16), total).astype(jnp.bfloat16)
+        slabs[k][...] = full[k * tall : (k + 1) * tall].astype(jnp.bfloat16)
 
 
 def add(n, total, terms):
+    width = total.shape[1]
     return pl.pallas_call(
         functools.partial(add_kernel, n),
-        out_shape=[VMEM((SLAB, total.shape[1]), jnp.bfloat16)] * n,
+        out_shape=[VMEM((slab_rows(width), width // folds(width)), jnp.bfloat16)] * n,
         in_specs=[spec(VMEM)] * (1 + len(terms)),
         out_specs=[spec(VMEM)] * n,
         compiler_params=limit(4),
@@ -397,27 +452,25 @@
     )(total, *terms)
 
 
-def combine_kernel(n, comb_ref, *refs):
-    slabs, out_ref = refs[:n], refs[n]
-    full = jnp.concatenate([ref[...] for ref in slabs], axis=0)
-    comb = comb_ref[...].T
-    high = comb.astype(jnp.bfloat16)
-    comb = comb - high.astype(jnp.float32)
-    mid = comb.astype(jnp.bfloat16)
-    low = (comb - mid.astype(jnp.float32)).astype(jnp.bfloat16)
-    out_ref[...] = (dot(high, full) + (dot(mid, full) + dot(low, full))).astype(jnp.bfloat16)
-
-
-def combine(comb, slabs):
-    n, width = len(slabs), slabs[0].shape[1]
-    return pl.pallas_call(
-        functools.partial(combine_kernel, n),
-        out_shape=jax.ShapeDtypeStruct((comb.shape[1], width), jnp.bfloat16),
+def combine_kernel(mix_ref, *refs):
+    slabs, out_ref = refs[:-1], refs[-1]
+    full = stack(slabs)
+    count, width = out_ref.shape
+    total = dot(mix_ref[0], full) + (dot(mix_ref[1], full) + dot(mix_ref[2], full))
+    for p, piece in pieces(width):
+        out_ref[:, piece] = total[p * count : (p + 1) * count].astype(jnp.bfloat16)
+
+
+def combine(width, mix, slabs):
+    n = len(slabs)
+    return pl.pallas_call(
+        combine_kernel,
+        out_shape=jax.ShapeDtypeStruct((mix.shape[1] // folds(width), width), jnp.bfloat16),
         in_specs=[spec(VMEM)] * (n + 1),
         out_specs=spec(VMEM),
         compiler_params=limit(4),
         name="combine",
-    )(comb, *slabs)
+    )(mix, *slabs)
 
 
 def swap(x, axis, k):
@@ -436,9 +489,9 @@
     comb, slabs = select(n, ids, route, tokens)
     slabs = [slabs[0]] + [swap(slabs[k], "expert", k) for k in range(1, n)]
     held = fetch(range(FETCH), width // 2, comb, w_up)
-    mine = compact(slabs, held[-1])
+    mine = compact(width, slabs, held[-1])
     rows = [mine] + [swap(mine, "tensor", k) for k in range(1, parts)]
-    sum_u, *more = own(range(FETCH, OWN), mine, held[:2], w_up)
+    sum_u, mix, *more = own(range(FETCH, OWN), n, mine, comb, held[:2], w_up)
     held = [*held[2:], *more]
     far = list(range(parts - 1, 1, -1))
     hidden, *sent = rest(far, rows, held, sum_u, w_gate, w_up, w_down)
@@ -448,7 +501,7 @@
     total = gather(keep(hidden, weight0), terms)
     back = add(n, total, [last])
     back = [back[0]] + [swap(back[k], "expert", k) for k in range(1, n)]
-    return combine(comb, back)
+    return combine(width, mix, back)
 
 
 def solution(mesh):

time: 51.4 us -> 49.2 us (0.957)
  local copies, waits for them, and re-layouts: 1.35 us -> 0.45 us
  Pallas kernels: 28.5 us -> 27.6 us
    unnamed x12, local copies, waits for them, and re-layouts: 1.35 us -> 0.45 us
    pallas_call x3, Pallas kernels: 5.85 us -> 5.21 us  [the longest x1 3.79 us: own(): pl.pallas_call(functools.partial(own_kernel, jobs, axis), out_shape=[VMEM...]
where the time goes in v4:
time: 49.2 us; the launch traced here: 49.1 us
  Pallas kernels  27.6 us (56%)
  starting transfers between devices  13.3 us (27%)
  waiting for transfers between devices  7.62 us (15%)
    ppermute x12, starting transfers between devices, swap(): return lax.ppermute(x, axis, [(i, i ^ k) for i in range(size)])  13.3 us
    pallas_call x1, Pallas kernels, rest(): pl.pallas_call(functools.partial(rest_kernel, outs, first), out_shape=[VM...  11.8 us
    ppermute x12, waiting for transfers between devices, swap(): return lax.ppermute(x, axis, [(i, i ^ k) for i in range(size)])  7.62 us
    pallas_call x1, Pallas kernels, near(): pl.pallas_call(near_kernel, out_shape=[VMEM((m, width), jnp.bfloat16), VM...  4.71 us
    pallas_call x1, Pallas kernels, own(): pl.pallas_call(functools.partial(own_kernel, jobs, axis), out_shape=[VMEM...  3.79 us
    pallas_call x1, Pallas kernels, fetch(): pl.pallas_call(functools.partial(fetch_kernel, jobs, half), out_shape=[VM...  3.01 us
    pallas_call x1, Pallas kernels, select(): pl.pallas_call(functools.partial(select_kernel, n), out_shape=[VMEM((n *...  1.4 us
    pallas_call x1, Pallas kernels, keep(): pl.pallas_call(keep_kernel, out_shape=VMEM((m, width), jnp.float32), in_s...  1.16 us
  transfers between devices with their start and end apart: 12, of which 6 were waited for; matrix products, arithmetic and copies ran while one was open for 0% of the time, Pallas kernels for 26%

profile of v4, /device:TPU:0, one launch (start us, length us, event | category | flops | bytes accessed | tf_op | source)
XLA Modules:
  0.0 49.1 jit_solution(16893042505161462321)
XLA Ops:
  0.0 1.4 %select.1 = (f32[64,80]{1,0:T(8,128)S(1)}, bf16[40,384]{1,0:T(8,128)(2,1)S(1)}, bf16[40,384]{1,0:T(8,128)(2,1)S(1)}, bf16[40,384]{1,0:T(8,128)(2,1)S(1)}, bf16[40,384]{1,0:T(8,128)(2,1)S(1)}) custom-call(s32[4,80]{1,0:T(4,128)} %bitcast.4, f32[4,80]{1,0:T(4,128)} %bitcast.5, bf16[80,1536]{1,0:T(8,128)(2,1)} %tok_hbm.1), custom_call_target="tpu_custom_call" | custom-call | flops 46000001024 | tf_op jit(solution)/shard_map/select/pallas_call | solution.py:118
  1.4 3.1 %collective-permute-start = (bf16[40,384]{1,0:T(8,128)(2,1)S(1)}, bf16[40,384]{1,0:T(8,128)(2,1)S(1)}, u32[]{:S(2)}, u32[]{:S(2)}) collective-permute-start(bf16[40,384]{1,0:T(8,128)(2,1)S(1)} %get-tuple-element.26), channel_id=1, source_target_pairs={{0,4},{4,0},{8,12},{12,8},{1,5},{5,1},{9,13},{13,9},{2,6},{6,2},{1... | collective-permute-start | bytes 92168 | tf_op jit(solution)/shard_map/ppermute | solution.py:478
  4.5 2.6 %collective-permute-start.1 = (bf16[40,384]{1,0:T(8,128)(2,1)S(1)}, bf16[40,384]{1,0:T(8,128)(2,1)S(1)}, u32[]{:S(2)}, u32[]{:S(2)}) collective-permute-start(bf16[40,384]{1,0:T(8,128)(2,1)S(1)} %get-tuple-element.27), channel_id=1, source_target_pairs={{0,8},{4,12},{8,0},{12,4},{1,9},{5,13},{9,1},{13,5},{2,10},{6,14},... | collective-permute-start | bytes 92168 | tf_op jit(solution)/shard_map/ppermute | solution.py:478
  7.1 3.0 %fetch.1 = (bf16[768,2048]{1,0:T(8,128)(2,1)S(1)}, bf16[768,2048]{1,0:T(8,128)(2,1)S(1)}) custom-call(f32[64,80]{1,0:T(8,128)S(1)} %get-tuple-element.29.order_ref.comb_ref, bf16[6144,2048]{1,0:T(8,128)(2,1)} %refs_8_.1), custom_call_target="tpu_custom_call" | custom-call | flops 230000000 | tf_op jit(solution)/shard_map/fetch/pallas_call | solution.py:180
  10.1 2.6 %collective-permute-done.2.refs_3_ = bf16[40,384]{1,0:T(8,128)(2,1)S(1)} collective-permute-done((bf16[40,384]{1,0:T(8,128)(2,1)S(1)}, bf16[40,384]{1,0:T(8,128)(2,1)S(1)}, u32[]{:S(2)}, u32[]{:S(2)}) %collective-permute-start.2) | collective-permute-done | bytes 30752 | tf_op jit(solution)/shard_map/ppermute | solution.py:478
  12.8 0.2 compact.1.rows_ref.refs_0_
  13.1 1.6 %collective-permute-start.4 = (bf16[40,1536]{1,0:T(8,128)(2,1)S(1)}, bf16[40,1536]{1,0:T(8,128)(2,1)S(1)}, u32[]{:S(2)}, u32[]{:S(2)}) collective-permute-start(bf16[40,1536]{1,0:T(8,128)(2,1)S(1)} %compact.1.rows_ref.refs_0_), channel_id=1, source_target_pairs={{0,2},{1,3},{2,0},{3,1},{4,6},{5,7},{6,4},{7,5},{8,10},{9,11},{10,... | collective-permute-start | bytes 368648 | tf_op jit(solution)/shard_map/ppermute | solution.py:478
  14.6 0.3 collective-permute-start.5
  15.0 3.8 %own.1 = (f32[40,2048]{1,0:T(8,128)S(1)}, bf16[3,320,160]{2,1,0:T(8,128)(2,1)S(1)}, bf16[768,2048]{1,0:T(8,128)(2,1)S(1)}, bf16[768,2048]{1,0:T(8,128)(2,1)S(1)}) custom-call(bf16[40,1536]{1,0:T(8,128)(2,1)S(1)} %compact.1.rows_ref.refs_0_, f32[64,80]{1,0:T(8,128)S(1)} %get-tuple-element.29.order_ref.comb_ref, ...), custom_call_target="tpu_custom_call" | custom-call | flops 230000000 | tf_op jit(solution)/shard_map/own/pallas_call | solution.py:225
  18.8 0.5 %collective-permute-done.4.refs_2_ = bf16[40,1536]{1,0:T(8,128)(2,1)S(1)} collective-permute-done((bf16[40,1536]{1,0:T(8,128)(2,1)S(1)}, bf16[40,1536]{1,0:T(8,128)(2,1)S(1)}, u32[]{:S(2)}, u32[]{:S(2)}) %collective-permute-start.4) | collective-permute-done | bytes 122912 | tf_op jit(solution)/shard_map/ppermute | solution.py:478
  19.3 1.7 %collective-permute-done.5.refs_3_ = bf16[40,1536]{1,0:T(8,128)(2,1)S(1)} collective-permute-done((bf16[40,1536]{1,0:T(8,128)(2,1)S(1)}, bf16[40,1536]{1,0:T(8,128)(2,1)S(1)}, u32[]{:S(2)}, u32[]{:S(2)}) %collective-permute-start.5) | collective-permute-done | bytes 122912 | tf_op jit(solution)/shard_map/ppermute | solution.py:478
  21.0 0.4 slice-done.5
  21.5 11.8 %rest.1 = (bf16[40,2048]{1,0:T(8,128)(2,1)S(1)}, bf16[40,1536]{1,0:T(8,128)(2,1)S(1)}, bf16[40,1536]{1,0:T(8,128)(2,1)S(1)}) custom-call(bf16[40,1536]{1,0:T(8,128)(2,1)S(1)} %compact.1.rows_ref.refs_0_, bf16[40,1536]{1,0:T(8,128)(2,1)S(1)} %collective-permute-done.3.refs_1_, bf16[40,1536]{1,0:T(8,128)(2,1)S(1)} %collective-permute-done.4.refs_2_, ...), custom_call_target="tpu_custom_call" | custom-call | flops 11500000256 | tf_op jit(solution)/shard_map/rest/pallas_call | solution.py:324
  33.3 1.5 %collective-permute-start.6 = (bf16[40,1536]{1,0:T(8,128)(2,1)S(1)}, bf16[40,1536]{1,0:T(8,128)(2,1)S(1)}, u32[]{:S(2)}, u32[]{:S(2)}) collective-permute-start(bf16[40,1536]{1,0:T(8,128)(2,1)S(1)} %get-tuple-element.38), channel_id=1, source_target_pairs={{0,3},{1,2},{2,1},{3,0},{4,7},{5,6},{6,5},{7,4},{8,11},{9,10},{10,... | collective-permute-start | bytes 368648 | tf_op jit(solution)/shard_map/ppermute | solution.py:478
  34.8 0.5 %collective-permute-start.7 = (bf16[40,1536]{1,0:T(8,128)(2,1)S(1)}, bf16[40,1536]{1,0:T(8,128)(2,1)S(1)}, u32[]{:S(2)}, u32[]{:S(2)}) collective-permute-start(bf16[40,1536]{1,0:T(8,128)(2,1)S(1)} %get-tuple-element.39), channel_id=1, source_target_pairs={{0,2},{1,3},{2,0},{3,1},{4,6},{5,7},{6,4},{7,5},{8,10},{9,11},{10,... | collective-permute-start | bytes 368648 | tf_op jit(solution)/shard_map/ppermute | solution.py:478
  35.3 4.7 %near.1 = (bf16[40,1536]{1,0:T(8,128)(2,1)S(1)}, bf16[2048,1536]{1,0:T(8,128)(2,1)S(1)}) custom-call(bf16[40,2048]{1,0:T(8,128)(2,1)S(1)} %get-tuple-element.36.hidden_ref, bf16[2048,6144]{1,0:T(8,128)(2,1)} %down_hbm.1), custom_call_target="tpu_custom_call" | custom-call | flops 4600000000 | tf_op jit(solution)/shard_map/near/pallas_call | solution.py:371
  40.1 1.2 %keep.1.total_ref = f32[40,1536]{1,0:T(8,128)S(1)} custom-call(bf16[40,2048]{1,0:T(8,128)(2,1)S(1)} %get-tuple-element.36.hidden_ref, bf16[2048,1536]{1,0:T(8,128)(2,1)S(1)} %get-tuple-element.37.weight_ref), custom_call_target="tpu_custom_call" | custom-call | flops 1150000000 | tf_op jit(solution)/shard_map/keep/pallas_call | solution.py:393
  41.3 0.3 collective-permute-done.7.refs_1_
  41.7 0.3 add.1
  42.1 1.7 %collective-permute-start.11 = (bf16[40,384]{1,0:T(8,128)(2,1)S(1)}, bf16[40,384]{1,0:T(8,128)(2,1)S(1)}, u32[]{:S(2)}, u32[]{:S(2)}) collective-permute-start(bf16[40,384]{1,0:T(8,128)(2,1)S(1)} %get-tuple-element.44), channel_id=1, source_target_pairs={{0,12},{4,8},{8,4},{12,0},{1,13},{5,9},{9,5},{13,1},{2,14},{6,10},... | collective-permute-start | bytes 92168 | tf_op jit(solution)/shard_map/ppermute | solution.py:478
  43.7 1.8 %collective-permute-start.9 = (bf16[40,384]{1,0:T(8,128)(2,1)S(1)}, bf16[40,384]{1,0:T(8,128)(2,1)S(1)}, u32[]{:S(2)}, u32[]{:S(2)}) collective-permute-start(bf16[40,384]{1,0:T(8,128)(2,1)S(1)} %get-tuple-element.42), channel_id=1, source_target_pairs={{0,4},{4,0},{8,12},{12,8},{1,5},{5,1},{9,13},{13,9},{2,6},{6,2},{1... | collective-permute-start | bytes 92168 | tf_op jit(solution)/shard_map/ppermute | solution.py:478
  45.5 1.6 %collective-permute-done.10.refs_2_ = bf16[40,384]{1,0:T(8,128)(2,1)S(1)} collective-permute-done((bf16[40,384]{1,0:T(8,128)(2,1)S(1)}, bf16[40,384]{1,0:T(8,128)(2,1)S(1)}, u32[]{:S(2)}, u32[]{:S(2)}) %collective-permute-start.10) | collective-permute-done | bytes 30752 | tf_op jit(solution)/shard_map/ppermute | solution.py:478
  47.2 0.8 %collective-permute-done.11.refs_3_ = bf16[40,384]{1,0:T(8,128)(2,1)S(1)} collective-permute-done((bf16[40,384]{1,0:T(8,128)(2,1)S(1)}, bf16[40,384]{1,0:T(8,128)(2,1)S(1)}, u32[]{:S(2)}, u32[]{:S(2)}) %collective-permute-start.11) | collective-permute-done | bytes 30752 | tf_op jit(solution)/shard_map/ppermute | solution.py:478
  48.0 1.1 %combine.1 = bf16[80,1536]{1,0:T(8,128)(2,1)} custom-call(bf16[3,320,160]{2,1,0:T(8,128)(2,1)S(1)} %get-tuple-element.32.mix_ref, bf16[40,384]{1,0:T(8,128)(2,1)S(1)} %get-tuple-element.41.refs_0_, bf16[40,384]{1,0:T(8,128)(2,1)S(1)} %collective-permute-done.9.refs_1_, bf16[40,384]{1,0:T(8,128)(2,1)S(1)} %collective-permute-done.10.refs_2_, ...), custom_call_target="tpu_custom_call" | custom-call | tf_op jit(solution)/shard_map/combine/pallas_call | solution.py:466
  (23 shorter events, 0.3 us)
Async XLA Ops:
  1.4 8.7 %collective-permute-start = (bf16[40,384]{1,0:T(8,128)(2,1)S(1)}, bf16[40,384]{1,0:T(8,128)(2,1)S(1)}, u32[]{:S(2)}, u32[]{:S(2)}) collective-permute-start(bf16[40,384]{1,0:T(8,128)(2,1)S(1)} %get-tuple-element.26), channel_id=1, source_target_pairs={{0,4},{4,0},{8,12},{12,8},{1,5},{5,1},{9,13},{13,9},{2,6},{6,2},{1... | collective-permute-start | bytes 92168 | tf_op jit(solution)/shard_map/ppermute | solution.py:478
  4.5 5.6 %collective-permute-start.1 = (bf16[40,384]{1,0:T(8,128)(2,1)S(1)}, bf16[40,384]{1,0:T(8,128)(2,1)S(1)}, u32[]{:S(2)}, u32[]{:S(2)}) collective-permute-start(bf16[40,384]{1,0:T(8,128)(2,1)S(1)} %get-tuple-element.27), channel_id=1, source_target_pairs={{0,8},{4,12},{8,0},{12,4},{1,9},{5,13},{9,1},{13,5},{2,10},{6,14},... | collective-permute-start | bytes 92168 | tf_op jit(solution)/shard_map/ppermute | solution.py:478
  7.1 5.7 %collective-permute-start.2 = (bf16[40,384]{1,0:T(8,128)(2,1)S(1)}, bf16[40,384]{1,0:T(8,128)(2,1)S(1)}, u32[]{:S(2)}, u32[]{:S(2)}) collective-permute-start(bf16[40,384]{1,0:T(8,128)(2,1)S(1)} %get-tuple-element.28), channel_id=1, source_target_pairs={{0,12},{4,8},{8,4},{12,0},{1,13},{5,9},{9,5},{13,1},{2,14},{6,10},... | collective-permute-start | bytes 92168 | tf_op jit(solution)/shard_map/ppermute | solution.py:478
  7.1 13.9 %slice-start = ((s8[25165824]{0:T(1024)(128)(4,1)}), s8[4194304]{0:T(1024)(128)(4,1)S(1)}, s32[]{:S(2)}) async-start(s8[25165824]{0:T(1024)(128)(4,1)} %bitcast.2), calls=%async_computation | async-start | bytes 8388608
  7.1 13.9 %slice-start.1 = ((s8[25165824]{0:T(1024)(128)(4,1)}), s8[4194304]{0:T(1024)(128)(4,1)S(1)}, s32[]{:S(2)}) async-start(s8[25165824]{0:T(1024)(128)(4,1)} %bitcast.2), calls=%async_computation.1 | async-start | bytes 8388608
  7.1 13.9 %slice-start.2 = ((s8[25165824]{0:T(1024)(128)(4,1)}), s8[4194304]{0:T(1024)(128)(4,1)S(1)}, s32[]{:S(2)}) async-start(s8[25165824]{0:T(1024)(128)(4,1)} %bitcast.2), calls=%async_computation.2 | async-start | bytes 8388608
  13.0 5.8 %collective-permute-start.3 = (bf16[40,1536]{1,0:T(8,128)(2,1)S(1)}, bf16[40,1536]{1,0:T(8,128)(2,1)S(1)}, u32[]{:S(2)}, u32[]{:S(2)}) collective-permute-start(bf16[40,1536]{1,0:T(8,128)(2,1)S(1)} %compact.1.rows_ref.refs_0_), channel_id=1, source_target_pairs={{0,1},{1,0},{2,3},{3,2},{4,5},{5,4},{6,7},{7,6},{8,9},{9,8},{10,11... | collective-permute-start | bytes 368648 | tf_op jit(solution)/shard_map/ppermute | solution.py:478
  13.1 6.2 %collective-permute-start.4 = (bf16[40,1536]{1,0:T(8,128)(2,1)S(1)}, bf16[40,1536]{1,0:T(8,128)(2,1)S(1)}, u32[]{:S(2)}, u32[]{:S(2)}) collective-permute-start(bf16[40,1536]{1,0:T(8,128)(2,1)S(1)} %compact.1.rows_ref.refs_0_), channel_id=1, source_target_pairs={{0,2},{1,3},{2,0},{3,1},{4,6},{5,7},{6,4},{7,5},{8,10},{9,11},{10,... | collective-permute-start | bytes 368648 | tf_op jit(solution)/shard_map/ppermute | solution.py:478
  14.6 6.4 %collective-permute-start.5 = (bf16[40,1536]{1,0:T(8,128)(2,1)S(1)}, bf16[40,1536]{1,0:T(8,128)(2,1)S(1)}, u32[]{:S(2)}, u32[]{:S(2)}) collective-permute-start(bf16[40,1536]{1,0:T(8,128)(2,1)S(1)} %compact.1.rows_ref.refs_0_), channel_id=1, source_target_pairs={{0,3},{1,2},{2,1},{3,0},{4,7},{5,6},{6,5},{7,4},{8,11},{9,10},{10,... | collective-permute-start | bytes 368648 | tf_op jit(solution)/shard_map/ppermute | solution.py:478
  15.0 6.1 %slice-start.3 = ((s8[25165824]{0:T(1024)(128)(4,1)}), s8[4194304]{0:T(1024)(128)(4,1)S(1)}, s32[]{:S(2)}) async-start(s8[25165824]{0:T(1024)(128)(4,1)} %bitcast.2), calls=%async_computation.3 | async-start | bytes 8388608
  15.0 6.1 %slice-start.4 = ((s8[25165824]{0:T(1024)(128)(4,1)}), s8[4194304]{0:T(1024)(128)(4,1)S(1)}, s32[]{:S(2)}) async-start(s8[25165824]{0:T(1024)(128)(4,1)} %bitcast.2), calls=%async_computation.4 | async-start | bytes 8388608
  15.0 6.5 %slice-start.5 = ((s8[25165824]{0:T(1024)(128)(4,1)}), s8[4194304]{0:T(1024)(128)(4,1)S(1)}, s32[]{:S(2)}) async-start(s8[25165824]{0:T(1024)(128)(4,1)} %bitcast.2), calls=%async_computation.5 | async-start | bytes 8388608
  33.3 8.0 %collective-permute-start.6 = (bf16[40,1536]{1,0:T(8,128)(2,1)S(1)}, bf16[40,1536]{1,0:T(8,128)(2,1)S(1)}, u32[]{:S(2)}, u32[]{:S(2)}) collective-permute-start(bf16[40,1536]{1,0:T(8,128)(2,1)S(1)} %get-tuple-element.38), channel_id=1, source_target_pairs={{0,3},{1,2},{2,1},{3,0},{4,7},{5,6},{6,5},{7,4},{8,11},{9,10},{10,... | collective-permute-start | bytes 368648 | tf_op jit(solution)/shard_map/ppermute | solution.py:478
  34.8 6.8 %collective-permute-start.7 = (bf16[40,1536]{1,0:T(8,128)(2,1)S(1)}, bf16[40,1536]{1,0:T(8,128)(2,1)S(1)}, u32[]{:S(2)}, u32[]{:S(2)}) collective-permute-start(bf16[40,1536]{1,0:T(8,128)(2,1)S(1)} %get-tuple-element.39), channel_id=1, source_target_pairs={{0,2},{1,3},{2,0},{3,1},{4,6},{5,7},{6,4},{7,5},{8,10},{9,11},{10,... | collective-permute-start | bytes 368648 | tf_op jit(solution)/shard_map/ppermute | solution.py:478
  40.0 1.6 %collective-permute-start.8 = (bf16[40,1536]{1,0:T(8,128)(2,1)S(1)}, bf16[40,1536]{1,0:T(8,128)(2,1)S(1)}, u32[]{:S(2)}, u32[]{:S(2)}) collective-permute-start(bf16[40,1536]{1,0:T(8,128)(2,1)S(1)} %get-tuple-element.40), channel_id=1, source_target_pairs={{0,1},{1,0},{2,3},{3,2},{4,5},{5,4},{6,7},{7,6},{8,9},{9,8},{10,11... | collective-permute-start | bytes 368648 | tf_op jit(solution)/shard_map/ppermute | solution.py:478
  42.0 5.2 %collective-permute-start.10 = (bf16[40,384]{1,0:T(8,128)(2,1)S(1)}, bf16[40,384]{1,0:T(8,128)(2,1)S(1)}, u32[]{:S(2)}, u32[]{:S(2)}) collective-permute-start(bf16[40,384]{1,0:T(8,128)(2,1)S(1)} %get-tuple-element.43), channel_id=1, source_target_pairs={{0,8},{4,12},{8,0},{12,4},{1,9},{5,13},{9,1},{13,5},{2,10},{6,14},... | collective-permute-start | bytes 92168 | tf_op jit(solution)/shard_map/ppermute | solution.py:478
  42.1 5.9 %collective-permute-start.11 = (bf16[40,384]{1,0:T(8,128)(2,1)S(1)}, bf16[40,384]{1,0:T(8,128)(2,1)S(1)}, u32[]{:S(2)}, u32[]{:S(2)}) collective-permute-start(bf16[40,384]{1,0:T(8,128)(2,1)S(1)} %get-tuple-element.44), channel_id=1, source_target_pairs={{0,12},{4,8},{8,4},{12,0},{1,13},{5,9},{9,5},{13,1},{2,14},{6,10},... | collective-permute-start | bytes 92168 | tf_op jit(solution)/shard_map/ppermute | solution.py:478
  43.7 4.2 %collective-permute-start.9 = (bf16[40,384]{1,0:T(8,128)(2,1)S(1)}, bf16[40,384]{1,0:T(8,128)(2,1)S(1)}, u32[]{:S(2)}, u32[]{:S(2)}) collective-permute-start(bf16[40,384]{1,0:T(8,128)(2,1)S(1)} %get-tuple-element.42), channel_id=1, source_target_pairs={{0,4},{4,0},{8,12},{12,8},{1,5},{5,1},{9,13},{13,9},{2,6},{6,2},{1... | collective-permute-start | bytes 92168 | tf_op jit(solution)/shard_map/ppermute | solution.py:478

commit v5 on v4

--- a/solution.py
+++ b/solution.py
@@ -12,7 +12,7 @@
 SLAB = 16
 FETCH = 2
 OWN = 4
-DOWNS = 3
+DOWNS = 4
 TILE = 512
 WIDE = 512
 MICRO = 1_150_000_000
@@ -235,6 +235,25 @@
     )(rows, comb, *held, w_up)
 
 
+def second_kernel(rows_ref, sum_u, up_low, up_high, out_ref):
+    half = rows_ref.shape[1] // 2
+    for tile in tiles(sum_u.shape[1]):
+        part = dot(rows_ref[:, :half], up_low[:, tile]) + dot(rows_ref[:, half:], up_high[:, tile])
+        out_ref[:, tile] = sum_u[:, tile] + part
+
+
+def second(rows, sum_u, held):
+    return pl.pallas_call(
+        second_kernel,
+        out_shape=VMEM(sum_u.shape, jnp.float32),
+        in_specs=[spec(VMEM)] * 4,
+        out_specs=spec(VMEM),
+        compiler_params=limit(2),
+        cost_estimate=lasts(1),
+        name="second",
+    )(rows, sum_u, *held)
+
+
 def down_copy(k, down_hbm, target, sem):
     width = target.shape[1]
     q = lax.axis_index("tensor")
@@ -245,7 +264,7 @@
 def rest_kernel(outs, first, *refs):
     parts = len(outs) + 2
     rows, refs = refs[:parts], refs[parts:]
-    held, refs = refs[: first - 2], refs[first - 2 :]
+    held, refs = refs[: first - 4], refs[first - 4 :]
     start_u, gate_ref, up_hbm, down_hbm, hidden_ref = refs[:5]
     sent, refs = refs[5 : 5 + len(outs)], refs[5 + len(outs) :]
     late, down2, sum_g, late_sems, down_sems = refs
@@ -288,9 +307,9 @@
     def _(step):
         at = pl.ds(pl.multiple_of(step * wide, 128), wide)
         total = start_u[:, at]
-        for k in range(1, parts):
-            total += dot(rows[k][:, :half], ups[2 * k - 2][:, at])
-            total += dot(rows[k][:, half:], ups[2 * k - 1][:, at])
+        for k in range(2, parts):
+            total += dot(rows[k][:, :half], ups[2 * k - 4][:, at])
+            total += dot(rows[k][:, half:], ups[2 * k - 3][:, at])
         gate = sum_g[:, at]
         hidden_ref[:, at] = (gate / (1.0 + jnp.exp(-gate)) * total).astype(jnp.bfloat16)
 
@@ -319,7 +338,7 @@
     m, n = sum_u.shape
     width = rows[0].shape[1]
     cuts = 2 if n % 256 == 0 else 1
-    first = 2 + len(held)
+    first = 4 + len(held)
     late = max(1, 2 * len(rows) - first)
     return pl.pallas_call(
         functools.partial(rest_kernel, outs, first),
@@ -333,7 +352,7 @@
             DMA((late,)),
             DMA((DOWNS,)),
         ],
-        compiler_params=limit(22),
+        compiler_params=limit(26),
         cost_estimate=lasts(10),
         name="rest",
     )(*rows, *held, sum_u, w_gate, w_up, w_down)
@@ -493,6 +512,8 @@
     rows = [mine] + [swap(mine, "tensor", k) for k in range(1, parts)]
     sum_u, mix, *more = own(range(FETCH, OWN), n, mine, comb, held[:2], w_up)
     held = [*held[2:], *more]
+    sum_u = second(rows[1], sum_u, held[:2])
+    held = held[2:]
     far = list(range(parts - 1, 1, -1))
     hidden, *sent = rest(far, rows, held, sum_u, w_gate, w_up, w_down)
     terms = [swap(x, "tensor", k) for k, x in zip(far, sent)]

time: 49.2 us -> 48 us (0.976)
  waiting for transfers between devices: 7.62 us -> 6.39 us
    pallas_call x1, Pallas kernels: 11.8 us -> 10.6 us  [rest(): pl.pallas_call(functools.partial(rest_kernel, outs, first), out_shape=[VM...]
    ppermute x12, waiting for transfers between devices: 7.62 us -> 6.39 us  [swap(): return lax.ppermute(x, axis, [(i, i ^ k) for i in range(size)])]
    pallas_call x0 -> x1, Pallas kernels: none -> 1.21 us  [second(): pl.pallas_call(second_kernel, out_shape=VMEM(sum_u.shape, jnp.float32), i...]
  transfers between devices with their start and end apart: 12 -> 12, of which waited for: 6 -> 5; matrix products, arithmetic and copies ran while one was open for 0% -> 0% of each run, Pallas kernels for 26% -> 29%
where the time goes in v5:
time: 48 us; the launch traced here: 47.8 us
  Pallas kernels  27.5 us (57%)
  starting transfers between devices  13.3 us (28%)
  waiting for transfers between devices  6.39 us (13%)
    ppermute x12, starting transfers between devices, swap(): return lax.ppermute(x, axis, [(i, i ^ k) for i in range(size)])  13.3 us
    pallas_call x1, Pallas kernels, rest(): pl.pallas_call(functools.partial(rest_kernel, outs, first), out_shape=[VM...  10.6 us
    ppermute x12, waiting for transfers between devices, swap(): return lax.ppermute(x, axis, [(i, i ^ k) for i in range(size)])  6.39 us
    pallas_call x1, Pallas kernels, near(): pl.pallas_call(near_kernel, out_shape=[VMEM((m, width), jnp.bfloat16), VM...  4.71 us
    pallas_call x1, Pallas kernels, own(): pl.pallas_call(functools.partial(own_kernel, jobs, axis), out_shape=[VMEM...  3.79 us
    pallas_call x1, Pallas kernels, fetch(): pl.pallas_call(functools.partial(fetch_kernel, jobs, half), out_shape=[VM...  3.01 us
    pallas_call x1, Pallas kernels, select(): pl.pallas_call(functools.partial(select_kernel, n), out_shape=[VMEM((n *...  1.4 us
    pallas_call x1, Pallas kernels, second(): pl.pallas_call(second_kernel, out_shape=VMEM(sum_u.shape, jnp.float32), i...  1.21 us
  transfers between devices with their start and end apart: 12, of which 5 were waited for; matrix products, arithmetic and copies ran while one was open for 0% of the time, Pallas kernels for 29%

profile of v5, /device:TPU:0, one launch (start us, length us, event | category | flops | bytes accessed | tf_op | source)
XLA Modules:
  0.0 47.8 jit_solution(8764334294718349510)
XLA Ops:
  0.0 1.4 %select.1 = (f32[64,80]{1,0:T(8,128)S(1)}, bf16[40,384]{1,0:T(8,128)(2,1)S(1)}, bf16[40,384]{1,0:T(8,128)(2,1)S(1)}, bf16[40,384]{1,0:T(8,128)(2,1)S(1)}, bf16[40,384]{1,0:T(8,128)(2,1)S(1)}) custom-call(s32[4,80]{1,0:T(4,128)} %bitcast.4, f32[4,80]{1,0:T(4,128)} %bitcast.5, bf16[80,1536]{1,0:T(8,128)(2,1)} %tok_hbm.1), custom_call_target="tpu_custom_call" | custom-call | flops 46000001024 | tf_op jit(solution)/shard_map/select/pallas_call | solution.py:118
  1.4 3.1 %collective-permute-start = (bf16[40,384]{1,0:T(8,128)(2,1)S(1)}, bf16[40,384]{1,0:T(8,128)(2,1)S(1)}, u32[]{:S(2)}, u32[]{:S(2)}) collective-permute-start(bf16[40,384]{1,0:T(8,128)(2,1)S(1)} %get-tuple-element.26), channel_id=1, source_target_pairs={{0,4},{4,0},{8,12},{12,8},{1,5},{5,1},{9,13},{13,9},{2,6},{6,2},{1... | collective-permute-start | bytes 92168 | tf_op jit(solution)/shard_map/ppermute | solution.py:497
  4.5 2.6 %collective-permute-start.1 = (bf16[40,384]{1,0:T(8,128)(2,1)S(1)}, bf16[40,384]{1,0:T(8,128)(2,1)S(1)}, u32[]{:S(2)}, u32[]{:S(2)}) collective-permute-start(bf16[40,384]{1,0:T(8,128)(2,1)S(1)} %get-tuple-element.27), channel_id=1, source_target_pairs={{0,8},{4,12},{8,0},{12,4},{1,9},{5,13},{9,1},{13,5},{2,10},{6,14},... | collective-permute-start | bytes 92168 | tf_op jit(solution)/shard_map/ppermute | solution.py:497
  7.1 3.0 %fetch.1 = (bf16[768,2048]{1,0:T(8,128)(2,1)S(1)}, bf16[768,2048]{1,0:T(8,128)(2,1)S(1)}) custom-call(f32[64,80]{1,0:T(8,128)S(1)} %get-tuple-element.29.order_ref.comb_ref, bf16[6144,2048]{1,0:T(8,128)(2,1)} %refs_6_.1), custom_call_target="tpu_custom_call" | custom-call | flops 230000000 | tf_op jit(solution)/shard_map/fetch/pallas_call | solution.py:180
  10.1 2.6 %collective-permute-done.2.refs_3_ = bf16[40,384]{1,0:T(8,128)(2,1)S(1)} collective-permute-done((bf16[40,384]{1,0:T(8,128)(2,1)S(1)}, bf16[40,384]{1,0:T(8,128)(2,1)S(1)}, u32[]{:S(2)}, u32[]{:S(2)}) %collective-permute-start.2) | collective-permute-done | bytes 30752 | tf_op jit(solution)/shard_map/ppermute | solution.py:497
  12.8 0.2 compact.1.rows_ref.refs_0_
  13.1 1.6 %collective-permute-start.4 = (bf16[40,1536]{1,0:T(8,128)(2,1)S(1)}, bf16[40,1536]{1,0:T(8,128)(2,1)S(1)}, u32[]{:S(2)}, u32[]{:S(2)}) collective-permute-start(bf16[40,1536]{1,0:T(8,128)(2,1)S(1)} %compact.1.rows_ref.refs_0_), channel_id=1, source_target_pairs={{0,2},{1,3},{2,0},{3,1},{4,6},{5,7},{6,4},{7,5},{8,10},{9,11},{10,... | collective-permute-start | bytes 368648 | tf_op jit(solution)/shard_map/ppermute | solution.py:497
  14.6 0.3 collective-permute-start.5
  15.0 3.8 %own.1 = (f32[40,2048]{1,0:T(8,128)S(1)}, bf16[3,320,160]{2,1,0:T(8,128)(2,1)S(1)}, bf16[768,2048]{1,0:T(8,128)(2,1)S(1)}, bf16[768,2048]{1,0:T(8,128)(2,1)S(1)}) custom-call(bf16[40,1536]{1,0:T(8,128)(2,1)S(1)} %compact.1.rows_ref.refs_0_, f32[64,80]{1,0:T(8,128)S(1)} %get-tuple-element.29.order_ref.comb_ref, ...), custom_call_target="tpu_custom_call" | custom-call | flops 230000000 | tf_op jit(solution)/shard_map/own/pallas_call | solution.py:225
  18.8 1.2 %second.1.refs_4_ = f32[40,2048]{1,0:T(8,128)S(1)} custom-call(bf16[40,1536]{1,0:T(8,128)(2,1)S(1)} %collective-permute-done.3.rows_ref.refs_1_, f32[40,2048]{1,0:T(8,128)S(1)} %get-tuple-element.33.sum_u, bf16[768,2048]{1,0:T(8,128)(2,1)S(1)} %get-tuple-element.34.up_low, bf16[768,2048]{1,0:T(8,128)(2,1)S(1)} %get-tuple-element.35.up_high), custom_call_target="tpu_custom_call" | custom-call | flops 1150000000 | tf_op jit(solution)/shard_map/second/pallas_call | solution.py:246
  20.0 1.0 %collective-permute-done.5.refs_3_ = bf16[40,1536]{1,0:T(8,128)(2,1)S(1)} collective-permute-done((bf16[40,1536]{1,0:T(8,128)(2,1)S(1)}, bf16[40,1536]{1,0:T(8,128)(2,1)S(1)}, u32[]{:S(2)}, u32[]{:S(2)}) %collective-permute-start.5) | collective-permute-done | bytes 122912 | tf_op jit(solution)/shard_map/ppermute | solution.py:497
  21.0 0.4 slice-done.5
  21.5 10.6 %rest.1 = (bf16[40,2048]{1,0:T(8,128)(2,1)S(1)}, bf16[40,1536]{1,0:T(8,128)(2,1)S(1)}, bf16[40,1536]{1,0:T(8,128)(2,1)S(1)}) custom-call(bf16[40,1536]{1,0:T(8,128)(2,1)S(1)} %compact.1.rows_ref.refs_0_, bf16[40,1536]{1,0:T(8,128)(2,1)S(1)} %collective-permute-done.3.rows_ref.refs_1_, bf16[40,1536]{1,0:T(8,128)(2,1)S(1)} %collective-permute-done.4.refs_2_, ...), custom_call_target="tpu_custom_call" | custom-call | flops 11500000256 | tf_op jit(solution)/shard_map/rest/pallas_call | solution.py:343
  32.0 1.5 %collective-permute-start.6 = (bf16[40,1536]{1,0:T(8,128)(2,1)S(1)}, bf16[40,1536]{1,0:T(8,128)(2,1)S(1)}, u32[]{:S(2)}, u32[]{:S(2)}) collective-permute-start(bf16[40,1536]{1,0:T(8,128)(2,1)S(1)} %get-tuple-element.38), channel_id=1, source_target_pairs={{0,3},{1,2},{2,1},{3,0},{4,7},{5,6},{6,5},{7,4},{8,11},{9,10},{10,... | collective-permute-start | bytes 368648 | tf_op jit(solution)/shard_map/ppermute | solution.py:497
  33.5 0.5 %collective-permute-start.7 = (bf16[40,1536]{1,0:T(8,128)(2,1)S(1)}, bf16[40,1536]{1,0:T(8,128)(2,1)S(1)}, u32[]{:S(2)}, u32[]{:S(2)}) collective-permute-start(bf16[40,1536]{1,0:T(8,128)(2,1)S(1)} %get-tuple-element.39), channel_id=1, source_target_pairs={{0,2},{1,3},{2,0},{3,1},{4,6},{5,7},{6,4},{7,5},{8,10},{9,11},{10,... | collective-permute-start | bytes 368648 | tf_op jit(solution)/shard_map/ppermute | solution.py:497
  34.1 4.7 %near.1 = (bf16[40,1536]{1,0:T(8,128)(2,1)S(1)}, bf16[2048,1536]{1,0:T(8,128)(2,1)S(1)}) custom-call(bf16[40,2048]{1,0:T(8,128)(2,1)S(1)} %get-tuple-element.36.hidden_ref, bf16[2048,6144]{1,0:T(8,128)(2,1)} %down_hbm.1), custom_call_target="tpu_custom_call" | custom-call | flops 4600000000 | tf_op jit(solution)/shard_map/near/pallas_call | solution.py:390
  38.9 1.2 %keep.1.total_ref = f32[40,1536]{1,0:T(8,128)S(1)} custom-call(bf16[40,2048]{1,0:T(8,128)(2,1)S(1)} %get-tuple-element.36.hidden_ref, bf16[2048,1536]{1,0:T(8,128)(2,1)S(1)} %get-tuple-element.37.weight_ref), custom_call_target="tpu_custom_call" | custom-call | flops 1150000000 | tf_op jit(solution)/shard_map/keep/pallas_call | solution.py:412
  40.1 0.3 collective-permute-done.7.refs_1_
  40.4 0.3 add.1
  40.8 1.7 %collective-permute-start.11 = (bf16[40,384]{1,0:T(8,128)(2,1)S(1)}, bf16[40,384]{1,0:T(8,128)(2,1)S(1)}, u32[]{:S(2)}, u32[]{:S(2)}) collective-permute-start(bf16[40,384]{1,0:T(8,128)(2,1)S(1)} %get-tuple-element.44), channel_id=1, source_target_pairs={{0,12},{4,8},{8,4},{12,0},{1,13},{5,9},{9,5},{13,1},{2,14},{6,10},... | collective-permute-start | bytes 92168 | tf_op jit(solution)/shard_map/ppermute | solution.py:497
  42.5 1.8 %collective-permute-start.9 = (bf16[40,384]{1,0:T(8,128)(2,1)S(1)}, bf16[40,384]{1,0:T(8,128)(2,1)S(1)}, u32[]{:S(2)}, u32[]{:S(2)}) collective-permute-start(bf16[40,384]{1,0:T(8,128)(2,1)S(1)} %get-tuple-element.42), channel_id=1, source_target_pairs={{0,4},{4,0},{8,12},{12,8},{1,5},{5,1},{9,13},{13,9},{2,6},{6,2},{1... | collective-permute-start | bytes 92168 | tf_op jit(solution)/shard_map/ppermute | solution.py:497
  44.3 1.3 %collective-permute-done.10.refs_2_ = bf16[40,384]{1,0:T(8,128)(2,1)S(1)} collective-permute-done((bf16[40,384]{1,0:T(8,128)(2,1)S(1)}, bf16[40,384]{1,0:T(8,128)(2,1)S(1)}, u32[]{:S(2)}, u32[]{:S(2)}) %collective-permute-start.10) | collective-permute-done | bytes 30752 | tf_op jit(solution)/shard_map/ppermute | solution.py:497
  45.6 1.1 %collective-permute-done.11.refs_3_ = bf16[40,384]{1,0:T(8,128)(2,1)S(1)} collective-permute-done((bf16[40,384]{1,0:T(8,128)(2,1)S(1)}, bf16[40,384]{1,0:T(8,128)(2,1)S(1)}, u32[]{:S(2)}, u32[]{:S(2)}) %collective-permute-start.11) | collective-permute-done | bytes 30752 | tf_op jit(solution)/shard_map/ppermute | solution.py:497
  46.7 1.1 %combine.1 = bf16[80,1536]{1,0:T(8,128)(2,1)} custom-call(bf16[3,320,160]{2,1,0:T(8,128)(2,1)S(1)} %get-tuple-element.32.mix_ref, bf16[40,384]{1,0:T(8,128)(2,1)S(1)} %get-tuple-element.41.refs_0_, bf16[40,384]{1,0:T(8,128)(2,1)S(1)} %collective-permute-done.9.refs_1_, bf16[40,384]{1,0:T(8,128)(2,1)S(1)} %collective-permute-done.10.refs_2_, ...), custom_call_target="tpu_custom_call" | custom-call | tf_op jit(solution)/shard_map/combine/pallas_call | solution.py:485
  (24 shorter events, 0.3 us)
Async XLA Ops:
  1.4 8.7 %collective-permute-start = (bf16[40,384]{1,0:T(8,128)(2,1)S(1)}, bf16[40,384]{1,0:T(8,128)(2,1)S(1)}, u32[]{:S(2)}, u32[]{:S(2)}) collective-permute-start(bf16[40,384]{1,0:T(8,128)(2,1)S(1)} %get-tuple-element.26), channel_id=1, source_target_pairs={{0,4},{4,0},{8,12},{12,8},{1,5},{5,1},{9,13},{13,9},{2,6},{6,2},{1... | collective-permute-start | bytes 92168 | tf_op jit(solution)/shard_map/ppermute | solution.py:497
  4.5 5.6 %collective-permute-start.1 = (bf16[40,384]{1,0:T(8,128)(2,1)S(1)}, bf16[40,384]{1,0:T(8,128)(2,1)S(1)}, u32[]{:S(2)}, u32[]{:S(2)}) collective-permute-start(bf16[40,384]{1,0:T(8,128)(2,1)S(1)} %get-tuple-element.27), channel_id=1, source_target_pairs={{0,8},{4,12},{8,0},{12,4},{1,9},{5,13},{9,1},{13,5},{2,10},{6,14},... | collective-permute-start | bytes 92168 | tf_op jit(solution)/shard_map/ppermute | solution.py:497
  7.1 5.7 %collective-permute-start.2 = (bf16[40,384]{1,0:T(8,128)(2,1)S(1)}, bf16[40,384]{1,0:T(8,128)(2,1)S(1)}, u32[]{:S(2)}, u32[]{:S(2)}) collective-permute-start(bf16[40,384]{1,0:T(8,128)(2,1)S(1)} %get-tuple-element.28), channel_id=1, source_target_pairs={{0,12},{4,8},{8,4},{12,0},{1,13},{5,9},{9,5},{13,1},{2,14},{6,10},... | collective-permute-start | bytes 92168 | tf_op jit(solution)/shard_map/ppermute | solution.py:497
  7.1 13.9 %slice-start = ((s8[25165824]{0:T(1024)(128)(4,1)}), s8[4194304]{0:T(1024)(128)(4,1)S(1)}, s32[]{:S(2)}) async-start(s8[25165824]{0:T(1024)(128)(4,1)} %bitcast.2), calls=%async_computation | async-start | bytes 8388608
  7.1 13.9 %slice-start.1 = ((s8[25165824]{0:T(1024)(128)(4,1)}), s8[4194304]{0:T(1024)(128)(4,1)S(1)}, s32[]{:S(2)}) async-start(s8[25165824]{0:T(1024)(128)(4,1)} %bitcast.2), calls=%async_computation.1 | async-start | bytes 8388608
  7.1 13.9 %slice-start.2 = ((s8[25165824]{0:T(1024)(128)(4,1)}), s8[4194304]{0:T(1024)(128)(4,1)S(1)}, s32[]{:S(2)}) async-start(s8[25165824]{0:T(1024)(128)(4,1)} %bitcast.2), calls=%async_computation.2 | async-start | bytes 8388608
  13.0 5.8 %collective-permute-start.3 = (bf16[40,1536]{1,0:T(8,128)(2,1)S(1)}, bf16[40,1536]{1,0:T(8,128)(2,1)S(1)}, u32[]{:S(2)}, u32[]{:S(2)}) collective-permute-start(bf16[40,1536]{1,0:T(8,128)(2,1)S(1)} %compact.1.rows_ref.refs_0_), channel_id=1, source_target_pairs={{0,1},{1,0},{2,3},{3,2},{4,5},{5,4},{6,7},{7,6},{8,9},{9,8},{10,11... | collective-permute-start | bytes 368648 | tf_op jit(solution)/shard_map/ppermute | solution.py:497
  13.1 6.9 %collective-permute-start.4 = (bf16[40,1536]{1,0:T(8,128)(2,1)S(1)}, bf16[40,1536]{1,0:T(8,128)(2,1)S(1)}, u32[]{:S(2)}, u32[]{:S(2)}) collective-permute-start(bf16[40,1536]{1,0:T(8,128)(2,1)S(1)} %compact.1.rows_ref.refs_0_), channel_id=1, source_target_pairs={{0,2},{1,3},{2,0},{3,1},{4,6},{5,7},{6,4},{7,5},{8,10},{9,11},{10,... | collective-permute-start | bytes 368648 | tf_op jit(solution)/shard_map/ppermute | solution.py:497
  14.6 6.4 %collective-permute-start.5 = (bf16[40,1536]{1,0:T(8,128)(2,1)S(1)}, bf16[40,1536]{1,0:T(8,128)(2,1)S(1)}, u32[]{:S(2)}, u32[]{:S(2)}) collective-permute-start(bf16[40,1536]{1,0:T(8,128)(2,1)S(1)} %compact.1.rows_ref.refs_0_), channel_id=1, source_target_pairs={{0,3},{1,2},{2,1},{3,0},{4,7},{5,6},{6,5},{7,4},{8,11},{9,10},{10,... | collective-permute-start | bytes 368648 | tf_op jit(solution)/shard_map/ppermute | solution.py:497
  14.9 6.1 %slice-start.3 = ((s8[25165824]{0:T(1024)(128)(4,1)}), s8[4194304]{0:T(1024)(128)(4,1)S(1)}, s32[]{:S(2)}) async-start(s8[25165824]{0:T(1024)(128)(4,1)} %bitcast.2), calls=%async_computation.3 | async-start | bytes 8388608
  15.0 6.1 %slice-start.4 = ((s8[25165824]{0:T(1024)(128)(4,1)}), s8[4194304]{0:T(1024)(128)(4,1)S(1)}, s32[]{:S(2)}) async-start(s8[25165824]{0:T(1024)(128)(4,1)} %bitcast.2), calls=%async_computation.4 | async-start | bytes 8388608
  15.0 6.5 %slice-start.5 = ((s8[25165824]{0:T(1024)(128)(4,1)}), s8[4194304]{0:T(1024)(128)(4,1)S(1)}, s32[]{:S(2)}) async-start(s8[25165824]{0:T(1024)(128)(4,1)} %bitcast.2), calls=%async_computation.5 | async-start | bytes 8388608
  32.0 8.0 %collective-permute-start.6 = (bf16[40,1536]{1,0:T(8,128)(2,1)S(1)}, bf16[40,1536]{1,0:T(8,128)(2,1)S(1)}, u32[]{:S(2)}, u32[]{:S(2)}) collective-permute-start(bf16[40,1536]{1,0:T(8,128)(2,1)S(1)} %get-tuple-element.38), channel_id=1, source_target_pairs={{0,3},{1,2},{2,1},{3,0},{4,7},{5,6},{6,5},{7,4},{8,11},{9,10},{10,... | collective-permute-start | bytes 368648 | tf_op jit(solution)/shard_map/ppermute | solution.py:497
  33.5 6.8 %collective-permute-start.7 = (bf16[40,1536]{1,0:T(8,128)(2,1)S(1)}, bf16[40,1536]{1,0:T(8,128)(2,1)S(1)}, u32[]{:S(2)}, u32[]{:S(2)}) collective-permute-start(bf16[40,1536]{1,0:T(8,128)(2,1)S(1)} %get-tuple-element.39), channel_id=1, source_target_pairs={{0,2},{1,3},{2,0},{3,1},{4,6},{5,7},{6,4},{7,5},{8,10},{9,11},{10,... | collective-permute-start | bytes 368648 | tf_op jit(solution)/shard_map/ppermute | solution.py:497
  38.8 1.6 %collective-permute-start.8 = (bf16[40,1536]{1,0:T(8,128)(2,1)S(1)}, bf16[40,1536]{1,0:T(8,128)(2,1)S(1)}, u32[]{:S(2)}, u32[]{:S(2)}) collective-permute-start(bf16[40,1536]{1,0:T(8,128)(2,1)S(1)} %get-tuple-element.40), channel_id=1, source_target_pairs={{0,1},{1,0},{2,3},{3,2},{4,5},{5,4},{6,7},{7,6},{8,9},{9,8},{10,11... | collective-permute-start | bytes 368648 | tf_op jit(solution)/shard_map/ppermute | solution.py:497
  40.7 4.9 %collective-permute-start.10 = (bf16[40,384]{1,0:T(8,128)(2,1)S(1)}, bf16[40,384]{1,0:T(8,128)(2,1)S(1)}, u32[]{:S(2)}, u32[]{:S(2)}) collective-permute-start(bf16[40,384]{1,0:T(8,128)(2,1)S(1)} %get-tuple-element.43), channel_id=1, source_target_pairs={{0,8},{4,12},{8,0},{12,4},{1,9},{5,13},{9,1},{13,5},{2,10},{6,14},... | collective-permute-start | bytes 92168 | tf_op jit(solution)/shard_map/ppermute | solution.py:497
  40.8 5.9 %collective-permute-start.11 = (bf16[40,384]{1,0:T(8,128)(2,1)S(1)}, bf16[40,384]{1,0:T(8,128)(2,1)S(1)}, u32[]{:S(2)}, u32[]{:S(2)}) collective-permute-start(bf16[40,384]{1,0:T(8,128)(2,1)S(1)} %get-tuple-element.44), channel_id=1, source_target_pairs={{0,12},{4,8},{8,4},{12,0},{1,13},{5,9},{9,5},{13,1},{2,14},{6,10},... | collective-permute-start | bytes 92168 | tf_op jit(solution)/shard_map/ppermute | solution.py:497
  42.5 4.2 %collective-permute-start.9 = (bf16[40,384]{1,0:T(8,128)(2,1)S(1)}, bf16[40,384]{1,0:T(8,128)(2,1)S(1)}, u32[]{:S(2)}, u32[]{:S(2)}) collective-permute-start(bf16[40,384]{1,0:T(8,128)(2,1)S(1)} %get-tuple-element.42), channel_id=1, source_target_pairs={{0,4},{4,0},{8,12},{12,8},{1,5},{5,1},{9,13},{13,9},{2,6},{6,2},{1... | collective-permute-start | bytes 92168 | tf_op jit(solution)/shard_map/ppermute | solution.py:497

commit v6 on v5

--- a/solution.py
+++ b/solution.py
@@ -12,7 +12,7 @@
 SLAB = 16
 FETCH = 2
 OWN = 4
-DOWNS = 4
+DOWNS = 2
 TILE = 512
 WIDE = 512
 MICRO = 1_150_000_000
@@ -53,6 +53,10 @@
 def pieces(width):
     size = width // folds(width)
     return [(p, slice(p * size, (p + 1) * size)) for p in range(folds(width))]
+
+
+def order(n):
+    return [0, *range(2, n), 1]
 
 
 def iota(shape, dim):
@@ -262,12 +266,12 @@
 
 
 def rest_kernel(outs, first, *refs):
-    parts = len(outs) + 2
+    parts = len(outs) + 3
     rows, refs = refs[:parts], refs[parts:]
     held, refs = refs[: first - 4], refs[first - 4 :]
-    start_u, gate_ref, up_hbm, down_hbm, hidden_ref = refs[:5]
-    sent, refs = refs[5 : 5 + len(outs)], refs[5 + len(outs) :]
-    late, down2, sum_g, late_sems, down_sems = refs
+    start_u, gate_ref, up_hbm, down_hbm, hidden_ref, next_ref = refs[:6]
+    sent, refs = refs[6 : 6 + len(outs)], refs[6 + len(outs) :]
+    late, down2, sum_g, late_sems, down_sems, next_sem = refs
     width = rows[0].shape[1]
     half = width // 2
     slots, deep = down2.shape[:2]
@@ -297,7 +301,8 @@
 
     middle = n // wide // 2
     pl.loop(0, middle)(gate_part)
-    for copy in downs[:slots]:
+    after = down_copy(2, down_hbm, next_ref, next_sem)
+    for copy in [*downs[:slots], after]:
         copy.start()
     pl.loop(middle, n // wide)(gate_part)
     for copy in lates:
@@ -332,6 +337,7 @@
 
             if piece + slots < len(downs):
                 downs[piece + slots].start()
+    after.wait()
 
 
 def rest(outs, rows, held, sum_u, w_gate, w_up, w_down):
@@ -342,82 +348,70 @@
     late = max(1, 2 * len(rows) - first)
     return pl.pallas_call(
         functools.partial(rest_kernel, outs, first),
-        out_shape=[VMEM((m, n), jnp.bfloat16)] + [VMEM((m, width), jnp.bfloat16)] * len(outs),
+        out_shape=[VMEM((m, n), jnp.bfloat16), VMEM((n, width), jnp.bfloat16)]
+        + [VMEM((m, width), jnp.bfloat16)] * len(outs),
         in_specs=[spec(VMEM)] * (len(rows) + len(held) + 2) + [spec(HBM)] * 2,
-        out_specs=[spec(VMEM)] * (1 + len(outs)),
+        out_specs=[spec(VMEM)] * (2 + len(outs)),
         scratch_shapes=[
             VMEM((late, width // 2, n), jnp.bfloat16),
             VMEM((DOWNS, n // cuts, width), jnp.bfloat16),
             VMEM((m, max(n, width)), jnp.float32),
             DMA((late,)),
             DMA((DOWNS,)),
+            DMA,
         ],
-        compiler_params=limit(26),
+        compiler_params=limit(20),
         cost_estimate=lasts(10),
         name="rest",
     )(*rows, *held, sum_u, w_gate, w_up, w_down)
 
 
-def near_kernel(hidden_ref, down_hbm, sent, next_ref, buf, total, sems):
-    cuts, deep = buf.shape[:2]
-    copies = []
-    for j in range(cuts):
-        rows_at = down_hbm.at[pl.ds(j * deep, deep), :]
-        copies.append(down_copy(1, rows_at, buf.at[j], sems.at[j]))
-    for j in range(cuts):
-        at = pl.ds(j * deep, deep)
-        copies.append(down_copy(0, down_hbm.at[at, :], next_ref.at[at, :], sems.at[cuts + j]))
-    for copy in copies:
-        copy.start()
-    for j in range(cuts):
-        copies[j].wait()
-        mid = hidden_ref[:, j * deep : (j + 1) * deep]
-        for tile in tiles(sent.shape[1]):
-            part = dot(mid, buf[j, :, tile])
-            if j > 0:
-                part += total[:, tile]
-            if j < cuts - 1:
-                total[:, tile] = part
-            else:
-                sent[:, tile] = part.astype(jnp.bfloat16)
-    for copy in copies[cuts:]:
-        copy.wait()
-
-
-def near(width, hidden, w_down):
-    m, n = hidden.shape
-    cuts = 2 if n % 256 == 0 else 1
-    return pl.pallas_call(
-        near_kernel,
-        out_shape=[VMEM((m, width), jnp.bfloat16), VMEM((n, width), jnp.bfloat16)],
-        in_specs=[spec(VMEM), spec(HBM)],
+def pass_kernel(k, hidden_ref, weight_ref, down_hbm, sent, next_ref, sem):
+    copy = down_copy(k, down_hbm, next_ref, sem)
+    copy.start()
+    half = sent.shape[1] // 2
+
+    @pl.loop(0, 2)
+    def _(step):
+        at = pl.ds(pl.multiple_of(step * half, 128), half)
+        sent[:, at] = dot(hidden_ref[...], weight_ref[:, at]).astype(jnp.bfloat16)
+
+    copy.wait()
+
+
+def pass_on(k, hidden, weight, w_down):
+    shape = (hidden.shape[0], weight.shape[1])
+    return pl.pallas_call(
+        functools.partial(pass_kernel, k),
+        out_shape=[VMEM(shape, jnp.bfloat16), VMEM(weight.shape, jnp.bfloat16)],
+        in_specs=[spec(VMEM)] * 2 + [spec(HBM)],
         out_specs=[spec(VMEM)] * 2,
-        scratch_shapes=[
-            VMEM((cuts, n // cuts, width), jnp.bfloat16),
-            VMEM((m, width), jnp.float32),
-            DMA((2 * cuts,)),
-        ],
-        compiler_params=limit(12),
-        cost_estimate=lasts(4),
-        name="near",
-    )(hidden, w_down)
-
-
-def keep_kernel(hidden_ref, weight_ref, total_ref):
-    total_ref[...] = dot(hidden_ref[...], weight_ref[...])
-
-
-def keep(hidden, weight):
+        scratch_shapes=[DMA],
+        compiler_params=limit(8),
+        cost_estimate=lasts(3),
+        name="pass_on",
+    )(hidden, weight, w_down)
+
+
+def keep_kernel(hidden_ref, weight_ref, *refs):
+    terms, total_ref = refs[:-1], refs[-1]
+    total = dot(hidden_ref[...], weight_ref[...])
+    for term in terms:
+        total = total + term[...].astype(jnp.float32)
+    total_ref[...] = total
+
+
+def keep(hidden, weight, terms):
     m, width = hidden.shape[0], weight.shape[1]
     return pl.pallas_call(
         keep_kernel,
         out_shape=VMEM((m, width), jnp.float32),
-        in_specs=[spec(VMEM)] * 2,
+        in_specs=[spec(VMEM)] * (2 + len(terms)),
         out_specs=spec(VMEM),
         compiler_params=limit(4),
         cost_estimate=lasts(1),
         name="keep",
-    )(hidden, weight)
+    )(hidden, weight, *terms)
 
 
 def gather_kernel(total_ref, *refs):
@@ -455,8 +449,8 @@
         take = (col == row // tall * SLOT + s) & (s >= 0) & (s < SLOT)
         part = dot(take.astype(jnp.bfloat16), total[:, piece])
         full = part if full is None else full + part
-    for k in range(n):
-        slabs[k][...] = full[k * tall : (k + 1) * tall].astype(jnp.bfloat16)
+    for slab, k in zip(slabs, order(n)):
+        slab[...] = full[k * tall : (k + 1) * tall].astype(jnp.bfloat16)
 
 
 def add(n, total, terms):
@@ -473,7 +467,7 @@
 
 def combine_kernel(mix_ref, *refs):
     slabs, out_ref = refs[:-1], refs[-1]
-    full = stack(slabs)
+    full = stack([slab for _, slab in sorted(zip(order(len(slabs)), slabs), key=lambda x: x[0])])
     count, width = out_ref.shape
     total = dot(mix_ref[0], full) + (dot(mix_ref[1], full) + dot(mix_ref[2], full))
     for p, piece in pieces(width):
@@ -514,14 +508,16 @@
     held = [*held[2:], *more]
     sum_u = second(rows[1], sum_u, held[:2])
     held = held[2:]
-    far = list(range(parts - 1, 1, -1))
-    hidden, *sent = rest(far, rows, held, sum_u, w_gate, w_up, w_down)
+    far = list(range(parts - 1, 2, -1))
+    hidden, weight, *sent = rest(far, rows, held, sum_u, w_gate, w_up, w_down)
     terms = [swap(x, "tensor", k) for k, x in zip(far, sent)]
-    sent, weight0 = near(width, hidden, w_down)
+    sent, weight = pass_on(1, hidden, weight, w_down)
+    late = swap(sent, "tensor", 2)
+    sent, weight = pass_on(0, hidden, weight, w_down)
     last = swap(sent, "tensor", 1)
-    total = gather(keep(hidden, weight0), terms)
+    total = gather(keep(hidden, weight, terms), [late])
     back = add(n, total, [last])
-    back = [back[0]] + [swap(back[k], "expert", k) for k in range(1, n)]
+    back = [swap(x, "expert", k) if k else x for k, x in zip(order(n), back)]
     return combine(width, mix, back)
 
 

time: 48 us -> 47.9 us (level)
  Pallas kernels: 27.5 us -> 26.8 us
  waiting for transfers between devices: 6.39 us -> 6.87 us
    pallas_call x1, Pallas kernels: 10.6 us -> 8.99 us  [rest(): pl.pallas_call(functools.partial(rest_kernel, outs, first), out_shape=[VM...]
    pallas_call x1 -> x2, Pallas kernels: 4.71 us -> 5.58 us  [pass_on(): pl.pallas_call(functools.partial(pass_kernel, k), out_shape=[VMEM(shape,...]
  transfers between devices with their start and end apart: 12 -> 12, of which waited for: 5 -> 5; matrix products, arithmetic and copies ran while one was open for 0% -> 0% of each run, Pallas kernels for 29% -> 31%
where the time goes in v6:
time: 47.9 us; the launch traced here: 47.7 us
  Pallas kernels  26.8 us (56%)
  starting transfers between devices  13.3 us (28%)
  waiting for transfers between devices  6.87 us (14%)
    ppermute x12, starting transfers between devices, swap(): return lax.ppermute(x, axis, [(i, i ^ k) for i in range(size)])  13.3 us
    pallas_call x1, Pallas kernels, rest(): pl.pallas_call(functools.partial(rest_kernel, outs, first), out_shape=[VM...  8.99 us
    ppermute x12, waiting for transfers between devices, swap(): return lax.ppermute(x, axis, [(i, i ^ k) for i in range(size)])  6.87 us
    pallas_call x2, Pallas kernels, pass_on(): pl.pallas_call(functools.partial(pass_kernel, k), out_shape=[VMEM(shape,...  5.58 us
    pallas_call x1, Pallas kernels, own(): pl.pallas_call(functools.partial(own_kernel, jobs, axis), out_shape=[VMEM...  3.79 us
    pallas_call x1, Pallas kernels, fetch(): pl.pallas_call(functools.partial(fetch_kernel, jobs, half), out_shape=[VM...  3.01 us
    pallas_call x1, Pallas kernels, select(): pl.pallas_call(functools.partial(select_kernel, n), out_shape=[VMEM((n *...  1.4 us
    pallas_call x1, Pallas kernels, second(): pl.pallas_call(second_kernel, out_shape=VMEM(sum_u.shape, jnp.float32), i...  1.21 us
  transfers between devices with their start and end apart: 12, of which 5 were waited for; matrix products, arithmetic and copies ran while one was open for 0% of the time, Pallas kernels for 31%

profile of v6, /device:TPU:0, one launch (start us, length us, event | category | flops | bytes accessed | tf_op | source)
XLA Modules:
  0.0 47.7 jit_solution(13040499888019997158)
XLA Ops:
  0.0 1.4 %select.1 = (f32[64,80]{1,0:T(8,128)S(1)}, bf16[40,384]{1,0:T(8,128)(2,1)S(1)}, bf16[40,384]{1,0:T(8,128)(2,1)S(1)}, bf16[40,384]{1,0:T(8,128)(2,1)S(1)}, bf16[40,384]{1,0:T(8,128)(2,1)S(1)}) custom-call(s32[4,80]{1,0:T(4,128)} %bitcast.4, f32[4,80]{1,0:T(4,128)} %bitcast.5, bf16[80,1536]{1,0:T(8,128)(2,1)} %tok_hbm.1), custom_call_target="tpu_custom_call" | custom-call | flops 46000001024 | tf_op jit(solution)/shard_map/select/pallas_call | solution.py:122
  1.4 3.1 %collective-permute-start = (bf16[40,384]{1,0:T(8,128)(2,1)S(1)}, bf16[40,384]{1,0:T(8,128)(2,1)S(1)}, u32[]{:S(2)}, u32[]{:S(2)}) collective-permute-start(bf16[40,384]{1,0:T(8,128)(2,1)S(1)} %get-tuple-element.28), channel_id=1, source_target_pairs={{0,4},{4,0},{8,12},{12,8},{1,5},{5,1},{9,13},{13,9},{2,6},{6,2},{1... | collective-permute-start | bytes 92168 | tf_op jit(solution)/shard_map/ppermute | solution.py:491
  4.5 2.6 %collective-permute-start.1 = (bf16[40,384]{1,0:T(8,128)(2,1)S(1)}, bf16[40,384]{1,0:T(8,128)(2,1)S(1)}, u32[]{:S(2)}, u32[]{:S(2)}) collective-permute-start(bf16[40,384]{1,0:T(8,128)(2,1)S(1)} %get-tuple-element.29), channel_id=1, source_target_pairs={{0,8},{4,12},{8,0},{12,4},{1,9},{5,13},{9,1},{13,5},{2,10},{6,14},... | collective-permute-start | bytes 92168 | tf_op jit(solution)/shard_map/ppermute | solution.py:491
  7.1 3.0 %fetch.1 = (bf16[768,2048]{1,0:T(8,128)(2,1)S(1)}, bf16[768,2048]{1,0:T(8,128)(2,1)S(1)}) custom-call(f32[64,80]{1,0:T(8,128)S(1)} %get-tuple-element.31.order_ref.comb_ref, bf16[6144,2048]{1,0:T(8,128)(2,1)} %refs_6_.1), custom_call_target="tpu_custom_call" | custom-call | flops 230000000 | tf_op jit(solution)/shard_map/fetch/pallas_call | solution.py:184
  10.1 2.6 %collective-permute-done.2.refs_3_ = bf16[40,384]{1,0:T(8,128)(2,1)S(1)} collective-permute-done((bf16[40,384]{1,0:T(8,128)(2,1)S(1)}, bf16[40,384]{1,0:T(8,128)(2,1)S(1)}, u32[]{:S(2)}, u32[]{:S(2)}) %collective-permute-start.2) | collective-permute-done | bytes 30752 | tf_op jit(solution)/shard_map/ppermute | solution.py:491
  13.1 1.6 %collective-permute-start.4 = (bf16[40,1536]{1,0:T(8,128)(2,1)S(1)}, bf16[40,1536]{1,0:T(8,128)(2,1)S(1)}, u32[]{:S(2)}, u32[]{:S(2)}) collective-permute-start(bf16[40,1536]{1,0:T(8,128)(2,1)S(1)} %compact.1.rows_ref.refs_0_), channel_id=1, source_target_pairs={{0,2},{1,3},{2,0},{3,1},{4,6},{5,7},{6,4},{7,5},{8,10},{9,11},{10,... | collective-permute-start | bytes 368648 | tf_op jit(solution)/shard_map/ppermute | solution.py:491
  14.6 0.3 collective-permute-start.5
  15.0 3.8 %own.1 = (f32[40,2048]{1,0:T(8,128)S(1)}, bf16[3,320,160]{2,1,0:T(8,128)(2,1)S(1)}, bf16[768,2048]{1,0:T(8,128)(2,1)S(1)}, bf16[768,2048]{1,0:T(8,128)(2,1)S(1)}) custom-call(bf16[40,1536]{1,0:T(8,128)(2,1)S(1)} %compact.1.rows_ref.refs_0_, f32[64,80]{1,0:T(8,128)S(1)} %get-tuple-element.31.order_ref.comb_ref, ...), custom_call_target="tpu_custom_call" | custom-call | flops 230000000 | tf_op jit(solution)/shard_map/own/pallas_call | solution.py:229
  18.8 1.2 %second.1.refs_4_ = f32[40,2048]{1,0:T(8,128)S(1)} custom-call(bf16[40,1536]{1,0:T(8,128)(2,1)S(1)} %collective-permute-done.3.rows_ref.refs_1_, f32[40,2048]{1,0:T(8,128)S(1)} %get-tuple-element.35.sum_u, bf16[768,2048]{1,0:T(8,128)(2,1)S(1)} %get-tuple-element.36.up_low, bf16[768,2048]{1,0:T(8,128)(2,1)S(1)} %get-tuple-element.37.up_high), custom_call_target="tpu_custom_call" | custom-call | flops 1150000000 | tf_op jit(solution)/shard_map/second/pallas_call | solution.py:250
  20.0 1.0 %collective-permute-done.5.refs_3_ = bf16[40,1536]{1,0:T(8,128)(2,1)S(1)} collective-permute-done((bf16[40,1536]{1,0:T(8,128)(2,1)S(1)}, bf16[40,1536]{1,0:T(8,128)(2,1)S(1)}, u32[]{:S(2)}, u32[]{:S(2)}) %collective-permute-start.5) | collective-permute-done | bytes 122912 | tf_op jit(solution)/shard_map/ppermute | solution.py:491
  21.0 0.4 slice-done.5
  21.5 9.0 %rest.1 = (bf16[40,2048]{1,0:T(8,128)(2,1)S(1)}, bf16[2048,1536]{1,0:T(8,128)(2,1)S(1)}, bf16[40,1536]{1,0:T(8,128)(2,1)S(1)}) custom-call(bf16[40,1536]{1,0:T(8,128)(2,1)S(1)} %compact.1.rows_ref.refs_0_, bf16[40,1536]{1,0:T(8,128)(2,1)S(1)} %collective-permute-done.3.rows_ref.refs_1_, bf16[40,1536]{1,0:T(8,128)(2,1)S(1)} %collective-permute-done.4.refs_2_, ...), custom_call_target="tpu_custom_call" | custom-call | flops 11500000256 | tf_op jit(solution)/shard_map/rest/pallas_call | solution.py:349
  30.5 1.5 %collective-permute-start.6 = (bf16[40,1536]{1,0:T(8,128)(2,1)S(1)}, bf16[40,1536]{1,0:T(8,128)(2,1)S(1)}, u32[]{:S(2)}, u32[]{:S(2)}) collective-permute-start(bf16[40,1536]{1,0:T(8,128)(2,1)S(1)} %get-tuple-element.42), channel_id=1, source_target_pairs={{0,3},{1,2},{2,1},{3,0},{4,7},{5,6},{6,5},{7,4},{8,11},{9,10},{10,... | collective-permute-start | bytes 368648 | tf_op jit(solution)/shard_map/ppermute | solution.py:491
  32.0 2.8 %pass_on.2 = (bf16[40,1536]{1,0:T(8,128)(2,1)S(1)}, bf16[2048,1536]{1,0:T(8,128)(2,1)S(1)}) custom-call(bf16[40,2048]{1,0:T(8,128)(2,1)S(1)} %get-tuple-element.38.hidden_ref, bf16[2048,1536]{1,0:T(8,128)(2,1)S(1)} %get-tuple-element.39.weight_ref, bf16[2048,6144]{1,0:T(8,128)(2,1)} %down_hbm.3), custom_call_target="tpu_custom_call" | custom-call | flops 3449999872 | tf_op jit(solution)/shard_map/pass_on/pallas_call | solution.py:384
  34.8 0.6 %collective-permute-start.7 = (bf16[40,1536]{1,0:T(8,128)(2,1)S(1)}, bf16[40,1536]{1,0:T(8,128)(2,1)S(1)}, u32[]{:S(2)}, u32[]{:S(2)}) collective-permute-start(bf16[40,1536]{1,0:T(8,128)(2,1)S(1)} %get-tuple-element.43), channel_id=1, source_target_pairs={{0,2},{1,3},{2,0},{3,1},{4,6},{5,7},{6,4},{7,5},{8,10},{9,11},{10,... | collective-permute-start | bytes 368648 | tf_op jit(solution)/shard_map/ppermute | solution.py:491
  35.4 2.8 %pass_on.3 = (bf16[40,1536]{1,0:T(8,128)(2,1)S(1)}, bf16[2048,1536]{1,0:T(8,128)(2,1)S(1)}) custom-call(bf16[40,2048]{1,0:T(8,128)(2,1)S(1)} %get-tuple-element.38.hidden_ref, bf16[2048,1536]{1,0:T(8,128)(2,1)S(1)} %get-tuple-element.40.weight_ref, bf16[2048,6144]{1,0:T(8,128)(2,1)} %down_hbm.3), custom_call_target="tpu_custom_call" | custom-call | flops 3449999872 | tf_op jit(solution)/shard_map/pass_on/pallas_call | solution.py:384
  38.3 1.2 %keep.1.total_ref = f32[40,1536]{1,0:T(8,128)S(1)} custom-call(bf16[40,2048]{1,0:T(8,128)(2,1)S(1)} %get-tuple-element.38.hidden_ref, bf16[2048,1536]{1,0:T(8,128)(2,1)S(1)} %get-tuple-element.41.weight_ref, bf16[40,1536]{1,0:T(8,128)(2,1)S(1)} %collective-permute-done.6.refs_0_), custom_call_target="tpu_custom_call" | custom-call | flops 1150000000 | tf_op jit(solution)/shard_map/keep/pallas_call | solution.py:406
  39.4 0.8 %collective-permute-done.7.refs_0_ = bf16[40,1536]{1,0:T(8,128)(2,1)S(1)} collective-permute-done((bf16[40,1536]{1,0:T(8,128)(2,1)S(1)}, bf16[40,1536]{1,0:T(8,128)(2,1)S(1)}, u32[]{:S(2)}, u32[]{:S(2)}) %collective-permute-start.7) | collective-permute-done | bytes 122912 | tf_op jit(solution)/shard_map/ppermute | solution.py:491
  40.3 0.3 add.1
  40.7 1.7 %collective-permute-start.10 = (bf16[40,384]{1,0:T(8,128)(2,1)S(1)}, bf16[40,384]{1,0:T(8,128)(2,1)S(1)}, u32[]{:S(2)}, u32[]{:S(2)}) collective-permute-start(bf16[40,384]{1,0:T(8,128)(2,1)S(1)} %get-tuple-element.47), channel_id=1, source_target_pairs={{0,12},{4,8},{8,4},{12,0},{1,13},{5,9},{9,5},{13,1},{2,14},{6,10},... | collective-permute-start | bytes 92168 | tf_op jit(solution)/shard_map/ppermute | solution.py:491
  42.3 1.8 %collective-permute-start.11 = (bf16[40,384]{1,0:T(8,128)(2,1)S(1)}, bf16[40,384]{1,0:T(8,128)(2,1)S(1)}, u32[]{:S(2)}, u32[]{:S(2)}) collective-permute-start(bf16[40,384]{1,0:T(8,128)(2,1)S(1)} %get-tuple-element.48), channel_id=1, source_target_pairs={{0,4},{4,0},{8,12},{12,8},{1,5},{5,1},{9,13},{13,9},{2,6},{6,2},{1... | collective-permute-start | bytes 92168 | tf_op jit(solution)/shard_map/ppermute | solution.py:491
  44.2 1.3 %collective-permute-done.9.refs_1_ = bf16[40,384]{1,0:T(8,128)(2,1)S(1)} collective-permute-done((bf16[40,384]{1,0:T(8,128)(2,1)S(1)}, bf16[40,384]{1,0:T(8,128)(2,1)S(1)}, u32[]{:S(2)}, u32[]{:S(2)}) %collective-permute-start.9) | collective-permute-done | bytes 30752 | tf_op jit(solution)/shard_map/ppermute | solution.py:491
  45.5 1.0 %collective-permute-done.10.refs_2_ = bf16[40,384]{1,0:T(8,128)(2,1)S(1)} collective-permute-done((bf16[40,384]{1,0:T(8,128)(2,1)S(1)}, bf16[40,384]{1,0:T(8,128)(2,1)S(1)}, u32[]{:S(2)}, u32[]{:S(2)}) %collective-permute-start.10) | collective-permute-done | bytes 30752 | tf_op jit(solution)/shard_map/ppermute | solution.py:491
  46.6 1.1 %combine.1 = bf16[80,1536]{1,0:T(8,128)(2,1)} custom-call(bf16[3,320,160]{2,1,0:T(8,128)(2,1)S(1)} %get-tuple-element.34.mix_ref, bf16[40,384]{1,0:T(8,128)(2,1)S(1)} %get-tuple-element.45.refs_0_, bf16[40,384]{1,0:T(8,128)(2,1)S(1)} %collective-permute-done.9.refs_1_, bf16[40,384]{1,0:T(8,128)(2,1)S(1)} %collective-permute-done.10.refs_2_, ...), custom_call_target="tpu_custom_call" | custom-call | tf_op jit(solution)/shard_map/combine/pallas_call | solution.py:479
  (25 shorter events, 0.5 us)
Async XLA Ops:
  1.4 8.7 %collective-permute-start = (bf16[40,384]{1,0:T(8,128)(2,1)S(1)}, bf16[40,384]{1,0:T(8,128)(2,1)S(1)}, u32[]{:S(2)}, u32[]{:S(2)}) collective-permute-start(bf16[40,384]{1,0:T(8,128)(2,1)S(1)} %get-tuple-element.28), channel_id=1, source_target_pairs={{0,4},{4,0},{8,12},{12,8},{1,5},{5,1},{9,13},{13,9},{2,6},{6,2},{1... | collective-permute-start | bytes 92168 | tf_op jit(solution)/shard_map/ppermute | solution.py:491
  4.5 5.6 %collective-permute-start.1 = (bf16[40,384]{1,0:T(8,128)(2,1)S(1)}, bf16[40,384]{1,0:T(8,128)(2,1)S(1)}, u32[]{:S(2)}, u32[]{:S(2)}) collective-permute-start(bf16[40,384]{1,0:T(8,128)(2,1)S(1)} %get-tuple-element.29), channel_id=1, source_target_pairs={{0,8},{4,12},{8,0},{12,4},{1,9},{5,13},{9,1},{13,5},{2,10},{6,14},... | collective-permute-start | bytes 92168 | tf_op jit(solution)/shard_map/ppermute | solution.py:491
  7.1 5.7 %collective-permute-start.2 = (bf16[40,384]{1,0:T(8,128)(2,1)S(1)}, bf16[40,384]{1,0:T(8,128)(2,1)S(1)}, u32[]{:S(2)}, u32[]{:S(2)}) collective-permute-start(bf16[40,384]{1,0:T(8,128)(2,1)S(1)} %get-tuple-element.30), channel_id=1, source_target_pairs={{0,12},{4,8},{8,4},{12,0},{1,13},{5,9},{9,5},{13,1},{2,14},{6,10},... | collective-permute-start | bytes 92168 | tf_op jit(solution)/shard_map/ppermute | solution.py:491
  7.1 13.9 %slice-start = ((s8[25165824]{0:T(1024)(128)(4,1)}), s8[4194304]{0:T(1024)(128)(4,1)S(1)}, s32[]{:S(2)}) async-start(s8[25165824]{0:T(1024)(128)(4,1)} %bitcast.2), calls=%async_computation | async-start | bytes 8388608
  7.1 13.9 %slice-start.1 = ((s8[25165824]{0:T(1024)(128)(4,1)}), s8[4194304]{0:T(1024)(128)(4,1)S(1)}, s32[]{:S(2)}) async-start(s8[25165824]{0:T(1024)(128)(4,1)} %bitcast.2), calls=%async_computation.1 | async-start | bytes 8388608
  7.1 13.9 %slice-start.2 = ((s8[25165824]{0:T(1024)(128)(4,1)}), s8[4194304]{0:T(1024)(128)(4,1)S(1)}, s32[]{:S(2)}) async-start(s8[25165824]{0:T(1024)(128)(4,1)} %bitcast.2), calls=%async_computation.2 | async-start | bytes 8388608
  13.0 5.8 %collective-permute-start.3 = (bf16[40,1536]{1,0:T(8,128)(2,1)S(1)}, bf16[40,1536]{1,0:T(8,128)(2,1)S(1)}, u32[]{:S(2)}, u32[]{:S(2)}) collective-permute-start(bf16[40,1536]{1,0:T(8,128)(2,1)S(1)} %compact.1.rows_ref.refs_0_), channel_id=1, source_target_pairs={{0,1},{1,0},{2,3},{3,2},{4,5},{5,4},{6,7},{7,6},{8,9},{9,8},{10,11... | collective-permute-start | bytes 368648 | tf_op jit(solution)/shard_map/ppermute | solution.py:491
  13.1 6.9 %collective-permute-start.4 = (bf16[40,1536]{1,0:T(8,128)(2,1)S(1)}, bf16[40,1536]{1,0:T(8,128)(2,1)S(1)}, u32[]{:S(2)}, u32[]{:S(2)}) collective-permute-start(bf16[40,1536]{1,0:T(8,128)(2,1)S(1)} %compact.1.rows_ref.refs_0_), channel_id=1, source_target_pairs={{0,2},{1,3},{2,0},{3,1},{4,6},{5,7},{6,4},{7,5},{8,10},{9,11},{10,... | collective-permute-start | bytes 368648 | tf_op jit(solution)/shard_map/ppermute | solution.py:491
  14.6 6.4 %collective-permute-start.5 = (bf16[40,1536]{1,0:T(8,128)(2,1)S(1)}, bf16[40,1536]{1,0:T(8,128)(2,1)S(1)}, u32[]{:S(2)}, u32[]{:S(2)}) collective-permute-start(bf16[40,1536]{1,0:T(8,128)(2,1)S(1)} %compact.1.rows_ref.refs_0_), channel_id=1, source_target_pairs={{0,3},{1,2},{2,1},{3,0},{4,7},{5,6},{6,5},{7,4},{8,11},{9,10},{10,... | collective-permute-start | bytes 368648 | tf_op jit(solution)/shard_map/ppermute | solution.py:491
  14.9 6.1 %slice-start.3 = ((s8[25165824]{0:T(1024)(128)(4,1)}), s8[4194304]{0:T(1024)(128)(4,1)S(1)}, s32[]{:S(2)}) async-start(s8[25165824]{0:T(1024)(128)(4,1)} %bitcast.2), calls=%async_computation.3 | async-start | bytes 8388608
  15.0 6.1 %slice-start.4 = ((s8[25165824]{0:T(1024)(128)(4,1)}), s8[4194304]{0:T(1024)(128)(4,1)S(1)}, s32[]{:S(2)}) async-start(s8[25165824]{0:T(1024)(128)(4,1)} %bitcast.2), calls=%async_computation.4 | async-start | bytes 8388608
  15.0 6.5 %slice-start.5 = ((s8[25165824]{0:T(1024)(128)(4,1)}), s8[4194304]{0:T(1024)(128)(4,1)S(1)}, s32[]{:S(2)}) async-start(s8[25165824]{0:T(1024)(128)(4,1)} %bitcast.2), calls=%async_computation.5 | async-start | bytes 8388608
  30.5 7.8 %collective-permute-start.6 = (bf16[40,1536]{1,0:T(8,128)(2,1)S(1)}, bf16[40,1536]{1,0:T(8,128)(2,1)S(1)}, u32[]{:S(2)}, u32[]{:S(2)}) collective-permute-start(bf16[40,1536]{1,0:T(8,128)(2,1)S(1)} %get-tuple-element.42), channel_id=1, source_target_pairs={{0,3},{1,2},{2,1},{3,0},{4,7},{5,6},{6,5},{7,4},{8,11},{9,10},{10,... | collective-permute-start | bytes 368648 | tf_op jit(solution)/shard_map/ppermute | solution.py:491
  34.8 5.5 %collective-permute-start.7 = (bf16[40,1536]{1,0:T(8,128)(2,1)S(1)}, bf16[40,1536]{1,0:T(8,128)(2,1)S(1)}, u32[]{:S(2)}, u32[]{:S(2)}) collective-permute-start(bf16[40,1536]{1,0:T(8,128)(2,1)S(1)} %get-tuple-element.43), channel_id=1, source_target_pairs={{0,2},{1,3},{2,0},{3,1},{4,6},{5,7},{6,4},{7,5},{8,10},{9,11},{10,... | collective-permute-start | bytes 368648 | tf_op jit(solution)/shard_map/ppermute | solution.py:491
  38.2 2.1 %collective-permute-start.8 = (bf16[40,1536]{1,0:T(8,128)(2,1)S(1)}, bf16[40,1536]{1,0:T(8,128)(2,1)S(1)}, u32[]{:S(2)}, u32[]{:S(2)}) collective-permute-start(bf16[40,1536]{1,0:T(8,128)(2,1)S(1)} %get-tuple-element.44), channel_id=1, source_target_pairs={{0,1},{1,0},{2,3},{3,2},{4,5},{5,4},{6,7},{7,6},{8,9},{9,8},{10,11... | collective-permute-start | bytes 368648 | tf_op jit(solution)/shard_map/ppermute | solution.py:491
  40.6 4.9 %collective-permute-start.9 = (bf16[40,384]{1,0:T(8,128)(2,1)S(1)}, bf16[40,384]{1,0:T(8,128)(2,1)S(1)}, u32[]{:S(2)}, u32[]{:S(2)}) collective-permute-start(bf16[40,384]{1,0:T(8,128)(2,1)S(1)} %get-tuple-element.46), channel_id=1, source_target_pairs={{0,8},{4,12},{8,0},{12,4},{1,9},{5,13},{9,1},{13,5},{2,10},{6,14},... | collective-permute-start | bytes 92168 | tf_op jit(solution)/shard_map/ppermute | solution.py:491
  40.7 5.9 %collective-permute-start.10 = (bf16[40,384]{1,0:T(8,128)(2,1)S(1)}, bf16[40,384]{1,0:T(8,128)(2,1)S(1)}, u32[]{:S(2)}, u32[]{:S(2)}) collective-permute-start(bf16[40,384]{1,0:T(8,128)(2,1)S(1)} %get-tuple-element.47), channel_id=1, source_target_pairs={{0,12},{4,8},{8,4},{12,0},{1,13},{5,9},{9,5},{13,1},{2,14},{6,10},... | collective-permute-start | bytes 92168 | tf_op jit(solution)/shard_map/ppermute | solution.py:491
  42.3 4.2 %collective-permute-start.11 = (bf16[40,384]{1,0:T(8,128)(2,1)S(1)}, bf16[40,384]{1,0:T(8,128)(2,1)S(1)}, u32[]{:S(2)}, u32[]{:S(2)}) collective-permute-start(bf16[40,384]{1,0:T(8,128)(2,1)S(1)} %get-tuple-element.48), channel_id=1, source_target_pairs={{0,4},{4,0},{8,12},{12,8},{1,5},{5,1},{9,13},{13,9},{2,6},{6,2},{1... | collective-permute-start | bytes 92168 | tf_op jit(solution)/shard_map/ppermute | solution.py:491
